TPU v7x, 512 devices: a whole 4x4x16 slice. The times are simulated.
512 devices in a mesh: replica: 8 (over y_lo, x), fsdp: 64 (over y_hi, z, core).
Axes of the slice: x: 4, y: 4 (y_hi: 2, y_lo: 2; y = y_hi * 2 + y_lo), z: 16, core: 2. Of those that a mesh axis runs over, the one named last changes fastest.
Arguments:
- inputs: bfloat16 [8, 8192, 4096], P('replica', 'fsdp'), may hold values from -6 to 6
- upstream: bfloat16 [8, 8192, 512], P('replica', 'fsdp'), may hold values from -6 to 6
- params: float32 [8, 4096, 512], P('replica', 'fsdp'), may hold values from -6 to 6
- first_moment: float32 [8, 4096, 512], P('replica', 'fsdp'), may hold values from -3 to 3
- second_moment: float32 [8, 4096, 512], P('replica', 'fsdp'), may hold values from 0.05 to 1
- anchor: float32 [4096, 512], P('fsdp'), may hold values from -6 to 6
- outer_moment: float32 [4096, 512], P('fsdp'), may hold values from -3 to 3
- step_count: int32 [1], replicated, may hold values from 1 to 8
Outputs:
- new_params: float32 [8, 4096, 512], P('replica', 'fsdp')
- new_first: float32 [8, 4096, 512], P('replica', 'fsdp')
- new_second: float32 [8, 4096, 512], P('replica', 'fsdp')
- new_anchor: float32 [4096, 512], P('fsdp')
- new_outer: float32 [4096, 512], P('fsdp')
- input_grad: bfloat16 [8, 8192, 4096], P('replica', 'fsdp')
All inputs are finite; a program needn't handle non-finite values.
Results may differ from a plain program's by a relative error of at most 0.006.
Values may be sent and summed in bfloat16 or wider, within the bound.
No kernel may reach another device: no remote copies, remote signals or barrier semaphores. Data moves between devices by JAX's collectives and lax.ppermute only.
A program may use at most 64 MiB of HBM per device.

v0:
```python
import math

import jax
import jax.numpy as jnp
from jax import lax
from jax.sharding import PartitionSpec as P


def body(inputs, upstream, params, first_moment, second_moment, anchor, outer_moment, step_count):
    tokens_in = inputs[0]
    cotangent = upstream[0]
    master = params[0]
    features = tokens_in.shape[1]
    inv_root = 1.0 / math.sqrt(features)
    outer_drift = anchor - master
    weight = lax.all_gather(master.astype(jnp.bfloat16), "fsdp", axis=0, tiled=True)
    preact = jnp.dot(tokens_in, weight, preferred_element_type=jnp.float32) * inv_root
    gating = jax.nn.sigmoid(preact)
    derivative = gating * (1.0 + preact * (1.0 - gating))
    delta_rows = (cotangent.astype(jnp.float32) * derivative * inv_root).astype(jnp.bfloat16)
    input_grad = jnp.dot(delta_rows, weight.T, preferred_element_type=jnp.float32).astype(
        jnp.bfloat16
    )
    columns = lax.all_to_all(tokens_in, "fsdp", split_axis=1, concat_axis=0, tiled=True)
    contract = (((0,), (0,)), ((), ()))
    all_delta = lax.all_gather(delta_rows, "fsdp", axis=0, tiled=True)
    weight_grad = lax.dot_general(columns, all_delta, contract, preferred_element_type=jnp.float32)
    new_first = 0.9 * first_moment[0] + 0.1 * weight_grad
    new_second = 0.95 * second_moment[0] + 0.05 * weight_grad * weight_grad
    steps = step_count[0].astype(jnp.float32)
    bias_one = 1.0 - jnp.power(jnp.float32(0.9), steps)
    bias_two = 1.0 - jnp.power(jnp.float32(0.95), steps)
    update = new_first / bias_one / (jnp.sqrt(new_second / bias_two) + 1e-08)
    inner = master - 0.1 * (update + 0.1 * master)
    replicas = lax.axis_size("replica")
    summed = lax.psum(outer_drift, "replica")
    outer_grad = summed / replicas
    new_outer = 0.9 * outer_moment + outer_grad
    new_anchor = anchor - 0.7 * (outer_grad + 0.9 * new_outer)
    new_params = 0.5 * new_anchor + 0.5 * inner
    return (
        new_params[None],
        new_first[None],
        new_second[None],
        new_anchor,
        new_outer,
        input_grad[None],
    )


def solution(mesh):
    placed = (
        P("replica", "fsdp", None),
        P("replica", "fsdp", None),
        P("replica", "fsdp", None),
        P("replica", "fsdp", None),
        P("replica", "fsdp", None),
        P("fsdp", None),
        P("fsdp", None),
        P(),
    )
    return jax.shard_map(
        body,
        mesh=mesh,
        in_specs=placed,
        out_specs=(
            P("replica", "fsdp", None),
            P("replica", "fsdp", None),
            P("replica", "fsdp", None),
            P("fsdp", None),
            P("fsdp", None),
            P("replica", "fsdp", None),
        ),
        check_vma=False,
    )
```

profile of v0, /device:TPU:1, one launch (start us, length us, event | category | flops | bytes accessed | tf_op | source)
XLA Modules:
  0.0 361.2 jit_solution(14309056206462872509)
XLA Ops:
  8.0 0.0 copy-start.1
  8.0 0.0 all-gather.3.cloned.1.call-start
  8.1 1.6 bitcast_convert_fusion
  9.7 0.0 all-gather.3.cloned.1.call-update
  9.7 0.0 all-reduce.2.cloned.1.call-start
  9.8 1.6 bitcast_subtract_fusion.1
  11.4 0.0 all-reduce.2.cloned.1.call-update
  11.4 0.0 copy-start.6
  11.4 0.0 all-gather.5.cloned.1.call-start
  11.5 158.6 %all-gather.3.cloned.1.call-done = bf16[4096,512]{1,0:T(8,128)(2,1)} async-done(((bf16[64,512]{1,0:T(8,128)(2,1)}), bf16[4096,512]{1,0:T(8,128)(2,1)}) %all-gather.3.cloned.1.call-update) | async-done | bytes 4194320 | tf_op jit(solution)/shard_map/all_gather | solution.py:16
  170.1 4.0 %fusion.5 = (bf16[128,512]{1,0:T(8,128)(2,1)}, f32[128,512]{1,0:T(8,128)S(1)}) fusion(bf16[1,128,512]{2,1,0:T(8,128)(2,1)} %param.9, bf16[4096,512]{1,0:T(8,128)(2,1)} %all-gather.3.cloned.1.call-done, bf16[1,128,4096]{2,1,0:T(8,128)(2,1)} %param.8), kind=kOutput, calls=%fused_computation.9 | convolution fusion | flops 537657344 | bytes 5767168 | tf_op jit(solution)/shard_map/dot_general | solution.py:17
  174.0 0.0 all-gather.5.cloned.1.call-update
  174.1 0.0 copy-done.1
  174.1 1.3 copy.14
  175.4 0.0 copy-start
  175.4 0.0 copy-start.2
  175.4 0.0 copy-start.3
  175.4 0.0 copy-start.4
  175.4 0.0 copy-start.5
  175.4 8.1 %all-to-all-start = ((bf16[128,64,64]{0,2,1:T(8,128)(2,1)}), bf16[128,64,64]{0,2,1:T(8,128)(2,1)S(1)}, u32[]{:S(2)}, u32[]{:S(2)}) async-start(bf16[128,64,64]{0,2,1:T(8,128)(2,1)} %bitcast.4), calls=%async_computation | async-start | bytes 2097152 | tf_op jit(solution)/shard_map/all_to_all | solution.py:24
  184.2 0.0 copy-done.6
  184.3 4.7 %fusion = bf16[1,128,4096]{2,1,0:T(8,128)(2,1)} fusion(bf16[4096,512]{1,0:T(8,128)(2,1)} %all-gather.3.cloned.1.call-done, f32[128,512]{1,0:T(8,128)S(1)} %get-tuple-element.12, bf16[1,128,512]{2,1,0:T(8,128)(2,1)S(1)} %copy-done.6), kind=kOutput, calls=%fused_computation.1 | convolution fusion | flops 538116096 | bytes 5636096 | tf_op jit(solution)/shard_map/dot_general | solution.py:21
  188.9 0.0 all-reduce.2.cloned.1.call-done
  188.9 55.4 %all-to-all-done = bf16[128,64,64]{0,2,1:T(8,128)(2,1)S(1)} async-done(((bf16[128,64,64]{0,2,1:T(8,128)(2,1)}), bf16[128,64,64]{0,2,1:T(8,128)(2,1)S(1)}, u32[]{:S(2)}, u32[]{:S(2)}) %all-to-all-start) | async-done | bytes 1048608 | tf_op jit(solution)/shard_map/all_to_all | solution.py:24
  244.3 103.5 %all-gather.5.cloned.1.call-done = bf16[8192,512]{1,0:T(8,128)(2,1)} async-done(((bf16[128,512]{1,0:T(8,128)(2,1)}), bf16[8192,512]{1,0:T(8,128)(2,1)}) %all-gather.5.cloned.1.call-update) | async-done | bytes 8388624 | tf_op jit(solution)/shard_map/all_gather | solution.py:26
  347.9 0.0 copy-done
  347.9 0.0 copy-done.2
  347.9 0.0 copy-done.3
  347.9 0.0 copy-done.4
  347.9 0.0 copy-done.5
  347.9 5.9 %fusion.13 = (f32[1,64,512]{2,1,0:T(8,128)}, f32[64,512]{1,0:T(8,128)}, f32[64,512]{1,0:T(8,128)}, f32[1,64,512]{2,1,0:T(8,128)}, f32[1,64,512]{2,1,0:T(8,128)}) fusion(f32[1,64,512]{2,1,0:T(8,128)S(1)} %copy-done, f32[]{:T(128)} %bitcast.9, f32[]{:T(128)} %bitcast.7, f32[1,64,512]{2,1,0:T(8,128)S(1)} %copy-done.3, f32[1,64,512]{2,1,0:T(8,128)S(1)} %copy-done.4, ...), kind=kOutput, calls=%fused_computation.22 | convolution fusion | flops 537657344 | bytes 10878984 | tf_op jit(solution)/shard_map/dot_general | solution.py:27
Async XLA Ops:
  8.0 166.1 %copy-start.1 = (bf16[1,128,4096]{2,1,0:T(8,128)(2,1)S(1)}, bf16[1,128,4096]{2,1,0:T(8,128)(2,1)}, u32[]{:S(2)}) copy-start(bf16[1,128,4096]{2,1,0:T(8,128)(2,1)} %param.8) | copy-start | bytes 3145732
  8.0 162.1 %all-gather.3.cloned.1.call-start = ((), (), s32[]{:S(2)}) async-start(), calls=%async_computation.2 | async-start | bytes 4259840 | tf_op jit(solution)/shard_map/all_gather | solution.py:16
  9.7 179.2 %all-reduce.2.cloned.1.call-start = ((), (), s32[]{:S(2)}) async-start(), calls=%async_computation.1 | async-start | bytes 262144 | tf_op jit(solution)/shard_map/psum | solution.py:36
  11.4 172.8 %copy-start.6 = (bf16[1,128,512]{2,1,0:T(8,128)(2,1)S(1)}, bf16[1,128,512]{2,1,0:T(8,128)(2,1)}, u32[]{:S(2)}) copy-start(bf16[1,128,512]{2,1,0:T(8,128)(2,1)} %param.9) | copy-start | bytes 393220
  11.4 336.4 %all-gather.5.cloned.1.call-start = ((), (), s32[]{:S(2)}) async-start(), calls=%async_computation.3 | async-start | bytes 8519680 | tf_op jit(solution)/shard_map/all_gather | solution.py:26
  175.4 172.5 %copy-start = (f32[1,64,512]{2,1,0:T(8,128)S(1)}, f32[1,64,512]{2,1,0:T(8,128)}, u32[]{:S(2)}) copy-start(f32[1,64,512]{2,1,0:T(8,128)} %param.10) | copy-start | bytes 393220
  175.4 172.5 %copy-start.2 = (f32[64,512]{1,0:T(8,128)S(1)}, f32[64,512]{1,0:T(8,128)}, u32[]{:S(2)}) copy-start(f32[64,512]{1,0:T(8,128)} %param.13) | copy-start | bytes 393220
  175.4 172.5 %copy-start.3 = (f32[1,64,512]{2,1,0:T(8,128)S(1)}, f32[1,64,512]{2,1,0:T(8,128)}, u32[]{:S(2)}) copy-start(f32[1,64,512]{2,1,0:T(8,128)} %param.11) | copy-start | bytes 393220
  175.4 172.5 %copy-start.4 = (f32[1,64,512]{2,1,0:T(8,128)S(1)}, f32[1,64,512]{2,1,0:T(8,128)}, u32[]{:S(2)}) copy-start(f32[1,64,512]{2,1,0:T(8,128)} %param.12) | copy-start | bytes 393220
  175.4 172.5 %copy-start.5 = (f32[64,512]{1,0:T(8,128)S(1)}, f32[64,512]{1,0:T(8,128)}, u32[]{:S(2)}) copy-start(f32[64,512]{1,0:T(8,128)} %param.14) | copy-start | bytes 393220
  175.4 68.9 %all-to-all-start = ((bf16[128,64,64]{0,2,1:T(8,128)(2,1)}), bf16[128,64,64]{0,2,1:T(8,128)(2,1)S(1)}, u32[]{:S(2)}, u32[]{:S(2)}) async-start(bf16[128,64,64]{0,2,1:T(8,128)(2,1)} %bitcast.4), calls=%async_computation | async-start | bytes 2097152 | tf_op jit(solution)/shard_map/all_to_all | solution.py:24
Sparse Core Ops, SparseCore 0:
  13.2 156.8 all-gather.2
  174.5 173.3 all-gather.4
Sparse Core Ops, SparseCore 1:
  13.6 89.2 all-reduce.1
where the time goes:
time: 361 us
  waiting for transfers between devices  318 us (88%)
  between operations  16.3 us (5%)
  matrix products  14.5 us (4%)
  starting transfers between devices  8.19 us (2%)
    all_gather x1, waiting for transfers between devices, body(): lax.all_gather(master.astype(jnp.bfloat16), 'fsdp', axis=0, tiled=True)  159 us
    all_gather x1, waiting for transfers between devices, body(): all_delta = lax.all_gather(delta_rows, 'fsdp', axis=0, tiled=True)  104 us
    all_to_all x1, waiting for transfers between devices, body(): lax.all_to_all(tokens_in, 'fsdp', split_axis=1, concat_axis=0, tiled=True)  55.4 us
    all_to_all x1, starting transfers between devices, body(): lax.all_to_all(tokens_in, 'fsdp', split_axis=1, concat_axis=0, tiled=True)  8.07 us
  transfers between devices with their start and end apart: 4, of which 3 were waited for; matrix products, arithmetic and copies ran while one was open for 3% of the time, Pallas kernels for 0%

commit v1 on v0

v1 whole, which is shorter than its diff:
```python
import math

import jax
import jax.numpy as jnp
from jax import lax
from jax.sharding import Mesh
from jax.sharding import PartitionSpec as P

Z = ("zh", "zl")
ZC = ("zh", "zl", "c")
SWAP = [(0, 1), (1, 0)]


def ring(step):
    return [(z, (z + step) % 16) for z in range(16)]


def ring_by_core(step):
    forward = [(2 * z, 2 * ((z + step) % 16)) for z in range(16)]
    backward = [(2 * z + 1, 2 * ((z - step) % 16) + 1) for z in range(16)]
    return forward + backward


def exchange(value, axes):
    return lax.all_to_all(value, axes, split_axis=0, concat_axis=0)


def gather_weight(own):
    same = exchange(jnp.broadcast_to(own[None], (4,) + own.shape), "zh")
    return [
        same,
        lax.ppermute(same, Z, ring(-1)),
        lax.ppermute(same, ZC, ring_by_core(2)),
        lax.ppermute(same, Z, ring(1)),
    ]


def scatter_grad(pieces):
    half = lambda value: value.astype(jnp.bfloat16)
    far = lax.ppermute(half(pieces[2]), ZC, ring_by_core(2))
    after = lax.ppermute(half(pieces[1]), Z, ring(1))
    before = lax.ppermute(half(pieces[3]), Z, ring(-1))
    wide = lambda value: value.astype(jnp.float32)
    summed = pieces[0] + wide(after) + wide(before) + wide(far)
    return jnp.sum(wide(exchange(half(summed), "zh")), axis=0)


def body(inputs, upstream, params, first_moment, second_moment, anchor, outer_moment, step_count):
    tokens_in = inputs[0]
    cotangent = upstream[0]
    master = params[0]
    rows, features = tokens_in.shape
    inv_root = 1.0 / math.sqrt(features)
    mine = lax.axis_index("y")
    turn = lax.axis_index("zl")

    summed = lax.psum(anchor - master, "replica")

    own = master.astype(jnp.bfloat16).reshape(64, 2, 256).transpose(1, 0, 2)
    own = exchange(own, "c").reshape(128, 256)
    weight = [piece.reshape(512, 256) for piece in gather_weight(own)]

    halves = tokens_in.reshape(rows, 2, 2048)
    kept = lax.dynamic_index_in_dim(halves, mine, 1, keepdims=False)
    given = lax.dynamic_index_in_dim(halves, 1 - mine, 1, keepdims=False)
    pair = jnp.stack([kept, lax.ppermute(given, "y", SWAP)])
    wide = lax.all_gather(pair, "c", axis=0).reshape(512, 4, 4, 128)
    wide = jnp.concatenate([wide, wide], axis=2)
    tokens = [
        lax.dynamic_slice_in_dim(wide, turn + k, 1, axis=2).reshape(512, 512) for k in range(4)
    ]
    both = jnp.stack([cotangent, lax.ppermute(cotangent, "y", SWAP)])
    both = both.reshape(2, rows, 2, 256).transpose(2, 0, 1, 3)
    both = exchange(both, "c").reshape(512, 256).astype(jnp.float32)

    partial = jnp.zeros((512, 256), jnp.float32)
    for k in range(4):
        partial += jnp.dot(tokens[k], weight[k], preferred_element_type=jnp.float32)
    other = lax.ppermute(partial, "y", SWAP).reshape(2, 2, rows, 256)
    other = jnp.flip(other, 1).reshape(512, 256)
    preact = (partial + other) * inv_root
    gating = jax.nn.sigmoid(preact)
    derivative = gating * (1.0 + preact * (1.0 - gating))
    delta = (both * derivative * inv_root).astype(jnp.bfloat16)

    contract = (((0,), (0,)), ((), ()))
    grads = [
        lax.dot_general(tokens[k], delta, contract, preferred_element_type=jnp.float32).reshape(
            4, 128, 256
        )
        for k in range(4)
    ]
    weight_grad = scatter_grad(grads)
    weight_grad = exchange(weight_grad.reshape(2, 64, 256), "c")
    weight_grad = weight_grad.transpose(1, 0, 2).reshape(64, 512)

    full = lax.all_gather(jnp.stack(weight), "c", axis=0)
    delta_own = exchange(delta.reshape(2, 256, 256), "c")
    back = [
        jnp.dot(delta_own[0], full[0, k].T, preferred_element_type=jnp.float32)
        + jnp.dot(delta_own[1], full[1, k].T, preferred_element_type=jnp.float32)
        for k in range(4)
    ]
    back = jnp.stack([b.astype(jnp.bfloat16).reshape(256, 4, 128) for b in back], axis=2)
    back = jnp.concatenate([back, back], axis=2)
    back = lax.dynamic_slice_in_dim(back, (4 - turn) % 4, 4, axis=2).reshape(2, rows, 2048)
    far = lax.ppermute(back[1], "y", SWAP)
    low = jnp.where(mine == 0, back[0], far)
    high = jnp.where(mine == 0, far, back[0])
    input_grad = jnp.concatenate([low, high], axis=1)

    new_first = 0.9 * first_moment[0] + 0.1 * weight_grad
    new_second = 0.95 * second_moment[0] + 0.05 * weight_grad * weight_grad
    steps = step_count[0].astype(jnp.float32)
    bias_one = 1.0 - jnp.power(jnp.float32(0.9), steps)
    bias_two = 1.0 - jnp.power(jnp.float32(0.95), steps)
    update = new_first / bias_one / (jnp.sqrt(new_second / bias_two) + 1e-08)
    inner = master - 0.1 * (update + 0.1 * master)
    outer_grad = summed / lax.axis_size("replica")
    new_outer = 0.9 * outer_moment + outer_grad
    new_anchor = anchor - 0.7 * (outer_grad + 0.9 * new_outer)
    new_params = 0.5 * new_anchor + 0.5 * inner
    return (
        new_params[None],
        new_first[None],
        new_second[None],
        new_anchor,
        new_outer,
        input_grad[None],
    )


def solution(mesh):
    replicas = mesh.shape["replica"]
    split = Mesh(mesh.devices.reshape(replicas, 2, 4, 4, 2), ("replica", "y", "zh", "zl", "c"))
    fsdp = ("y", "zh", "zl", "c")
    sharded = P("replica", fsdp, None)
    shared = P(fsdp, None)
    return jax.shard_map(
        body,
        mesh=split,
        in_specs=(sharded, sharded, sharded, sharded, sharded, shared, shared, P()),
        out_specs=(sharded, sharded, sharded, shared, shared, sharded),
        check_vma=False,
    )
```

time: 361 us -> 283 us (0.78); the launches traced: 361 us -> 278 us
  waiting for transfers between devices: 318 us -> 83.6 us
  starting transfers between devices: 8.19 us -> 55.4 us
  blocking collectives: 0 us -> 44.7 us
  other arithmetic: 3.27 us -> 34 us
  local copies, waits for them, and re-layouts: 1.37 us -> 20.6 us
  matrix products: 14.5 us -> 22.7 us
    all_gather x2, waiting for transfers between devices: 262 us -> 0.02 us  [the longest x1 0.02 us: body(): wide = lax.all_gather(pair, 'c', axis=0).reshape(512, 4, 4, 128)]
    all_to_all x0 -> x3, blocking collectives: none -> 44.7 us  [exchange(): return lax.all_to_all(value, axes, split_axis=0, concat_axis=0)]
    all_to_all x1 -> x3, waiting for transfers between devices: 55.4 us -> 13.1 us  [exchange(): return lax.all_to_all(value, axes, split_axis=0, concat_axis=0)]
    ppermute x0 -> x10, starting transfers between devices: none -> 40.6 us  [the longest x1 7.26 us: gather_weight(): lax.ppermute(same, Z, ring(1))]
    psum x1, waiting for transfers between devices: 0.01 us -> 38.2 us  [body(): summed = lax.psum(anchor - master, 'replica')]
    ppermute x0 -> x10, waiting for transfers between devices: none -> 32.2 us  [the longest x1 8.6 us: body(): both = jnp.stack([cotangent, lax.ppermute(cotangent, 'y', SWAP)])]
    concatenate x0 -> x1, other arithmetic: none -> 23.9 us  [body(): wide = jnp.concatenate([wide, wide], axis=2)]
    dot_general x3 -> x16, matrix products: 14.5 us -> 22.7 us  [the longest x4 7.09 us: body(): lax.dot_general(tokens[k], delta, contract, preferred_element_type=jnp.fl...]
  transfers between devices with their start and end apart: 4 -> 16, of which waited for: 3 -> 7; matrix products, arithmetic and copies ran while one was open for 3% -> 21% of each run, Pallas kernels for 0% -> 0%
where the time goes in v1:
time: 283 us; the launch traced here: 278 us
  waiting for transfers between devices  83.6 us (30%)
  starting transfers between devices  55.4 us (20%)
  blocking collectives  44.7 us (16%)
  other arithmetic  34 us (12%)
  matrix products  22.7 us (8%)
  local copies, waits for them, and re-layouts  20.6 us (7%)
  between operations  16.8 us (6%)
    all_to_all x3, blocking collectives, exchange(): return lax.all_to_all(value, axes, split_axis=0, concat_axis=0)  44.7 us
    psum x1, waiting for transfers between devices, body(): summed = lax.psum(anchor - master, 'replica')  38.2 us
    concatenate x1, other arithmetic, body(): wide = jnp.concatenate([wide, wide], axis=2)  23.9 us
    all_to_all x3, starting transfers between devices, exchange(): return lax.all_to_all(value, axes, split_axis=0, concat_axis=0)  14.6 us
    all_to_all x3, waiting for transfers between devices, exchange(): return lax.all_to_all(value, axes, split_axis=0, concat_axis=0)  13.1 us
    ppermute x1, waiting for transfers between devices, body(): both = jnp.stack([cotangent, lax.ppermute(cotangent, 'y', SWAP)])  8.6 us
    ppermute x1, waiting for transfers between devices, body(): pair = jnp.stack([kept, lax.ppermute(given, 'y', SWAP)])  8.09 us
    ppermute x1, waiting for transfers between devices, gather_weight(): lax.ppermute(same, ZC, ring_by_core(2))  7.62 us
  transfers between devices with their start and end apart: 16, of which 7 were waited for; matrix products, arithmetic and copies ran while one was open for 21% of the time, Pallas kernels for 0%

profile of v1, /device:TPU:1, one launch (start us, length us, event | category | flops | bytes accessed | tf_op | source)
XLA Modules:
  0.0 277.9 jit_solution(9253695420330036274)
XLA Ops:
  8.0 1.6 copy.36
  10.0 5.7 %collective-permute-start = (bf16[128,2048]{1,0:T(8,128)(2,1)S(1)}, bf16[128,2048]{1,0:T(8,128)(2,1)S(1)}, u32[]{:S(2)}, u32[]{:S(2)}) collective-permute-start(bf16[128,2048]{1,0:T(8,128)(2,1)S(1)} %bitcast.177), channel_id=1, source_target_pairs={{0,32},{32,0},{1,33},{33,1},{2,34},{34,2},{3,35},{35,3},{4,36},{36... | collective-permute-start | bytes 1572872 | tf_op jit(solution)/shard_map/ppermute | solution.py:66
  15.9 8.1 %collective-permute-done = bf16[128,2048]{1,0:T(8,128)(2,1)S(1)} collective-permute-done((bf16[128,2048]{1,0:T(8,128)(2,1)S(1)}, bf16[128,2048]{1,0:T(8,128)(2,1)S(1)}, u32[]{:S(2)}, u32[]{:S(2)}) %collective-permute-start) | collective-permute-done | bytes 524320 | tf_op jit(solution)/shard_map/ppermute | solution.py:66
  25.2 8.9 %all_to_all.30 = bf16[2,64,256]{2,1,0:T(8,128)(2,1)S(1)} all-to-all(bf16[2,64,256]{2,1,0:T(8,128)(2,1)S(1)} %copy.42), channel_id=1, replica_groups=mesh['replica'=8,'y'=2,'zh'=4,'zl'=4,'c'=2] {'c'}, dimensions={0} | all-to-all | bytes 131072 | tf_op jit(solution)/shard_map/all_to_all | solution.py:25
  34.1 27.9 %all_to_all.31 = bf16[4,128,256]{2,1,0:T(8,128)(2,1)S(1)} all-to-all(bf16[4,128,256]{2,1,0:T(8,128)(2,1)S(1)} %broadcast_in_dim.16), channel_id=1, replica_groups=mesh['replica'=8,'y'=2,'zh'=4,'zl'=4,'c'=2] {'zh'}, dimensions={0} | all-to-all | bytes 524288 | tf_op jit(solution)/shard_map/all_to_all | solution.py:25
  62.0 3.8 %collective-permute-start.2 = (bf16[4,128,256]{2,1,0:T(8,128)(2,1)S(1)}, bf16[4,128,256]{2,1,0:T(8,128)(2,1)S(1)}, u32[]{:S(2)}, u32[]{:S(2)}) collective-permute-start(bf16[4,128,256]{2,1,0:T(8,128)(2,1)S(1)} %all_to_all.31), channel_id=1, source_target_pairs={{0,30},{2,0},{4,2},{6,4},{8,6},{10,8},{12,10},{14,12},{16,14},{18,... | collective-permute-start | bytes 786440 | tf_op jit(solution)/shard_map/ppermute | solution.py:32
  65.9 7.3 %collective-permute-start.4 = (bf16[4,128,256]{2,1,0:T(8,128)(2,1)S(1)}, bf16[4,128,256]{2,1,0:T(8,128)(2,1)S(1)}, u32[]{:S(2)}, u32[]{:S(2)}) collective-permute-start(bf16[4,128,256]{2,1,0:T(8,128)(2,1)S(1)} %all_to_all.31), channel_id=1, source_target_pairs={{0,2},{2,4},{4,6},{6,8},{8,10},{10,12},{12,14},{14,16},{16,18},{18... | collective-permute-start | bytes 786440 | tf_op jit(solution)/shard_map/ppermute | solution.py:34
  73.1 3.4 %collective-permute-start.3 = (bf16[4,128,256]{2,1,0:T(8,128)(2,1)S(1)}, bf16[4,128,256]{2,1,0:T(8,128)(2,1)S(1)}, u32[]{:S(2)}, u32[]{:S(2)}) collective-permute-start(bf16[4,128,256]{2,1,0:T(8,128)(2,1)S(1)} %all_to_all.31), channel_id=1, source_target_pairs={{0,4},{2,6},{4,8},{6,10},{8,12},{10,14},{12,16},{14,18},{16,20},{1... | collective-permute-start | bytes 786440 | tf_op jit(solution)/shard_map/ppermute | solution.py:33
  77.2 7.6 %collective-permute-done.3 = bf16[4,128,256]{2,1,0:T(8,128)(2,1)S(1)} collective-permute-done((bf16[4,128,256]{2,1,0:T(8,128)(2,1)S(1)}, bf16[4,128,256]{2,1,0:T(8,128)(2,1)S(1)}, u32[]{:S(2)}, u32[]{:S(2)}) %collective-permute-start.3) | collective-permute-done | bytes 262176 | tf_op jit(solution)/shard_map/ppermute | solution.py:33
  84.9 1.2 pad_maximum_fusion.1
  86.1 3.2 %reshape.123 = bf16[512,4,4,128]{3,2,1,0:T(4,128)(2,1)S(1)} reshape(bf16[4,128,2048]{2,1,0:T(8,128)(2,1)} %all-gather.5.cloned.1.call-done) | data formatting | bytes 4194304 | tf_op jit(solution)/shard_map/reshape | solution.py:67
  89.3 23.9 %fusion.7 = (bf16[512,4,1,128]{3,2,1,0:T(2,128)(2,1)}, bf16[512,4,1,128]{3,2,1,0:T(2,128)(2,1)S(1)}, bf16[512,4,1,128]{3,2,1,0:T(2,128)(2,1)}, bf16[512,4,1,128]{3,2,1,0:T(2,128)(2,1)}) fusion(s32[]{:T(128)S(6)} %select_n.44, bf16[512,4,4,128]{3,2,1,0:T(4,128)(2,1)S(1)} %reshape.123, s32[]{:T(128)S(6)} %select_n.45, s32[]{:T(128)S(6)} %select_n.46, ...), kind=kLoop, calls=%fused_computation.24 | loop fusion | flops 4194304 | bytes 4194320 | tf_op jit(solution)/shard_map/concatenate | solution.py:68
  113.2 2.4 copy.39
  115.6 1.3 copy.45
  117.0 1.1 fusion.37
  118.1 2.1 fusion.38
  120.2 2.3 copy.43
  122.6 1.3 copy.44
  123.9 1.4 convolution_add_fusion.5
  125.4 1.3 fusion
  126.7 4.8 %collective-permute-start.5 = (f32[512,256]{1,0:T(8,128)S(1)}, f32[512,256]{1,0:T(8,128)S(1)}, u32[]{:S(2)}, u32[]{:S(2)}) collective-permute-start(f32[512,256]{1,0:T(8,128)S(1)} %fusion), channel_id=1, source_target_pairs={{0,32},{32,0},{1,33},{33,1},{2,34},{34,2},{3,35},{35,3},{4,36},{36... | collective-permute-start | bytes 1572872 | tf_op jit(solution)/shard_map/ppermute | solution.py:79
  131.5 2.0 collective-permute-start.1
  134.5 8.6 %collective-permute-done.1 = bf16[128,512]{1,0:T(8,128)(2,1)} collective-permute-done((bf16[128,512]{1,0:T(8,128)(2,1)}, bf16[128,512]{1,0:T(8,128)(2,1)}, u32[]{:S(2)}, u32[]{:S(2)}) %collective-permute-start.1) | collective-permute-done | bytes 131104 | tf_op jit(solution)/shard_map/ppermute | solution.py:72
  144.8 7.7 %all-to-all-start = ((bf16[2,2,128,256]{3,2,1,0:T(8,128)(2,1)}), bf16[2,2,128,256]{3,2,1,0:T(8,128)(2,1)S(1)}, u32[]{:S(2)}, u32[]{:S(2)}) async-start(bf16[2,2,128,256]{3,2,1,0:T(8,128)(2,1)} %maximum_bitcast_fusion.1), calls=%async_computation | async-start | bytes 524288 | tf_op jit(solution)/shard_map/all_to_all | solution.py:25
  155.3 3.5 %all-to-all-start.5 = ((bf16[2,256,256]{2,1,0:T(8,128)(2,1)}), bf16[2,256,256]{2,1,0:T(8,128)(2,1)S(1)}, u32[]{:S(2)}, u32[]{:S(2)}) async-start(bf16[2,256,256]{2,1,0:T(8,128)(2,1)} %bitcast.36), calls=%async_computation.5 | async-start | bytes 524288 | tf_op jit(solution)/shard_map/all_to_all | solution.py:25
  159.0 1.9 convolution_convert_fusion.2
  161.0 2.0 convolution_convert_fusion.1
  162.9 1.9 convolution_convert_fusion
  164.9 1.2 fusion.17
  166.1 1.2 fusion.4
  167.4 1.2 fusion.18
  168.6 1.2 fusion.3
  169.9 1.2 fusion.19
  171.1 1.2 fusion.2
  172.4 1.2 fusion.20
  173.6 1.2 fusion.1
  177.3 4.8 %collective-permute-start.9 = (bf16[128,2048]{1,0:T(8,128)(2,1)S(1)}, bf16[128,2048]{1,0:T(8,128)(2,1)S(1)}, u32[]{:S(2)}, u32[]{:S(2)}) collective-permute-start(bf16[128,2048]{1,0:T(8,128)(2,1)S(1)} %squeeze.71), channel_id=1, source_target_pairs={{0,32},{32,0},{1,33},{33,1},{2,34},{34,2},{3,35},{35,3},{4,36},{36... | collective-permute-start | bytes 1572872 | tf_op jit(solution)/shard_map/ppermute | solution.py:107
  182.1 1.9 collective-permute-start.6
  184.1 4.6 %collective-permute-start.7 = (bf16[4,128,256]{2,1,0:T(8,128)(2,1)}, bf16[4,128,256]{2,1,0:T(8,128)(2,1)}, u32[]{:S(2)}, u32[]{:S(2)}) collective-permute-start(bf16[4,128,256]{2,1,0:T(8,128)(2,1)} %convolution_convert_fusion.1), channel_id=1, source_target_pairs={{0,30},{2,0},{4,2},{6,4},{8,6},{10,8},{12,10},{14,12},{16,14},{18,... | collective-permute-start | bytes 786440 | tf_op jit(solution)/shard_map/ppermute | solution.py:42
  188.6 2.4 collective-permute-start.8
  193.5 1.2 fusion.14
  194.8 7.2 %collective-permute-done.8 = bf16[4,128,256]{2,1,0:T(8,128)(2,1)} collective-permute-done((bf16[4,128,256]{2,1,0:T(8,128)(2,1)}, bf16[4,128,256]{2,1,0:T(8,128)(2,1)}, u32[]{:S(2)}, u32[]{:S(2)}) %collective-permute-start.8) | collective-permute-done | bytes 262176 | tf_op jit(solution)/shard_map/ppermute | solution.py:40
  202.0 1.9 add_convert_fusion
  203.9 3.4 %all-to-all-start.3 = ((bf16[4,128,256]{2,1,0:T(8,128)(2,1)}), bf16[4,128,256]{2,1,0:T(8,128)(2,1)S(1)}, u32[]{:S(2)}, u32[]{:S(2)}) async-start(bf16[4,128,256]{2,1,0:T(8,128)(2,1)} %add_convert_fusion), calls=%async_computation.3 | async-start | bytes 524288 | tf_op jit(solution)/shard_map/all_to_all | solution.py:25
  208.5 13.1 %all-to-all-done.3 = bf16[4,128,256]{2,1,0:T(8,128)(2,1)S(1)} async-done(((bf16[4,128,256]{2,1,0:T(8,128)(2,1)}), bf16[4,128,256]{2,1,0:T(8,128)(2,1)S(1)}, u32[]{:S(2)}, u32[]{:S(2)}) %all-to-all-start.3) | async-done | bytes 262176 | tf_op jit(solution)/shard_map/all_to_all | solution.py:25
  221.7 7.8 %all_to_all.32 = f32[2,64,256]{2,1,0:T(8,128)S(1)} all-to-all(f32[2,64,256]{2,1,0:T(8,128)S(1)} %bitcast.175), channel_id=1, replica_groups=mesh['replica'=8,'y'=2,'zh'=4,'zl'=4,'c'=2] {'c'}, dimensions={0} | all-to-all | bytes 262144 | tf_op jit(solution)/shard_map/all_to_all | solution.py:25
  230.5 38.2 %all-reduce.2.cloned.1.call-done = f32[64,512]{1,0:T(8,128)} async-done(((f32[64,512]{1,0:T(8,128)}), f32[64,512]{1,0:T(8,128)}) %all-reduce.2.cloned.1.call-update) | async-done | bytes 131088 | tf_op jit(solution)/shard_map/psum | solution.py:57
  268.7 1.7 fusion.36
  (79 shorter events, 14.8 us)
Async XLA Ops:
  8.0 78.1 %all-gather.5.cloned.1.call-start = ((), (), s32[]{:S(2)}) async-start(), calls=%async_computation.7 | async-start | bytes 3145728 | tf_op jit(solution)/shard_map/all_gather | solution.py:67
  10.0 14.0 %collective-permute-start = (bf16[128,2048]{1,0:T(8,128)(2,1)S(1)}, bf16[128,2048]{1,0:T(8,128)(2,1)S(1)}, u32[]{:S(2)}, u32[]{:S(2)}) collective-permute-start(bf16[128,2048]{1,0:T(8,128)(2,1)S(1)} %bitcast.177), channel_id=1, source_target_pairs={{0,32},{32,0},{1,33},{33,1},{2,34},{34,2},{3,35},{35,3},{4,36},{36... | collective-permute-start | bytes 1572872 | tf_op jit(solution)/shard_map/ppermute | solution.py:66
  15.6 9.5 %copy-start.2 = (f32[1,64,512]{2,1,0:T(8,128)S(1)}, f32[1,64,512]{2,1,0:T(8,128)}, u32[]{:S(2)}) copy-start(f32[1,64,512]{2,1,0:T(8,128)} %param.10) | copy-start | bytes 393220
  25.1 139.8 %all-gather.7.cloned.1.call-start = ((), (), s32[]{:S(2)}) async-start(), calls=%async_computation.8 | async-start | bytes 3145728 | tf_op jit(solution)/shard_map/all_gather | solution.py:97
  62.0 14.5 %collective-permute-start.2 = (bf16[4,128,256]{2,1,0:T(8,128)(2,1)S(1)}, bf16[4,128,256]{2,1,0:T(8,128)(2,1)S(1)}, u32[]{:S(2)}, u32[]{:S(2)}) collective-permute-start(bf16[4,128,256]{2,1,0:T(8,128)(2,1)S(1)} %all_to_all.31), channel_id=1, source_target_pairs={{0,30},{2,0},{4,2},{6,4},{8,6},{10,8},{12,10},{14,12},{16,14},{18,... | collective-permute-start | bytes 786440 | tf_op jit(solution)/shard_map/ppermute | solution.py:32
  65.9 11.4 %collective-permute-start.4 = (bf16[4,128,256]{2,1,0:T(8,128)(2,1)S(1)}, bf16[4,128,256]{2,1,0:T(8,128)(2,1)S(1)}, u32[]{:S(2)}, u32[]{:S(2)}) collective-permute-start(bf16[4,128,256]{2,1,0:T(8,128)(2,1)S(1)} %all_to_all.31), channel_id=1, source_target_pairs={{0,2},{2,4},{4,6},{6,8},{8,10},{10,12},{12,14},{14,16},{16,18},{18... | collective-permute-start | bytes 786440 | tf_op jit(solution)/shard_map/ppermute | solution.py:34
  73.1 11.7 %collective-permute-start.3 = (bf16[4,128,256]{2,1,0:T(8,128)(2,1)S(1)}, bf16[4,128,256]{2,1,0:T(8,128)(2,1)S(1)}, u32[]{:S(2)}, u32[]{:S(2)}) collective-permute-start(bf16[4,128,256]{2,1,0:T(8,128)(2,1)S(1)} %all_to_all.31), channel_id=1, source_target_pairs={{0,4},{2,6},{4,8},{6,10},{8,12},{10,14},{12,16},{14,18},{16,20},{1... | collective-permute-start | bytes 786440 | tf_op jit(solution)/shard_map/ppermute | solution.py:33
  76.5 9.5 %copy-start.3 = (bf16[4,128,256]{2,1,0:T(8,128)(2,1)}, bf16[4,128,256]{2,1,0:T(8,128)(2,1)S(1)}, u32[]{:S(2)}) copy-start(bf16[4,128,256]{2,1,0:T(8,128)(2,1)S(1)} %collective-permute-done.2) | copy-start | bytes 786436
  77.2 8.8 %copy-start.6 = (bf16[4,128,256]{2,1,0:T(8,128)(2,1)}, bf16[4,128,256]{2,1,0:T(8,128)(2,1)S(1)}, u32[]{:S(2)}) copy-start(bf16[4,128,256]{2,1,0:T(8,128)(2,1)S(1)} %collective-permute-done.4) | copy-start | bytes 786436
  84.9 1.2 copy-start.5
  113.2 2.4 copy-start
  118.1 5.8 %copy-start.4 = (bf16[4,128,256]{2,1,0:T(8,128)(2,1)S(1)}, bf16[4,128,256]{2,1,0:T(8,128)(2,1)}, u32[]{:S(2)}) copy-start(bf16[4,128,256]{2,1,0:T(8,128)(2,1)} %copy-done.3) | copy-start | bytes 786436
  123.9 1.5 copy-start.1
  126.7 25.8 %collective-permute-start.5 = (f32[512,256]{1,0:T(8,128)S(1)}, f32[512,256]{1,0:T(8,128)S(1)}, u32[]{:S(2)}, u32[]{:S(2)}) collective-permute-start(f32[512,256]{1,0:T(8,128)S(1)} %fusion), channel_id=1, source_target_pairs={{0,32},{32,0},{1,33},{33,1},{2,34},{34,2},{3,35},{35,3},{4,36},{36... | collective-permute-start | bytes 1572872 | tf_op jit(solution)/shard_map/ppermute | solution.py:79
  131.5 11.5 %collective-permute-start.1 = (bf16[128,512]{1,0:T(8,128)(2,1)}, bf16[128,512]{1,0:T(8,128)(2,1)}, u32[]{:S(2)}, u32[]{:S(2)}) collective-permute-start(bf16[128,512]{1,0:T(8,128)(2,1)} %bitcast.9), channel_id=1, source_target_pairs={{0,32},{32,0},{1,33},{33,1},{2,34},{34,2},{3,35},{35,3},{4,36},{36... | collective-permute-start | bytes 393224 | tf_op jit(solution)/shard_map/ppermute | solution.py:72
  144.8 9.6 %all-to-all-start = ((bf16[2,2,128,256]{3,2,1,0:T(8,128)(2,1)}), bf16[2,2,128,256]{3,2,1,0:T(8,128)(2,1)S(1)}, u32[]{:S(2)}, u32[]{:S(2)}) async-start(bf16[2,2,128,256]{3,2,1,0:T(8,128)(2,1)} %maximum_bitcast_fusion.1), calls=%async_computation | async-start | bytes 524288 | tf_op jit(solution)/shard_map/all_to_all | solution.py:25
  152.5 0.8 copy-start.10
  155.3 9.5 %all-to-all-start.5 = ((bf16[2,256,256]{2,1,0:T(8,128)(2,1)}), bf16[2,256,256]{2,1,0:T(8,128)(2,1)S(1)}, u32[]{:S(2)}, u32[]{:S(2)}) async-start(bf16[2,256,256]{2,1,0:T(8,128)(2,1)} %bitcast.36), calls=%async_computation.5 | async-start | bytes 524288 | tf_op jit(solution)/shard_map/all_to_all | solution.py:25
  158.8 109.9 %all-reduce.2.cloned.1.call-start = ((), (), s32[]{:S(2)}) async-start(), calls=%async_computation.6 | async-start | bytes 262144 | tf_op jit(solution)/shard_map/psum | solution.py:57
  175.8 15.2 %copy-start.9 = (f32[64,512]{1,0:T(8,128)S(1)}, f32[64,512]{1,0:T(8,128)}, u32[]{:S(2)}) copy-start(f32[64,512]{1,0:T(8,128)} %param.13) | copy-start | bytes 393220
  177.3 30.0 %collective-permute-start.9 = (bf16[128,2048]{1,0:T(8,128)(2,1)S(1)}, bf16[128,2048]{1,0:T(8,128)(2,1)S(1)}, u32[]{:S(2)}, u32[]{:S(2)}) collective-permute-start(bf16[128,2048]{1,0:T(8,128)(2,1)S(1)} %squeeze.71), channel_id=1, source_target_pairs={{0,32},{32,0},{1,33},{33,1},{2,34},{34,2},{3,35},{35,3},{4,36},{36... | collective-permute-start | bytes 1572872 | tf_op jit(solution)/shard_map/ppermute | solution.py:107
  182.1 12.7 %collective-permute-start.6 = (bf16[4,128,256]{2,1,0:T(8,128)(2,1)}, bf16[4,128,256]{2,1,0:T(8,128)(2,1)}, u32[]{:S(2)}, u32[]{:S(2)}) collective-permute-start(bf16[4,128,256]{2,1,0:T(8,128)(2,1)} %convolution_convert_fusion.2), channel_id=1, source_target_pairs={{0,2},{2,4},{4,6},{6,8},{8,10},{10,12},{12,14},{14,16},{16,18},{18... | collective-permute-start | bytes 786440 | tf_op jit(solution)/shard_map/ppermute | solution.py:41
  184.1 10.8 %collective-permute-start.7 = (bf16[4,128,256]{2,1,0:T(8,128)(2,1)}, bf16[4,128,256]{2,1,0:T(8,128)(2,1)}, u32[]{:S(2)}, u32[]{:S(2)}) collective-permute-start(bf16[4,128,256]{2,1,0:T(8,128)(2,1)} %convolution_convert_fusion.1), channel_id=1, source_target_pairs={{0,30},{2,0},{4,2},{6,4},{8,6},{10,8},{12,10},{14,12},{16,14},{18,... | collective-permute-start | bytes 786440 | tf_op jit(solution)/shard_map/ppermute | solution.py:42
  188.6 13.3 %collective-permute-start.8 = (bf16[4,128,256]{2,1,0:T(8,128)(2,1)}, bf16[4,128,256]{2,1,0:T(8,128)(2,1)}, u32[]{:S(2)}, u32[]{:S(2)}) collective-permute-start(bf16[4,128,256]{2,1,0:T(8,128)(2,1)} %convolution_convert_fusion), channel_id=1, source_target_pairs={{0,4},{2,6},{4,8},{6,10},{8,12},{10,14},{12,16},{14,18},{16,20},{1... | collective-permute-start | bytes 786440 | tf_op jit(solution)/shard_map/ppermute | solution.py:40
  203.9 17.7 %all-to-all-start.3 = ((bf16[4,128,256]{2,1,0:T(8,128)(2,1)}), bf16[4,128,256]{2,1,0:T(8,128)(2,1)S(1)}, u32[]{:S(2)}, u32[]{:S(2)}) async-start(bf16[4,128,256]{2,1,0:T(8,128)(2,1)} %add_convert_fusion), calls=%async_computation.3 | async-start | bytes 524288 | tf_op jit(solution)/shard_map/all_to_all | solution.py:25
  207.4 22.3 %copy-start.7 = (f32[1,64,512]{2,1,0:T(8,128)S(1)}, f32[1,64,512]{2,1,0:T(8,128)}, u32[]{:S(2)}) copy-start(f32[1,64,512]{2,1,0:T(8,128)} %param.12) | copy-start | bytes 393220
  207.4 22.3 %copy-start.8 = (f32[1,64,512]{2,1,0:T(8,128)S(1)}, f32[1,64,512]{2,1,0:T(8,128)}, u32[]{:S(2)}) copy-start(f32[1,64,512]{2,1,0:T(8,128)} %param.11) | copy-start | bytes 393220
  207.4 61.3 %copy-start.11 = (f32[64,512]{1,0:T(8,128)S(1)}, f32[64,512]{1,0:T(8,128)}, u32[]{:S(2)}) copy-start(f32[64,512]{1,0:T(8,128)} %param.14) | copy-start | bytes 393220
Sparse Core Ops, SparseCore 0:
  25.2 30.8 all-gather.4
  86.2 18.9 all-gather.6
Sparse Core Ops, SparseCore 1:
  191.8 76.8 all-reduce.1

commit v2 on v0

v2 whole, which is shorter than its diff:
```python
import math

import jax
import jax.numpy as jnp
from jax import lax
from jax.experimental import pallas as pl
from jax.experimental.pallas import tpu as pltpu
from jax.sharding import Mesh
from jax.sharding import PartitionSpec as P

Z = ("zh", "zl")
ZC = ("zh", "zl", "c")
SWAP = [(0, 1), (1, 0)]
BF16 = jnp.bfloat16
F32 = jnp.float32


def ring(step):
    return [(z, (z + step) % 16) for z in range(16)]


def ring_by_core(step):
    forward = [(2 * z, 2 * ((z + step) % 16)) for z in range(16)]
    backward = [(2 * z + 1, 2 * ((z - step) % 16) + 1) for z in range(16)]
    return forward + backward


def call(kernel, out_shape, flops, moved, operands, pinned=()):
    smem = pl.BlockSpec(memory_space=pltpu.SMEM)
    vmem = pl.BlockSpec(memory_space=pltpu.VMEM)
    hold = pl.BlockSpec(memory_space=pl.ANY)
    used = len(operands)

    def run(*refs):
        kernel(*refs[:used], *refs[used + len(pinned) :])

    return pl.pallas_call(
        run,
        out_shape=out_shape,
        in_specs=[smem] + [vmem] * (used - 1) + [hold] * len(pinned),
        out_specs=[vmem] * len(out_shape),
        compiler_params=pltpu.CompilerParams(vmem_limit_bytes=32 * 1024 * 1024),
        cost_estimate=pl.CostEstimate(flops=flops, bytes_accessed=moved, transcendentals=0),
    )(*operands, *pinned)


def shape(dims, dtype):
    return jax.ShapeDtypeStruct(dims, dtype)


def block(turn, k, high):
    return pl.multiple_of((high * 4 + lax.rem(turn + k, 4)) * 128, 128)


def weight_kernel(place, master, out):
    rounded = master[...].astype(BF16)
    for high in range(4):
        out[2 * high] = rounded[:, 0:256]
        out[2 * high + 1] = rounded[:, 256:512]


def give_kernel(place, x, cotangent, anchor, master, send, drift):
    drift[...] = anchor[...] - master[...]
    half = pl.multiple_of((1 - place[1]) * 2048, 2048)
    send[:, 0:2048] = x[:, pl.ds(half, 2048)]
    send[:, 2048:2560] = cotangent[...]


def share_kernel(place, x, got, cotangent, drift, send, kept):
    kept[...] = drift[...]
    half = pl.multiple_of(place[1] * 2048, 2048)
    keys = pl.multiple_of((1 - place[2]) * 256, 256)
    send[0:128, 0:2048] = x[:, pl.ds(half, 2048)]
    send[0:128, 2048:2304] = cotangent[:, pl.ds(keys, 256)]
    send[128:256, 0:2048] = got[:, 0:2048]
    send[128:256, 2048:2304] = got[:, pl.ds(pl.multiple_of(2048 + keys, 256), 256)]


def weight_kernel(place, master, out):
    rounded = master[...].astype(BF16)
    for high in range(4):
        out[2 * high] = rounded[:, 0:256]
        out[2 * high + 1] = rounded[:, 256:512]


def give_kernel(place, x, cotangent, anchor, master, send, drift):
    drift[...] = anchor[...] - master[...]
    half = pl.multiple_of((1 - place[1]) * 2048, 2048)
    send[:, 0:2048] = x[:, pl.ds(half, 2048)]
    send[:, 2048:2560] = cotangent[...]


def share_kernel(place, x, got, cotangent, drift, send, kept):
    kept[...] = drift[...]
    half = pl.multiple_of(place[1] * 2048, 2048)
    keys = pl.multiple_of((1 - place[2]) * 256, 256)
    send[0:128, 0:2048] = x[:, pl.ds(half, 2048)]
    send[0:128, 2048:2304] = cotangent[:, pl.ds(keys, 256)]
    send[128:256, 0:2048] = got[:, 0:2048]
    send[128:256, 2048:2304] = got[:, pl.ds(pl.multiple_of(2048 + keys, 256), 256)]


def order_kernel(place, x, got, near, cotangent, tokens, upstream):
    turn, mine, core = place[0], place[1], place[2]
    half = pl.multiple_of(mine * 2048, 2048)
    keys = pl.multiple_of(core * 256, 256)
    for k in range(4):
        for high in range(4):
            start = block(turn, k, high)
            to = pl.ds(high * 128, 128)
            tokens[k, 0:128, to] = x[:, pl.ds(pl.multiple_of(half + start, 128), 128)]
            tokens[k, 128:256, to] = got[:, pl.ds(start, 128)]
            tokens[k, 256:512, to] = near[:, pl.ds(start, 128)]
    upstream[0:128, :] = cotangent[:, pl.ds(keys, 256)]
    upstream[128:256, :] = got[:, pl.ds(pl.multiple_of(2048 + keys, 256), 256)]
    upstream[256:512, :] = near[:, 2048:2304]


def preact_own_kernel(place, x, got, w0, w1, w2, w3, partial, tokens):
    turn = place[0]
    half = pl.multiple_of(place[1] * 2048, 2048)
    total = jnp.zeros((256, 256), F32)
    for k, weight in enumerate((w0, w1, w2, w3)):
        for high in range(4):
            start = block(turn, k, high)
            to = pl.ds(high * 128, 128)
            tokens[k, 0:128, to] = x[:, pl.ds(pl.multiple_of(half + start, 128), 128)]
            tokens[k, 128:256, to] = got[:, pl.ds(start, 128)]
        total += jnp.dot(tokens[k], weight[...], preferred_element_type=F32)
    partial[...] = total


def preact_near_kernel(place, near, w0, w1, w2, w3, partial, tokens):
    turn = place[0]
    total = jnp.zeros((256, 256), F32)
    for k, weight in enumerate((w0, w1, w2, w3)):
        for high in range(4):
            to = pl.ds(high * 128, 128)
            tokens[k, :, to] = near[:, pl.ds(block(turn, k, high), 128)]
        total += jnp.dot(tokens[k], weight[...], preferred_element_type=F32)
    partial[...] = total


def turn_kernel(place, own, other, cotangent, got, near, w0, w1, w2, w3, turned, upstream, packed):
    keys = pl.multiple_of(place[2] * 256, 256)
    for k, weight in enumerate((w0, w1, w2, w3)):
        turned[k, :, 0:256] = own[k].T
        turned[k, :, 256:512] = other[k].T
        packed[k] = weight[...]
    upstream[0:128, :] = cotangent[:, pl.ds(keys, 256)]
    upstream[128:256, :] = got[:, pl.ds(pl.multiple_of(2048 + keys, 256), 256)]
    upstream[256:512, :] = near[:, 2048:2304]


def delta_kernel(inv_root, place, p0, p1, o0, o1, upstream, turned, delta, g0, g1, g2, g3):
    for row in range(0, 512, 128):
        here = slice(row, row + 128)
        mine = slice(row % 256, row % 256 + 128)
        theirs = slice((row ^ 128) % 256, (row ^ 128) % 256 + 128)
        partial, other = (p0, o0) if row < 256 else (p1, o1)
        preact = (partial[mine, :] + other[theirs, :]) * inv_root
        gating = jax.nn.sigmoid(preact)
        derivative = gating * (1.0 + preact * (1.0 - gating))
        rows = upstream[here, :].astype(F32) * derivative * inv_root
        delta[here, :] = rows.astype(BF16)
    for k, grad in ((2, g2), (1, g1), (3, g3), (0, g0)):
        full = jnp.dot(turned[k], delta[...], preferred_element_type=F32)
        grad[...] = full.astype(grad.dtype)


def back(delta, weight):
    return lax.dot_general(delta, weight, (((1,), (1,)), ((), ())), preferred_element_type=F32)


def back_kernel(place, delta, near, weight, near_weight, out, away):
    turn = place[0]
    for k in range(4):
        total = back(delta[0:256, :], weight[k]) + back(near[...], near_weight[k])
        total = total.astype(BF16)
        for high in range(4):
            to = pl.ds(block(turn, k, high), 128)
            out[:, to] = total[0:128, high * 128 : high * 128 + 128]
            away[:, to] = total[128:256, high * 128 : high * 128 + 128]


def total_kernel(place, g0, after, before, far, drift, total, kept):
    kept[...] = drift[...]
    summed = g0[...] + after[...].astype(F32) + before[...].astype(F32) + far[...].astype(F32)
    total[...] = summed.astype(BF16)


def body(inputs, upstream, params, first_moment, second_moment, anchor, outer_moment, step_count):
    tokens_in = inputs[0]
    cotangent = upstream[0]
    master = params[0]
    rows, features = tokens_in.shape
    inv_root = 1.0 / math.sqrt(features)
    mine = lax.axis_index("y")
    core = lax.axis_index("c")
    place = jnp.stack([lax.axis_index("zl"), mine, core]).astype(jnp.int32)

    (own,) = call(weight_kernel, [shape((8, 64, 256), BF16)], 0, 1 << 19, (place, master))
    same = lax.all_to_all(own, ("zh", "c"), split_axis=0, concat_axis=0).reshape(512, 256)
    weight = [
        same,
        lax.ppermute(same, Z, ring(-1)),
        lax.ppermute(same, ZC, ring_by_core(2)),
        lax.ppermute(same, Z, ring(1)),
    ]

    replicas = lax.axis_size("replica")

    def fold(value, flip):
        if flip >= replicas:
            return value
        pairs = [(r, r ^ flip) for r in range(replicas)]
        return value + lax.ppermute(value, "replica", pairs)

    given, drift = call(
        give_kernel,
        [shape((rows, 2560), BF16), shape((64, 512), F32)],
        0,
        1 << 20,
        (place, tokens_in, cotangent, anchor, master),
    )
    got = lax.ppermute(given, "y", SWAP)
    drift = fold(drift, 1)
    shared, drift = call(
        share_kernel,
        [shape((256, 2304), BF16), shape((64, 512), F32)],
        0,
        2 << 20,
        (place, tokens_in, got, cotangent, drift),
        weight[1:],
    )
    near = lax.ppermute(shared, "c", SWAP)

    partial_shapes = [shape((256, 256), F32), shape((4, 256, 512), BF16)]
    cost = 2 * 256 * 2048 * 256
    partial, tokens = call(
        preact_own_kernel, partial_shapes, cost, 3 << 20, (place, tokens_in, got, *weight)
    )
    other = lax.ppermute(partial, "y", SWAP)
    partial_near, tokens_near = call(
        preact_near_kernel, partial_shapes, cost, 3 << 20, (place, near, *weight)
    )
    other_near = lax.ppermute(partial_near, "y", SWAP)
    turned, both, packed = call(
        turn_kernel,
        [shape((4, 512, 512), BF16), shape((512, 256), BF16), shape((4, 512, 256), BF16)],
        0,
        4 << 20,
        (place, tokens, tokens_near, cotangent, got, near, *weight),
        (partial_near,),
    )
    near_weight = lax.ppermute(packed, "c", SWAP)
    drift = fold(drift, 3)
    delta, g0, g1, g2, g3 = call(
        lambda *refs: delta_kernel(inv_root, *refs),
        [shape((512, 256), BF16), shape((512, 256), F32)] + [shape((512, 256), BF16)] * 3,
        2 * 512 * 2048 * 256,
        5 << 20,
        (place, partial, partial_near, other, other_near, both, turned),
        (drift, near_weight),
    )

    far = lax.ppermute(g2, ZC, ring_by_core(2))
    after = lax.ppermute(g1, Z, ring(1))
    before = lax.ppermute(g3, Z, ring(-1))

    near_delta = lax.ppermute(delta[256:], "c", SWAP)
    stay, away = call(
        back_kernel,
        [shape((rows, 2048), BF16)] * 2,
        2 * 256 * 2048 * 512,
        4 << 20,
        (place, delta, near_delta, packed, near_weight),
        (after, before, far),
    )
    back_far = lax.ppermute(away, "y", SWAP)
    input_grad = jnp.concatenate(
        [jnp.where(mine == 0, stay, back_far), jnp.where(mine == 0, back_far, stay)], axis=1
    )

    total, drift = call(
        total_kernel,
        [shape((512, 256), BF16), shape((64, 512), F32)],
        0,
        2 << 20,
        (place, g0, after, before, far, drift),
        (away,),
    )
    parts = lax.all_to_all(total.reshape(8, 64, 256), ("zh", "c"), split_axis=0, concat_axis=0)
    weight_grad = jnp.sum(parts.reshape(4, 2, 64, 256).astype(F32), axis=0)
    weight_grad = weight_grad.transpose(1, 0, 2).reshape(64, 512)
    summed = fold(drift, 4)

    new_first = 0.9 * first_moment[0] + 0.1 * weight_grad
    new_second = 0.95 * second_moment[0] + 0.05 * weight_grad * weight_grad
    steps = step_count[0].astype(F32)
    bias_one = 1.0 - jnp.power(jnp.float32(0.9), steps)
    bias_two = 1.0 - jnp.power(jnp.float32(0.95), steps)
    update = new_first / bias_one / (jnp.sqrt(new_second / bias_two) + 1e-08)
    inner = master - 0.1 * (update + 0.1 * master)
    outer_grad = summed / replicas
    new_outer = 0.9 * outer_moment + outer_grad
    new_anchor = anchor - 0.7 * (outer_grad + 0.9 * new_outer)
    new_params = 0.5 * new_anchor + 0.5 * inner
    return (
        new_params[None],
        new_first[None],
        new_second[None],
        new_anchor,
        new_outer,
        input_grad[None],
    )


def solution(mesh):
    replicas = mesh.shape["replica"]
    split = Mesh(mesh.devices.reshape(replicas, 2, 4, 4, 2), ("replica", "y", "zh", "zl", "c"))
    fsdp = ("y", "zh", "zl", "c")
    sharded = P("replica", fsdp, None)
    shared = P(fsdp, None)
    return jax.shard_map(
        body,
        mesh=split,
        in_specs=(sharded, sharded, sharded, sharded, sharded, shared, shared, P()),
        out_specs=(sharded, sharded, sharded, shared, shared, sharded),
        check_vma=False,
    )
```

time: 361 us -> 144 us (0.40)
  the two profiles are of different devices: /device:TPU:1 before, /device:TPU:32 now
where the time goes in v2:
time: 144 us
  starting transfers between devices  70 us (49%)
  waiting for transfers between devices  54.1 us (38%)
  Pallas kernels  9.77 us (7%)
  local copies, waits for them, and re-layouts  5.11 us (4%)
  other arithmetic  2.9 us (2%)
  between operations  1.73 us (1%)
    all_to_all x1, waiting for transfers between devices, body(): lax.all_to_all(total.reshape(8, 64, 256), ('zh', 'c'), split_axis=0, conc...  18.7 us
    all_to_all x1, starting transfers between devices, body(): lax.all_to_all(own, ('zh', 'c'), split_axis=0, concat_axis=0)  14.2 us
    all_to_all x1, waiting for transfers between devices, body(): lax.all_to_all(own, ('zh', 'c'), split_axis=0, concat_axis=0)  11.6 us
    ppermute x3, starting transfers between devices, fold(): return value + lax.ppermute(value, 'replica', pairs)  10.7 us
    pallas_call x9, Pallas kernels, call(): pl.pallas_call(run, out_shape=out_shape, in_specs=[smem] + [vmem] * (used...  9.77 us
    ppermute x3, waiting for transfers between devices, fold(): return value + lax.ppermute(value, 'replica', pairs)  7.09 us
    ppermute x1, starting transfers between devices, body(): lax.ppermute(same, ZC, ring_by_core(2))  6.01 us
    ppermute x1, starting transfers between devices, body(): other = lax.ppermute(partial, 'y', SWAP)  5.12 us
  transfers between devices with their start and end apart: 18, of which 11 were waited for; matrix products, arithmetic and copies ran while one was open for 2% of the time, Pallas kernels for 2%

profile of v2, /device:TPU:32, one launch (start us, length us, event | category | flops | bytes accessed | tf_op | source)
XLA Modules:
  0.0 143.6 jit_solution(7867319730626785637)
XLA Ops:
  0.7 0.9 copy-done.4
  1.6 1.3 shard_map.128
  2.9 14.2 %all-to-all-start = ((bf16[8,64,256]{2,1,0:T(8,128)(2,1)}), bf16[8,64,256]{2,1,0:T(8,128)(2,1)S(1)}, u32[]{:S(2)}, u32[]{:S(2)}) async-start(bf16[8,64,256]{2,1,0:T(8,128)(2,1)} %shard_map.128), calls=%async_computation | async-start | bytes 524288 | tf_op jit(solution)/shard_map/all_to_all | solution.py:203
  17.1 1.2 copy-done
  18.3 0.9 copy-done.2
  19.2 0.9 copy-done.5
  20.1 0.9 copy-done.7
  21.0 0.6 shard_map.127
  21.6 5.1 %collective-permute-start = (bf16[128,2560]{1,0:T(8,128)(2,1)S(1)}, bf16[128,2560]{1,0:T(8,128)(2,1)S(1)}, u32[]{:S(2)}, u32[]{:S(2)}) collective-permute-start(bf16[128,2560]{1,0:T(8,128)(2,1)S(1)} %get-tuple-element.26), channel_id=1, source_target_pairs={{0,32},{32,0},{1,33},{33,1},{2,34},{34,2},{3,35},{35,3},{4,36},{36... | collective-permute-start | bytes 1966088 | tf_op jit(solution)/shard_map/ppermute | solution.py:226
  26.7 11.6 %all-to-all-done = bf16[8,64,256]{2,1,0:T(8,128)(2,1)S(1)} async-done(((bf16[8,64,256]{2,1,0:T(8,128)(2,1)}), bf16[8,64,256]{2,1,0:T(8,128)(2,1)S(1)}, u32[]{:S(2)}, u32[]{:S(2)}) %all-to-all-start) | async-done | bytes 262176 | tf_op jit(solution)/shard_map/all_to_all | solution.py:203
  38.3 1.9 %collective-permute-start.1 = (bf16[512,256]{1,0:T(8,128)(2,1)S(1)}, bf16[512,256]{1,0:T(8,128)(2,1)S(1)}, u32[]{:S(2)}, u32[]{:S(2)}) collective-permute-start(bf16[512,256]{1,0:T(8,128)(2,1)S(1)} %bitcast.33), channel_id=1, source_target_pairs={{0,30},{2,0},{4,2},{6,4},{8,6},{10,8},{12,10},{14,12},{16,14},{18,... | collective-permute-start | bytes 786440 | tf_op jit(solution)/shard_map/ppermute | solution.py:206
  40.2 6.0 %collective-permute-start.2 = (bf16[512,256]{1,0:T(8,128)(2,1)S(1)}, bf16[512,256]{1,0:T(8,128)(2,1)S(1)}, u32[]{:S(2)}, u32[]{:S(2)}) collective-permute-start(bf16[512,256]{1,0:T(8,128)(2,1)S(1)} %bitcast.34), channel_id=1, source_target_pairs={{0,4},{2,6},{4,8},{6,10},{8,12},{10,14},{12,16},{14,18},{16,20},{1... | collective-permute-start | bytes 786440 | tf_op jit(solution)/shard_map/ppermute | solution.py:207
  46.3 1.9 %collective-permute-start.3 = (bf16[512,256]{1,0:T(8,128)(2,1)S(1)}, bf16[512,256]{1,0:T(8,128)(2,1)S(1)}, u32[]{:S(2)}, u32[]{:S(2)}) collective-permute-start(bf16[512,256]{1,0:T(8,128)(2,1)S(1)} %bitcast.35), channel_id=1, source_target_pairs={{0,2},{2,4},{4,6},{6,8},{8,10},{10,12},{12,14},{14,16},{16,18},{18... | collective-permute-start | bytes 786440 | tf_op jit(solution)/shard_map/ppermute | solution.py:208
  48.2 3.4 %collective-permute-start.4 = (f32[64,512]{1,0:T(8,128)S(1)}, f32[64,512]{1,0:T(8,128)S(1)}, u32[]{:S(2)}, u32[]{:S(2)}) collective-permute-start(f32[64,512]{1,0:T(8,128)S(1)} %get-tuple-element.28), channel_id=1, source_target_pairs={{0,64},{64,0},{128,192},{192,128},{256,320},{320,256},{384,448},{4... | collective-permute-start | bytes 393224 | tf_op jit(solution)/shard_map/ppermute | solution.py:217
  51.6 3.5 %collective-permute-done.4 = f32[64,512]{1,0:T(8,128)S(1)} collective-permute-done((f32[64,512]{1,0:T(8,128)S(1)}, f32[64,512]{1,0:T(8,128)S(1)}, u32[]{:S(2)}, u32[]{:S(2)}) %collective-permute-start.4) | collective-permute-done | bytes 131104 | tf_op jit(solution)/shard_map/ppermute | solution.py:217
  55.1 3.9 %collective-permute-done.3.refs_6_.refs_7_.refs_5_.refs_9_ = bf16[512,256]{1,0:T(8,128)(2,1)S(1)} collective-permute-done((bf16[512,256]{1,0:T(8,128)(2,1)S(1)}, bf16[512,256]{1,0:T(8,128)(2,1)S(1)}, u32[]{:S(2)}, u32[]{:S(2)}) %collective-permute-start.3) | collective-permute-done | bytes 262176 | tf_op jit(solution)/shard_map/ppermute | solution.py:208
  59.0 0.6 shard_map.130
  59.7 1.9 %collective-permute-start.5 = (bf16[256,2304]{1,0:T(8,128)(2,1)S(1)}, bf16[256,2304]{1,0:T(8,128)(2,1)S(1)}, u32[]{:S(2)}, u32[]{:S(2)}) collective-permute-start(bf16[256,2304]{1,0:T(8,128)(2,1)S(1)} %get-tuple-element.29), channel_id=1, source_target_pairs={{0,1},{1,0},{2,3},{3,2},{4,5},{5,4},{6,7},{7,6},{8,9},{9,8},{10,11... | collective-permute-start | bytes 3538952 | tf_op jit(solution)/shard_map/ppermute | solution.py:236
  61.6 1.1 shard_map.129
  62.7 1.7 %collective-permute-done.5.refs_1_.refs_5_ = bf16[256,2304]{1,0:T(8,128)(2,1)S(1)} collective-permute-done((bf16[256,2304]{1,0:T(8,128)(2,1)S(1)}, bf16[256,2304]{1,0:T(8,128)(2,1)S(1)}, u32[]{:S(2)}, u32[]{:S(2)}) %collective-permute-start.5) | collective-permute-done | bytes 1179680 | tf_op jit(solution)/shard_map/ppermute | solution.py:236
  64.4 1.0 shard_map.131
  65.4 1.2 shard_map.132
  66.6 2.0 %collective-permute-start.9 = (bf16[4,512,256]{2,1,0:T(8,128)(2,1)S(1)}, bf16[4,512,256]{2,1,0:T(8,128)(2,1)S(1)}, u32[]{:S(2)}, u32[]{:S(2)}) collective-permute-start(bf16[4,512,256]{2,1,0:T(8,128)(2,1)S(1)} %get-tuple-element.36.refs_3_), channel_id=1, source_target_pairs={{0,1},{1,0},{2,3},{3,2},{4,5},{5,4},{6,7},{7,6},{8,9},{9,8},{10,11... | collective-permute-start | bytes 3145736 | tf_op jit(solution)/shard_map/ppermute | solution.py:256
  68.7 5.1 %collective-permute-start.6 = (f32[256,256]{1,0:T(8,128)S(1)}, f32[256,256]{1,0:T(8,128)S(1)}, u32[]{:S(2)}, u32[]{:S(2)}) collective-permute-start(f32[256,256]{1,0:T(8,128)S(1)} %get-tuple-element.27.refs_1_), channel_id=1, source_target_pairs={{0,32},{32,0},{1,33},{33,1},{2,34},{34,2},{3,35},{35,3},{4,36},{36... | collective-permute-start | bytes 786440 | tf_op jit(solution)/shard_map/ppermute | solution.py:243
  73.8 2.2 %collective-permute-start.7 = (f32[256,256]{1,0:T(8,128)S(1)}, f32[256,256]{1,0:T(8,128)S(1)}, u32[]{:S(2)}, u32[]{:S(2)}) collective-permute-start(f32[256,256]{1,0:T(8,128)S(1)} %get-tuple-element.30.refs_10_.refs_2_), channel_id=1, source_target_pairs={{0,32},{32,0},{1,33},{33,1},{2,34},{34,2},{3,35},{35,3},{4,36},{36... | collective-permute-start | bytes 786440 | tf_op jit(solution)/shard_map/ppermute | solution.py:247
  76.0 4.7 %collective-permute-start.8 = (f32[64,512]{1,0:T(8,128)S(1)}, f32[64,512]{1,0:T(8,128)S(1)}, u32[]{:S(2)}, u32[]{:S(2)}) collective-permute-start(f32[64,512]{1,0:T(8,128)S(1)} %get-tuple-element.35), channel_id=1, source_target_pairs={{0,192},{64,128},{128,64},{192,0},{256,448},{320,384},{384,320},{4... | collective-permute-start | bytes 393224 | tf_op jit(solution)/shard_map/ppermute | solution.py:217
  80.7 3.6 %collective-permute-done.8 = f32[64,512]{1,0:T(8,128)S(1)} collective-permute-done((f32[64,512]{1,0:T(8,128)S(1)}, f32[64,512]{1,0:T(8,128)S(1)}, u32[]{:S(2)}, u32[]{:S(2)}) %collective-permute-start.8) | collective-permute-done | bytes 131104 | tf_op jit(solution)/shard_map/ppermute | solution.py:217
  84.4 1.9 %collective-permute-done.7.refs_4_ = f32[256,256]{1,0:T(8,128)S(1)} collective-permute-done((f32[256,256]{1,0:T(8,128)S(1)}, f32[256,256]{1,0:T(8,128)S(1)}, u32[]{:S(2)}, u32[]{:S(2)}) %collective-permute-start.7) | collective-permute-done | bytes 262176 | tf_op jit(solution)/shard_map/ppermute | solution.py:247
  86.3 1.3 shard_map.133
  87.6 2.4 %collective-permute-start.10 = (bf16[512,256]{1,0:T(8,128)(2,1)S(1)}, bf16[512,256]{1,0:T(8,128)(2,1)S(1)}, u32[]{:S(2)}, u32[]{:S(2)}) collective-permute-start(bf16[512,256]{1,0:T(8,128)(2,1)S(1)} %get-tuple-element.38), channel_id=1, source_target_pairs={{0,2},{2,4},{4,6},{6,8},{8,10},{10,12},{12,14},{14,16},{16,18},{18... | collective-permute-start | bytes 786440 | tf_op jit(solution)/shard_map/ppermute | solution.py:268
  90.0 3.5 %collective-permute-start.11 = (bf16[512,256]{1,0:T(8,128)(2,1)S(1)}, bf16[512,256]{1,0:T(8,128)(2,1)S(1)}, u32[]{:S(2)}, u32[]{:S(2)}) collective-permute-start(bf16[512,256]{1,0:T(8,128)(2,1)S(1)} %get-tuple-element.39), channel_id=1, source_target_pairs={{0,30},{2,0},{4,2},{6,4},{8,6},{10,8},{12,10},{14,12},{16,14},{18,... | collective-permute-start | bytes 786440 | tf_op jit(solution)/shard_map/ppermute | solution.py:269
  93.5 2.6 %collective-permute-start.12 = (bf16[512,256]{1,0:T(8,128)(2,1)S(1)}, bf16[512,256]{1,0:T(8,128)(2,1)S(1)}, u32[]{:S(2)}, u32[]{:S(2)}) collective-permute-start(bf16[512,256]{1,0:T(8,128)(2,1)S(1)} %get-tuple-element.40), channel_id=1, source_target_pairs={{0,4},{2,6},{4,8},{6,10},{8,12},{10,14},{12,16},{14,18},{16,20},{1... | collective-permute-start | bytes 786440 | tf_op jit(solution)/shard_map/ppermute | solution.py:267
  96.1 1.9 %collective-permute-start.13 = (bf16[256,256]{1,0:T(8,128)(2,1)S(1)}, bf16[256,256]{1,0:T(8,128)(2,1)S(1)}, u32[]{:S(2)}, u32[]{:S(2)}) collective-permute-start(bf16[256,256]{1,0:T(8,128)(2,1)S(1)} %slice.3), channel_id=1, source_target_pairs={{0,1},{1,0},{2,3},{3,2},{4,5},{5,4},{6,7},{7,6},{8,9},{9,8},{10,11... | collective-permute-start | bytes 393224 | tf_op jit(solution)/shard_map/ppermute | solution.py:271
  98.1 1.3 collective-permute-done.13.refs_2_
  99.4 3.9 %collective-permute-done.11.refs_6_.refs_3_ = bf16[512,256]{1,0:T(8,128)(2,1)S(1)} collective-permute-done((bf16[512,256]{1,0:T(8,128)(2,1)S(1)}, bf16[512,256]{1,0:T(8,128)(2,1)S(1)}, u32[]{:S(2)}, u32[]{:S(2)}) %collective-permute-start.11) | collective-permute-done | bytes 262176 | tf_op jit(solution)/shard_map/ppermute | solution.py:269
  103.3 3.4 %collective-permute-done.12.refs_7_.refs_4_ = bf16[512,256]{1,0:T(8,128)(2,1)S(1)} collective-permute-done((bf16[512,256]{1,0:T(8,128)(2,1)S(1)}, bf16[512,256]{1,0:T(8,128)(2,1)S(1)}, u32[]{:S(2)}, u32[]{:S(2)}) %collective-permute-start.12) | collective-permute-done | bytes 262176 | tf_op jit(solution)/shard_map/ppermute | solution.py:267
  106.7 1.3 shard_map.134
  108.0 5.1 %collective-permute-start.15 = (bf16[128,2048]{1,0:T(8,128)(2,1)S(1)}, bf16[128,2048]{1,0:T(8,128)(2,1)S(1)}, u32[]{:S(2)}, u32[]{:S(2)}) collective-permute-start(bf16[128,2048]{1,0:T(8,128)(2,1)S(1)} %get-tuple-element.42.refs_6_), channel_id=1, source_target_pairs={{0,32},{32,0},{1,33},{33,1},{2,34},{34,2},{3,35},{35,3},{4,36},{36... | collective-permute-start | bytes 1572872 | tf_op jit(solution)/shard_map/ppermute | solution.py:280
  113.8 1.4 shard_map.135
  115.2 3.4 %all-to-all-start.1 = ((bf16[8,64,256]{2,1,0:T(8,128)(2,1)}), bf16[8,64,256]{2,1,0:T(8,128)(2,1)S(1)}, u32[]{:S(2)}, u32[]{:S(2)}) async-start(bf16[8,64,256]{2,1,0:T(8,128)(2,1)} %bitcast.8), calls=%async_computation.1 | async-start | bytes 524288 | tf_op jit(solution)/shard_map/all_to_all | solution.py:293
  118.6 2.6 %collective-permute-start.14 = (f32[64,512]{1,0:T(8,128)S(1)}, f32[64,512]{1,0:T(8,128)S(1)}, u32[]{:S(2)}, u32[]{:S(2)}) collective-permute-start(f32[64,512]{1,0:T(8,128)S(1)} %get-tuple-element.43), channel_id=1, source_target_pairs={{0,256},{64,320},{128,384},{192,448},{256,0},{320,64},{384,128},{4... | collective-permute-start | bytes 393224 | tf_op jit(solution)/shard_map/ppermute | solution.py:217
  121.2 0.5 collective-permute-done.15
  121.7 0.1 broadcast_select_fusion.1
  121.9 1.0 maximum_bitcast_fusion
  122.9 18.7 %all-to-all-done.1 = bf16[8,64,256]{2,1,0:T(8,128)(2,1)S(1)} async-done(((bf16[8,64,256]{2,1,0:T(8,128)(2,1)}), bf16[8,64,256]{2,1,0:T(8,128)(2,1)S(1)}, u32[]{:S(2)}, u32[]{:S(2)}) %all-to-all-start.1) | async-done | bytes 262176 | tf_op jit(solution)/shard_map/all_to_all | solution.py:293
  141.9 0.1 reshape.71
  142.0 0.7 fusion.6
  142.8 0.8 multiply_bitcast_fusion
  (33 shorter events, 0.3 us)
Async XLA Ops:
  0.6 58.4 %copy-start.3 = (bf16[1,128,512]{2,1,0:T(8,128)(2,1)S(1)}, bf16[1,128,512]{2,1,0:T(8,128)(2,1)}, u32[]{:S(2)}) copy-start(bf16[1,128,512]{2,1,0:T(8,128)(2,1)} %param.9) | copy-start | bytes 393220
  0.7 0.9 copy-start.4
  2.9 35.4 %all-to-all-start = ((bf16[8,64,256]{2,1,0:T(8,128)(2,1)}), bf16[8,64,256]{2,1,0:T(8,128)(2,1)S(1)}, u32[]{:S(2)}, u32[]{:S(2)}) async-start(bf16[8,64,256]{2,1,0:T(8,128)(2,1)} %shard_map.128), calls=%async_computation | async-start | bytes 524288 | tf_op jit(solution)/shard_map/all_to_all | solution.py:203
  17.1 1.2 copy-start
  18.3 0.9 copy-start.2
  19.2 0.9 copy-start.5
  20.1 0.9 copy-start.7
  21.0 38.0 %copy-start.1 = (bf16[1,128,4096]{2,1,0:T(8,128)(2,1)S(1)}, bf16[1,128,4096]{2,1,0:T(8,128)(2,1)}, u32[]{:S(2)}) copy-start(bf16[1,128,4096]{2,1,0:T(8,128)(2,1)} %param.8) | copy-start | bytes 3145732
  21.6 33.4 %collective-permute-start = (bf16[128,2560]{1,0:T(8,128)(2,1)S(1)}, bf16[128,2560]{1,0:T(8,128)(2,1)S(1)}, u32[]{:S(2)}, u32[]{:S(2)}) collective-permute-start(bf16[128,2560]{1,0:T(8,128)(2,1)S(1)} %get-tuple-element.26), channel_id=1, source_target_pairs={{0,32},{32,0},{1,33},{33,1},{2,34},{34,2},{3,35},{35,3},{4,36},{36... | collective-permute-start | bytes 1966088 | tf_op jit(solution)/shard_map/ppermute | solution.py:226
  38.3 16.8 %collective-permute-start.1 = (bf16[512,256]{1,0:T(8,128)(2,1)S(1)}, bf16[512,256]{1,0:T(8,128)(2,1)S(1)}, u32[]{:S(2)}, u32[]{:S(2)}) collective-permute-start(bf16[512,256]{1,0:T(8,128)(2,1)S(1)} %bitcast.33), channel_id=1, source_target_pairs={{0,30},{2,0},{4,2},{6,4},{8,6},{10,8},{12,10},{14,12},{16,14},{18,... | collective-permute-start | bytes 786440 | tf_op jit(solution)/shard_map/ppermute | solution.py:206
  40.2 14.9 %collective-permute-start.2 = (bf16[512,256]{1,0:T(8,128)(2,1)S(1)}, bf16[512,256]{1,0:T(8,128)(2,1)S(1)}, u32[]{:S(2)}, u32[]{:S(2)}) collective-permute-start(bf16[512,256]{1,0:T(8,128)(2,1)S(1)} %bitcast.34), channel_id=1, source_target_pairs={{0,4},{2,6},{4,8},{6,10},{8,12},{10,14},{12,16},{14,18},{16,20},{1... | collective-permute-start | bytes 786440 | tf_op jit(solution)/shard_map/ppermute | solution.py:207
  46.3 12.8 %collective-permute-start.3 = (bf16[512,256]{1,0:T(8,128)(2,1)S(1)}, bf16[512,256]{1,0:T(8,128)(2,1)S(1)}, u32[]{:S(2)}, u32[]{:S(2)}) collective-permute-start(bf16[512,256]{1,0:T(8,128)(2,1)S(1)} %bitcast.35), channel_id=1, source_target_pairs={{0,2},{2,4},{4,6},{6,8},{8,10},{10,12},{12,14},{14,16},{16,18},{18... | collective-permute-start | bytes 786440 | tf_op jit(solution)/shard_map/ppermute | solution.py:208
  48.2 6.9 %collective-permute-start.4 = (f32[64,512]{1,0:T(8,128)S(1)}, f32[64,512]{1,0:T(8,128)S(1)}, u32[]{:S(2)}, u32[]{:S(2)}) collective-permute-start(f32[64,512]{1,0:T(8,128)S(1)} %get-tuple-element.28), channel_id=1, source_target_pairs={{0,64},{64,0},{128,192},{192,128},{256,320},{320,256},{384,448},{4... | collective-permute-start | bytes 393224 | tf_op jit(solution)/shard_map/ppermute | solution.py:217
  59.7 4.7 %collective-permute-start.5 = (bf16[256,2304]{1,0:T(8,128)(2,1)S(1)}, bf16[256,2304]{1,0:T(8,128)(2,1)S(1)}, u32[]{:S(2)}, u32[]{:S(2)}) collective-permute-start(bf16[256,2304]{1,0:T(8,128)(2,1)S(1)} %get-tuple-element.29), channel_id=1, source_target_pairs={{0,1},{1,0},{2,3},{3,2},{4,5},{5,4},{6,7},{7,6},{8,9},{9,8},{10,11... | collective-permute-start | bytes 3538952 | tf_op jit(solution)/shard_map/ppermute | solution.py:236
  66.6 19.7 %collective-permute-start.9 = (bf16[4,512,256]{2,1,0:T(8,128)(2,1)S(1)}, bf16[4,512,256]{2,1,0:T(8,128)(2,1)S(1)}, u32[]{:S(2)}, u32[]{:S(2)}) collective-permute-start(bf16[4,512,256]{2,1,0:T(8,128)(2,1)S(1)} %get-tuple-element.36.refs_3_), channel_id=1, source_target_pairs={{0,1},{1,0},{2,3},{3,2},{4,5},{5,4},{6,7},{7,6},{8,9},{9,8},{10,11... | collective-permute-start | bytes 3145736 | tf_op jit(solution)/shard_map/ppermute | solution.py:256
  68.7 15.7 %collective-permute-start.6 = (f32[256,256]{1,0:T(8,128)S(1)}, f32[256,256]{1,0:T(8,128)S(1)}, u32[]{:S(2)}, u32[]{:S(2)}) collective-permute-start(f32[256,256]{1,0:T(8,128)S(1)} %get-tuple-element.27.refs_1_), channel_id=1, source_target_pairs={{0,32},{32,0},{1,33},{33,1},{2,34},{34,2},{3,35},{35,3},{4,36},{36... | collective-permute-start | bytes 786440 | tf_op jit(solution)/shard_map/ppermute | solution.py:243
  73.8 12.5 %collective-permute-start.7 = (f32[256,256]{1,0:T(8,128)S(1)}, f32[256,256]{1,0:T(8,128)S(1)}, u32[]{:S(2)}, u32[]{:S(2)}) collective-permute-start(f32[256,256]{1,0:T(8,128)S(1)} %get-tuple-element.30.refs_10_.refs_2_), channel_id=1, source_target_pairs={{0,32},{32,0},{1,33},{33,1},{2,34},{34,2},{3,35},{35,3},{4,36},{36... | collective-permute-start | bytes 786440 | tf_op jit(solution)/shard_map/ppermute | solution.py:247
  76.0 8.3 %collective-permute-start.8 = (f32[64,512]{1,0:T(8,128)S(1)}, f32[64,512]{1,0:T(8,128)S(1)}, u32[]{:S(2)}, u32[]{:S(2)}) collective-permute-start(f32[64,512]{1,0:T(8,128)S(1)} %get-tuple-element.35), channel_id=1, source_target_pairs={{0,192},{64,128},{128,64},{192,0},{256,448},{320,384},{384,320},{4... | collective-permute-start | bytes 393224 | tf_op jit(solution)/shard_map/ppermute | solution.py:217
  87.6 11.7 %collective-permute-start.10 = (bf16[512,256]{1,0:T(8,128)(2,1)S(1)}, bf16[512,256]{1,0:T(8,128)(2,1)S(1)}, u32[]{:S(2)}, u32[]{:S(2)}) collective-permute-start(bf16[512,256]{1,0:T(8,128)(2,1)S(1)} %get-tuple-element.38), channel_id=1, source_target_pairs={{0,2},{2,4},{4,6},{6,8},{8,10},{10,12},{12,14},{14,16},{16,18},{18... | collective-permute-start | bytes 786440 | tf_op jit(solution)/shard_map/ppermute | solution.py:268
  90.0 13.3 %collective-permute-start.11 = (bf16[512,256]{1,0:T(8,128)(2,1)S(1)}, bf16[512,256]{1,0:T(8,128)(2,1)S(1)}, u32[]{:S(2)}, u32[]{:S(2)}) collective-permute-start(bf16[512,256]{1,0:T(8,128)(2,1)S(1)} %get-tuple-element.39), channel_id=1, source_target_pairs={{0,30},{2,0},{4,2},{6,4},{8,6},{10,8},{12,10},{14,12},{16,14},{18,... | collective-permute-start | bytes 786440 | tf_op jit(solution)/shard_map/ppermute | solution.py:269
  93.5 13.2 %collective-permute-start.12 = (bf16[512,256]{1,0:T(8,128)(2,1)S(1)}, bf16[512,256]{1,0:T(8,128)(2,1)S(1)}, u32[]{:S(2)}, u32[]{:S(2)}) collective-permute-start(bf16[512,256]{1,0:T(8,128)(2,1)S(1)} %get-tuple-element.40), channel_id=1, source_target_pairs={{0,4},{2,6},{4,8},{6,10},{8,12},{10,14},{12,16},{14,18},{16,20},{1... | collective-permute-start | bytes 786440 | tf_op jit(solution)/shard_map/ppermute | solution.py:267
  96.1 3.2 %collective-permute-start.13 = (bf16[256,256]{1,0:T(8,128)(2,1)S(1)}, bf16[256,256]{1,0:T(8,128)(2,1)S(1)}, u32[]{:S(2)}, u32[]{:S(2)}) collective-permute-start(bf16[256,256]{1,0:T(8,128)(2,1)S(1)} %slice.3), channel_id=1, source_target_pairs={{0,1},{1,0},{2,3},{3,2},{4,5},{5,4},{6,7},{7,6},{8,9},{9,8},{10,11... | collective-permute-start | bytes 393224 | tf_op jit(solution)/shard_map/ppermute | solution.py:271
  108.0 13.7 %collective-permute-start.15 = (bf16[128,2048]{1,0:T(8,128)(2,1)S(1)}, bf16[128,2048]{1,0:T(8,128)(2,1)S(1)}, u32[]{:S(2)}, u32[]{:S(2)}) collective-permute-start(bf16[128,2048]{1,0:T(8,128)(2,1)S(1)} %get-tuple-element.42.refs_6_), channel_id=1, source_target_pairs={{0,32},{32,0},{1,33},{33,1},{2,34},{34,2},{3,35},{35,3},{4,36},{36... | collective-permute-start | bytes 1572872 | tf_op jit(solution)/shard_map/ppermute | solution.py:280
  115.2 26.5 %all-to-all-start.1 = ((bf16[8,64,256]{2,1,0:T(8,128)(2,1)}), bf16[8,64,256]{2,1,0:T(8,128)(2,1)S(1)}, u32[]{:S(2)}, u32[]{:S(2)}) async-start(bf16[8,64,256]{2,1,0:T(8,128)(2,1)} %bitcast.8), calls=%async_computation.1 | async-start | bytes 524288 | tf_op jit(solution)/shard_map/all_to_all | solution.py:293
  118.6 24.1 %collective-permute-start.14 = (f32[64,512]{1,0:T(8,128)S(1)}, f32[64,512]{1,0:T(8,128)S(1)}, u32[]{:S(2)}, u32[]{:S(2)}) collective-permute-start(f32[64,512]{1,0:T(8,128)S(1)} %get-tuple-element.43), channel_id=1, source_target_pairs={{0,256},{64,320},{128,384},{192,448},{256,0},{320,64},{384,128},{4... | collective-permute-start | bytes 393224 | tf_op jit(solution)/shard_map/ppermute | solution.py:217
  121.8 20.1 %copy-start.9 = (f32[1,64,512]{2,1,0:T(8,128)S(1)}, f32[1,64,512]{2,1,0:T(8,128)}, u32[]{:S(2)}) copy-start(f32[1,64,512]{2,1,0:T(8,128)} %param.12) | copy-start | bytes 393220
  121.9 20.1 %copy-start.10 = (f32[1,64,512]{2,1,0:T(8,128)S(1)}, f32[1,64,512]{2,1,0:T(8,128)}, u32[]{:S(2)}) copy-start(f32[1,64,512]{2,1,0:T(8,128)} %param.11) | copy-start | bytes 393220
  121.9 20.9 %copy-start.6 = (f32[1,64,512]{2,1,0:T(8,128)S(1)}, f32[1,64,512]{2,1,0:T(8,128)}, u32[]{:S(2)}) copy-start(f32[1,64,512]{2,1,0:T(8,128)} %param.10) | copy-start | bytes 393220
  121.9 20.9 %copy-start.8 = (f32[64,512]{1,0:T(8,128)S(1)}, f32[64,512]{1,0:T(8,128)}, u32[]{:S(2)}) copy-start(f32[64,512]{1,0:T(8,128)} %refs_3_.1) | copy-start | bytes 393220
  121.9 20.9 %copy-start.11 = (f32[64,512]{1,0:T(8,128)S(1)}, f32[64,512]{1,0:T(8,128)}, u32[]{:S(2)}) copy-start(f32[64,512]{1,0:T(8,128)} %param.14) | copy-start | bytes 393220

commit v3 on v2

v3 whole, which is shorter than its diff:
```python
import math

import jax
import jax.numpy as jnp
from jax import lax
from jax.experimental import pallas as pl
from jax.experimental.pallas import tpu as pltpu
from jax.sharding import Mesh
from jax.sharding import PartitionSpec as P

Z = ("zh", "zl")
ZC = ("zh", "zl", "c")
SWAP = [(0, 1), (1, 0)]
VMEM = 6 * 1024 * 1024
BESIDE = 20_000_000_000
BF16 = jnp.bfloat16
F32 = jnp.float32


def ring(step):
    return [(z, (z + step) % 16) for z in range(16)]


def ring_by_core(step):
    forward = [(2 * z, 2 * ((z + step) % 16)) for z in range(16)]
    backward = [(2 * z + 1, 2 * ((z - step) % 16) + 1) for z in range(16)]
    return forward + backward


def call(kernel, out_shape, flops, moved, operands, pinned=()):
    smem = pl.BlockSpec(memory_space=pltpu.SMEM)
    vmem = pl.BlockSpec(memory_space=pltpu.VMEM)
    hold = pl.BlockSpec(memory_space=pl.ANY)
    used = len(operands)

    def run(*refs):
        kernel(*refs[:used], *refs[used + len(pinned) :])

    return pl.pallas_call(
        run,
        out_shape=out_shape,
        in_specs=[smem] + [vmem] * (used - 1) + [hold] * len(pinned),
        out_specs=[vmem] * len(out_shape),
        compiler_params=pltpu.CompilerParams(vmem_limit_bytes=VMEM),
        cost_estimate=pl.CostEstimate(flops=flops, bytes_accessed=moved, transcendentals=0),
    )(*operands, *pinned)


def shape(dims, dtype):
    return jax.ShapeDtypeStruct(dims, dtype)


def block(turn, k, high):
    return pl.multiple_of((high * 4 + lax.rem(turn + k, 4)) * 128, 128)


def pack_kernel(place, w0, w1, w2, w3, packed):
    for k, weight in enumerate((w0, w1, w2, w3)):
        packed[k] = weight[...]


def preact_kernel(place, x, from_y, from_core, from_both, packed, anchor, master, partial, tokens, drift):
    drift[...] = anchor[...] - master[...]
    turn = place[0]
    half = pl.multiple_of(place[1] * 2048, 2048)
    total = jnp.zeros((512, 256), F32)
    for k in range(4):
        for high in range(4):
            start = block(turn, k, high)
            to = pl.ds(high * 128, 128)
            tokens[k, 0:128, to] = x[:, pl.ds(pl.multiple_of(half + start, 128), 128)]
            tokens[k, 128:256, to] = from_y[:, pl.ds(start, 128)]
            tokens[k, 256:384, to] = from_core[:, pl.ds(start, 128)]
            tokens[k, 384:512, to] = from_both[:, pl.ds(start, 128)]
        total += jnp.dot(tokens[k], packed[k], preferred_element_type=F32)
    for j in range(4):
        partial[:, j * 256 : j * 256 + 256] = total[j * 128 : j * 128 + 128, :]


def delta_kernel(
    inv_root, place, partial, other, cotangent, from_y, from_core, from_both, tokens, delta, g0, g1, g2, g3
):
    keys = pl.multiple_of(place[2] * 256, 256)
    upstream = (
        cotangent[:, pl.ds(keys, 256)],
        from_y[:, pl.ds(pl.multiple_of(2048 + keys, 256), 256)],
        from_core[:, 2048:2304],
        from_both[:, pl.ds(pl.multiple_of(2048 + keys, 256), 256)],
    )
    for j in range(4):
        i = j ^ 1
        preact = partial[:, j * 256 : j * 256 + 256] + other[:, i * 256 : i * 256 + 256]
        preact = preact * inv_root
        gating = jax.nn.sigmoid(preact)
        derivative = gating * (1.0 + preact * (1.0 - gating))
        rows = upstream[j].astype(F32) * derivative * inv_root
        delta[j * 128 : j * 128 + 128, :] = rows.astype(BF16)
    for k, grad in ((2, g2), (1, g1), (3, g3), (0, g0)):
        full = lax.dot_general(
            tokens[k], delta[...], (((0,), (0,)), ((), ())), preferred_element_type=F32
        )
        grad[...] = full.astype(grad.dtype)


def back(delta, weight):
    return lax.dot_general(delta, weight, (((1,), (1,)), ((), ())), preferred_element_type=F32)


def back_kernel(place, delta, near, weight, near_weight, out, away):
    turn = place[0]
    for k in range(4):
        total = back(delta[0:256, :], weight[k]) + back(near[...], near_weight[k])
        total = total.astype(BF16)
        for high in range(4):
            to = pl.ds(block(turn, k, high), 128)
            out[:, to] = total[0:128, high * 128 : high * 128 + 128]
            away[:, to] = total[128:256, high * 128 : high * 128 + 128]


def join_kernel(place, stay, far, out, sems):
    copies = []
    for source, y in ((stay, place[1]), (far, 1 - place[1])):
        to = out.at[:, pl.ds(pl.multiple_of(y * 2048, 2048), 2048)]
        copies.append(pltpu.make_async_copy(source, to, sems.at[len(copies)]))
    for copy in copies:
        copy.start()
    for copy in copies:
        copy.wait()


def total_kernel(place, g0, after, before, far, drift, total, kept):
    kept[...] = drift[...]
    summed = g0[...] + after[...].astype(F32) + before[...].astype(F32) + far[...].astype(F32)
    total[...] = summed.astype(BF16)


def sum_kernel(place, parts, out):
    for core in range(2):
        total = parts[core].astype(F32)
        for high in range(1, 4):
            total += parts[2 * high + core].astype(F32)
        out[:, core * 256 : core * 256 + 256] = total


def body(inputs, upstream, params, first_moment, second_moment, anchor, outer_moment, step_count):
    tokens_in = inputs[0]
    cotangent = upstream[0]
    master = params[0]
    rows, features = tokens_in.shape
    inv_root = 1.0 / math.sqrt(features)
    mine = lax.axis_index("y")
    core = lax.axis_index("c")
    place = jnp.stack([lax.axis_index("zl"), mine, core]).astype(jnp.int32)

    own = master.astype(BF16).reshape(64, 2, 256).transpose(1, 0, 2)
    own = jnp.broadcast_to(own[None], (4, 2, 64, 256)).reshape(8, 64, 256)
    same = lax.all_to_all(own, ("zh", "c"), split_axis=0, concat_axis=0).reshape(512, 256)
    weight = [
        same,
        lax.ppermute(same, Z, ring(-1)),
        lax.ppermute(same, ZC, ring_by_core(2)),
        lax.ppermute(same, Z, ring(1)),
    ]

    replicas = lax.axis_size("replica")

    def fold(value, flip):
        if flip >= replicas:
            return value
        pairs = [(r, r ^ flip) for r in range(replicas)]
        return value + lax.ppermute(value, "replica", pairs)

    def columns(y, keys):
        return jnp.concatenate(
            [lax.dynamic_slice_in_dim(tokens_in, y * 2048, 2048, axis=1), keys], axis=1
        )

    from_y = lax.ppermute(columns(1 - mine, cotangent), "y", SWAP)
    near_keys = jnp.where(core == 0, cotangent[:, 256:], cotangent[:, :256])
    from_core = lax.ppermute(columns(mine, near_keys), "c", SWAP)
    square = (from_y, from_core, lax.ppermute(from_y, "c", SWAP))

    (packed,) = call(
        pack_kernel, [shape((4, 512, 256), BF16)], BESIDE, 2 << 20, (place, *weight)
    )
    partial, tokens, drift = call(
        preact_kernel,
        [
            shape((rows, 1024), F32),
            shape((4, 512, 512), BF16),
            shape((64, 512), F32),
        ],
        2 * 512 * 2048 * 256,
        6 << 20,
        (place, tokens_in, *square, packed, anchor, master),
    )
    other = lax.ppermute(partial, "y", SWAP)
    drift = fold(drift, 1)
    near_weight = lax.ppermute(packed, "c", SWAP)
    delta, g0, g1, g2, g3 = call(
        lambda *refs: delta_kernel(inv_root, *refs),
        [shape((512, 256), BF16), shape((512, 256), F32)]
        + [shape((512, 256), BF16)] * 3,
        2 * 512 * 2048 * 256,
        5 << 20,
        (place, partial, other, cotangent, *square, tokens),
        (drift,),
    )
    far = lax.ppermute(g2, ZC, ring_by_core(2))
    after = lax.ppermute(g1, Z, ring(1))
    before = lax.ppermute(g3, Z, ring(-1))

    total, drift = call(
        total_kernel,
        [shape((512, 256), BF16), shape((64, 512), F32)],
        0,
        2 << 20,
        (place, g0, after, before, far, fold(drift, 3)),
    )
    parts = lax.all_to_all(total.reshape(8, 64, 256), ("zh", "c"), split_axis=0, concat_axis=0)
    (weight_grad,) = call(sum_kernel, [shape((64, 512), F32)], BESIDE, 1 << 19, (place, parts))
    summed = fold(drift, 4)

    near_delta = lax.ppermute(delta[256:], "c", SWAP)
    stay, away = call(
        back_kernel,
        [shape((rows, 2048), BF16)] * 2,
        2 * 256 * 2048 * 512,
        4 << 20,
        (place, delta, near_delta, packed, near_weight),
        (total,),
    )
    back_far = lax.ppermute(away, "y", SWAP)
    input_grad = jnp.concatenate(
        [jnp.where(mine == 0, stay, back_far), jnp.where(mine == 0, back_far, stay)], axis=1
    )

    new_first = 0.9 * first_moment[0] + 0.1 * weight_grad
    new_second = 0.95 * second_moment[0] + 0.05 * weight_grad * weight_grad
    steps = step_count[0].astype(F32)
    bias_one = 1.0 - jnp.power(jnp.float32(0.9), steps)
    bias_two = 1.0 - jnp.power(jnp.float32(0.95), steps)
    update = new_first / bias_one / (jnp.sqrt(new_second / bias_two) + 1e-08)
    inner = master - 0.1 * (update + 0.1 * master)
    outer_grad = summed / replicas
    new_outer = 0.9 * outer_moment + outer_grad
    new_anchor = anchor - 0.7 * (outer_grad + 0.9 * new_outer)
    new_params = 0.5 * new_anchor + 0.5 * inner
    return (
        new_params[None],
        new_first[None],
        new_second[None],
        new_anchor,
        new_outer,
        input_grad[None],
    )


def solution(mesh):
    replicas = mesh.shape["replica"]
    split = Mesh(mesh.devices.reshape(replicas, 2, 4, 4, 2), ("replica", "y", "zh", "zl", "c"))
    fsdp = ("y", "zh", "zl", "c")
    sharded = P("replica", fsdp, None)
    shared = P(fsdp, None)
    return jax.shard_map(
        body,
        mesh=split,
        in_specs=(sharded, sharded, sharded, sharded, sharded, shared, shared, P()),
        out_specs=(sharded, sharded, sharded, shared, shared, sharded),
        check_vma=False,
    )
```

time: 144 us -> 140 us (0.972)
  the two profiles are of different devices: /device:TPU:32 before, /device:TPU:38 now
where the time goes in v3:
time: 140 us; the launch traced here: 139 us
  starting transfers between devices  68.3 us (49%)
  waiting for transfers between devices  56.1 us (40%)
  Pallas kernels  6.98 us (5%)
  other arithmetic  4.93 us (4%)
  between operations  1.71 us (1%)
    all_to_all x1, waiting for transfers between devices, body(): lax.all_to_all(own, ('zh', 'c'), split_axis=0, concat_axis=0)  15.1 us
    all_to_all x1, starting transfers between devices, body(): lax.all_to_all(own, ('zh', 'c'), split_axis=0, concat_axis=0)  14.3 us
    all_to_all x1, waiting for transfers between devices, body(): lax.all_to_all(total.reshape(8, 64, 256), ('zh', 'c'), split_axis=0, conc...  14.1 us
    ppermute x3, waiting for transfers between devices, fold(): return value + lax.ppermute(value, 'replica', pairs)  10.5 us
    ppermute x3, starting transfers between devices, fold(): return value + lax.ppermute(value, 'replica', pairs)  7.7 us
    pallas_call x6, Pallas kernels, call(): pl.pallas_call(run, out_shape=out_shape, in_specs=[smem] + [vmem] * (used...  6.98 us
    ppermute x1, starting transfers between devices, body(): lax.ppermute(same, ZC, ring_by_core(2))  6.01 us
    ppermute x1, waiting for transfers between devices, body(): back_far = lax.ppermute(away, 'y', SWAP)  5.29 us
  transfers between devices with their start and end apart: 18, of which 9 were waited for; matrix products, arithmetic and copies ran while one was open for 2% of the time, Pallas kernels for 4%

profile of v3, /device:TPU:38, one launch (start us, length us, event | category | flops | bytes accessed | tf_op | source)
XLA Modules:
  0.0 138.9 jit_solution(14613636030911825359)
XLA Ops:
  0.6 1.0 convert_element_type.11
  1.7 0.7 broadcast_in_dim.18
  2.4 14.3 %all-to-all-start = ((bf16[8,64,256]{2,1,0:T(8,128)(2,1)}), bf16[8,64,256]{2,1,0:T(8,128)(2,1)S(1)}, u32[]{:S(2)}, u32[]{:S(2)}) async-start(bf16[8,64,256]{2,1,0:T(8,128)(2,1)} %bitcast.8), calls=%async_computation | async-start | bytes 524288 | tf_op jit(solution)/shard_map/all_to_all | solution.py:157
  16.7 0.1 dynamic-slice_bitcast_fusion
  16.9 0.9 pad_maximum_fusion
  17.7 5.1 %collective-permute-start = (bf16[128,2560]{1,0:T(8,128)(2,1)}, bf16[128,2560]{1,0:T(8,128)(2,1)S(1)}, u32[]{:S(2)}, u32[]{:S(2)}) collective-permute-start(bf16[128,2560]{1,0:T(8,128)(2,1)} %pad_maximum_fusion), channel_id=1, source_target_pairs={{0,32},{32,0},{1,33},{33,1},{2,34},{34,2},{3,35},{35,3},{4,36},{36... | collective-permute-start | bytes 1966088 | tf_op jit(solution)/shard_map/ppermute | solution.py:178
  22.9 15.1 %all-to-all-done = bf16[8,64,256]{2,1,0:T(8,128)(2,1)S(1)} async-done(((bf16[8,64,256]{2,1,0:T(8,128)(2,1)}), bf16[8,64,256]{2,1,0:T(8,128)(2,1)S(1)}, u32[]{:S(2)}, u32[]{:S(2)}) %all-to-all-start) | async-done | bytes 262176 | tf_op jit(solution)/shard_map/all_to_all | solution.py:157
  38.0 1.9 %collective-permute-start.3 = (bf16[512,256]{1,0:T(8,128)(2,1)S(1)}, bf16[512,256]{1,0:T(8,128)(2,1)S(1)}, u32[]{:S(2)}, u32[]{:S(2)}) collective-permute-start(bf16[512,256]{1,0:T(8,128)(2,1)S(1)} %bitcast.42), channel_id=1, source_target_pairs={{0,30},{2,0},{4,2},{6,4},{8,6},{10,8},{12,10},{14,12},{16,14},{18,... | collective-permute-start | bytes 786440 | tf_op jit(solution)/shard_map/ppermute | solution.py:160
  39.9 6.0 %collective-permute-start.4 = (bf16[512,256]{1,0:T(8,128)(2,1)S(1)}, bf16[512,256]{1,0:T(8,128)(2,1)S(1)}, u32[]{:S(2)}, u32[]{:S(2)}) collective-permute-start(bf16[512,256]{1,0:T(8,128)(2,1)S(1)} %bitcast.43), channel_id=1, source_target_pairs={{0,4},{2,6},{4,8},{6,10},{8,12},{10,14},{12,16},{14,18},{16,20},{1... | collective-permute-start | bytes 786440 | tf_op jit(solution)/shard_map/ppermute | solution.py:161
  45.9 1.9 %collective-permute-start.5 = (bf16[512,256]{1,0:T(8,128)(2,1)S(1)}, bf16[512,256]{1,0:T(8,128)(2,1)}, u32[]{:S(2)}, u32[]{:S(2)}) collective-permute-start(bf16[512,256]{1,0:T(8,128)(2,1)S(1)} %bitcast.44), channel_id=1, source_target_pairs={{0,2},{2,4},{4,6},{6,8},{8,10},{10,12},{12,14},{14,16},{16,18},{18... | collective-permute-start | bytes 786440 | tf_op jit(solution)/shard_map/ppermute | solution.py:162
  47.8 0.9 pad_maximum_fusion.1
  48.7 1.9 %collective-permute-start.1 = (bf16[128,2304]{1,0:T(8,128)(2,1)}, bf16[128,2304]{1,0:T(8,128)(2,1)S(1)}, u32[]{:S(2)}, u32[]{:S(2)}) collective-permute-start(bf16[128,2304]{1,0:T(8,128)(2,1)} %pad_maximum_fusion.1), channel_id=1, source_target_pairs={{0,1},{1,0},{2,3},{3,2},{4,5},{5,4},{6,7},{7,6},{8,9},{9,8},{10,11... | collective-permute-start | bytes 1769480 | tf_op jit(solution)/shard_map/ppermute | solution.py:180
  50.6 0.1 pad_add_fusion.refs_0_
  50.7 2.5 %collective-permute-start.2 = (bf16[128,2560]{1,0:T(8,128)(2,1)S(1)}, bf16[128,2560]{1,0:T(8,128)(2,1)S(1)}, u32[]{:S(2)}, u32[]{:S(2)}) collective-permute-start(bf16[128,2560]{1,0:T(8,128)(2,1)S(1)} %collective-permute-done.refs_2_.refs_4_), channel_id=1, source_target_pairs={{0,1},{1,0},{2,3},{3,2},{4,5},{5,4},{6,7},{7,6},{8,9},{9,8},{10,11... | collective-permute-start | bytes 1966088 | tf_op jit(solution)/shard_map/ppermute | solution.py:181
  53.2 0.0 collective-permute-done.3.refs_2_
  53.2 0.8 collective-permute-done.4.refs_3_
  54.1 4.7 %collective-permute-done.5.refs_4_ = bf16[512,256]{1,0:T(8,128)(2,1)} collective-permute-done((bf16[512,256]{1,0:T(8,128)(2,1)S(1)}, bf16[512,256]{1,0:T(8,128)(2,1)}, u32[]{:S(2)}, u32[]{:S(2)}) %collective-permute-start.5) | collective-permute-done | bytes 262176 | tf_op jit(solution)/shard_map/ppermute | solution.py:162
  58.8 1.0 shard_map.127.refs_5_.refs_3_
  59.8 1.9 %collective-permute-start.14 = (bf16[4,512,256]{2,1,0:T(8,128)(2,1)S(1)}, bf16[4,512,256]{2,1,0:T(8,128)(2,1)S(1)}, u32[]{:S(2)}, u32[]{:S(2)}) collective-permute-start(bf16[4,512,256]{2,1,0:T(8,128)(2,1)S(1)} %shard_map.127.refs_5_.refs_3_), channel_id=1, source_target_pairs={{0,1},{1,0},{2,3},{3,2},{4,5},{5,4},{6,7},{7,6},{8,9},{9,8},{10,11... | collective-permute-start | bytes 3145736 | tf_op jit(solution)/shard_map/ppermute | solution.py:199
  61.7 0.0 collective-permute-done.2.refs_4_.refs_6_
  61.8 1.4 shard_map.128
  63.2 5.1 %collective-permute-start.6 = (f32[128,1024]{1,0:T(8,128)S(1)}, f32[128,1024]{1,0:T(8,128)S(1)}, u32[]{:S(2)}, u32[]{:S(2)}) collective-permute-start(f32[128,1024]{1,0:T(8,128)S(1)} %get-tuple-element.18.refs_1_), channel_id=1, source_target_pairs={{0,32},{32,0},{1,33},{33,1},{2,34},{34,2},{3,35},{35,3},{4,36},{36... | collective-permute-start | bytes 1572872 | tf_op jit(solution)/shard_map/ppermute | solution.py:197
  68.3 2.7 %collective-permute-start.7 = (f32[64,512]{1,0:T(8,128)S(1)}, f32[64,512]{1,0:T(8,128)S(1)}, u32[]{:S(2)}, u32[]{:S(2)}) collective-permute-start(f32[64,512]{1,0:T(8,128)S(1)} %get-tuple-element.20), channel_id=1, source_target_pairs={{0,64},{64,0},{128,192},{192,128},{256,320},{320,256},{384,448},{4... | collective-permute-start | bytes 393224 | tf_op jit(solution)/shard_map/ppermute | solution.py:171
  71.0 4.8 %collective-permute-done.7 = f32[64,512]{1,0:T(8,128)S(1)} collective-permute-done((f32[64,512]{1,0:T(8,128)S(1)}, f32[64,512]{1,0:T(8,128)S(1)}, u32[]{:S(2)}, u32[]{:S(2)}) %collective-permute-start.7) | collective-permute-done | bytes 131104 | tf_op jit(solution)/shard_map/ppermute | solution.py:171
  75.8 5.1 %collective-permute-done.6.refs_2_ = f32[128,1024]{1,0:T(8,128)S(1)} collective-permute-done((f32[128,1024]{1,0:T(8,128)S(1)}, f32[128,1024]{1,0:T(8,128)S(1)}, u32[]{:S(2)}, u32[]{:S(2)}) %collective-permute-start.6) | collective-permute-done | bytes 524320 | tf_op jit(solution)/shard_map/ppermute | solution.py:197
  80.9 1.4 shard_map.129
  82.3 2.4 %collective-permute-start.8 = (bf16[512,256]{1,0:T(8,128)(2,1)S(1)}, bf16[512,256]{1,0:T(8,128)(2,1)S(1)}, u32[]{:S(2)}, u32[]{:S(2)}) collective-permute-start(bf16[512,256]{1,0:T(8,128)(2,1)S(1)} %get-tuple-element.22), channel_id=1, source_target_pairs={{0,2},{2,4},{4,6},{6,8},{8,10},{10,12},{12,14},{14,16},{16,18},{18... | collective-permute-start | bytes 786440 | tf_op jit(solution)/shard_map/ppermute | solution.py:210
  84.6 3.5 %collective-permute-start.9 = (bf16[512,256]{1,0:T(8,128)(2,1)S(1)}, bf16[512,256]{1,0:T(8,128)(2,1)S(1)}, u32[]{:S(2)}, u32[]{:S(2)}) collective-permute-start(bf16[512,256]{1,0:T(8,128)(2,1)S(1)} %get-tuple-element.23), channel_id=1, source_target_pairs={{0,30},{2,0},{4,2},{6,4},{8,6},{10,8},{12,10},{14,12},{16,14},{18,... | collective-permute-start | bytes 786440 | tf_op jit(solution)/shard_map/ppermute | solution.py:211
  88.1 2.6 %collective-permute-start.10 = (bf16[512,256]{1,0:T(8,128)(2,1)S(1)}, bf16[512,256]{1,0:T(8,128)(2,1)S(1)}, u32[]{:S(2)}, u32[]{:S(2)}) collective-permute-start(bf16[512,256]{1,0:T(8,128)(2,1)S(1)} %get-tuple-element.24), channel_id=1, source_target_pairs={{0,4},{2,6},{4,8},{6,10},{8,12},{10,14},{12,16},{14,18},{16,20},{1... | collective-permute-start | bytes 786440 | tf_op jit(solution)/shard_map/ppermute | solution.py:209
  90.8 2.4 %collective-permute-start.11 = (f32[64,512]{1,0:T(8,128)S(1)}, f32[64,512]{1,0:T(8,128)S(1)}, u32[]{:S(2)}, u32[]{:S(2)}) collective-permute-start(f32[64,512]{1,0:T(8,128)S(1)} %add.42.refs_8_), channel_id=1, source_target_pairs={{0,192},{64,128},{128,64},{192,0},{256,448},{320,384},{384,320},{4... | collective-permute-start | bytes 393224 | tf_op jit(solution)/shard_map/ppermute | solution.py:171
  93.2 5.8 %collective-permute-done.11 = f32[64,512]{1,0:T(8,128)S(1)} collective-permute-done((f32[64,512]{1,0:T(8,128)S(1)}, f32[64,512]{1,0:T(8,128)S(1)}, u32[]{:S(2)}, u32[]{:S(2)}) %collective-permute-start.11) | collective-permute-done | bytes 131104 | tf_op jit(solution)/shard_map/ppermute | solution.py:171
  99.0 1.9 %collective-permute-start.13 = (bf16[256,256]{1,0:T(8,128)(2,1)S(1)}, bf16[256,256]{1,0:T(8,128)(2,1)S(1)}, u32[]{:S(2)}, u32[]{:S(2)}) collective-permute-start(bf16[256,256]{1,0:T(8,128)(2,1)S(1)} %slice.11), channel_id=1, source_target_pairs={{0,1},{1,0},{2,3},{3,2},{4,5},{5,4},{6,7},{7,6},{8,9},{9,8},{10,11... | collective-permute-start | bytes 393224 | tf_op jit(solution)/shard_map/ppermute | solution.py:224
  100.9 0.0 collective-permute-done.9.refs_3_
  100.9 0.4 collective-permute-done.10.refs_4_
  101.3 1.3 shard_map.130
  102.7 0.0 collective-permute-done.13.refs_2_
  102.7 0.0 collective-permute-done.14.refs_4_
  102.7 1.3 shard_map.132
  103.9 5.1 %collective-permute-start.15 = (bf16[128,2048]{1,0:T(8,128)(2,1)S(1)}, bf16[128,2048]{1,0:T(8,128)(2,1)S(1)}, u32[]{:S(2)}, u32[]{:S(2)}) collective-permute-start(bf16[128,2048]{1,0:T(8,128)(2,1)S(1)} %get-tuple-element.29), channel_id=1, source_target_pairs={{0,32},{32,0},{1,33},{33,1},{2,34},{34,2},{3,35},{35,3},{4,36},{36... | collective-permute-start | bytes 1572872 | tf_op jit(solution)/shard_map/ppermute | solution.py:233
  109.8 4.5 %all-to-all-start.1 = ((bf16[8,64,256]{2,1,0:T(8,128)(2,1)}), bf16[8,64,256]{2,1,0:T(8,128)(2,1)S(1)}, u32[]{:S(2)}, u32[]{:S(2)}) async-start(bf16[8,64,256]{2,1,0:T(8,128)(2,1)} %bitcast.12), calls=%async_computation.1 | async-start | bytes 524288 | tf_op jit(solution)/shard_map/all_to_all | solution.py:220
  114.2 2.6 %collective-permute-start.12 = (f32[64,512]{1,0:T(8,128)S(1)}, f32[64,512]{1,0:T(8,128)S(1)}, u32[]{:S(2)}, u32[]{:S(2)}) collective-permute-start(f32[64,512]{1,0:T(8,128)S(1)} %get-tuple-element.25), channel_id=1, source_target_pairs={{0,256},{64,320},{128,384},{192,448},{256,0},{320,64},{384,128},{4... | collective-permute-start | bytes 393224 | tf_op jit(solution)/shard_map/ppermute | solution.py:171
  116.8 5.3 %collective-permute-done.15 = bf16[128,2048]{1,0:T(8,128)(2,1)S(1)} collective-permute-done((bf16[128,2048]{1,0:T(8,128)(2,1)S(1)}, bf16[128,2048]{1,0:T(8,128)(2,1)S(1)}, u32[]{:S(2)}, u32[]{:S(2)}) %collective-permute-start.15) | collective-permute-done | bytes 524320 | tf_op jit(solution)/shard_map/ppermute | solution.py:233
  122.1 0.1 broadcast_select_fusion.1
  122.3 1.0 maximum_bitcast_fusion
  123.3 14.1 %all-to-all-done.1.refs_1_ = bf16[8,64,256]{2,1,0:T(8,128)(2,1)S(1)} async-done(((bf16[8,64,256]{2,1,0:T(8,128)(2,1)}), bf16[8,64,256]{2,1,0:T(8,128)(2,1)S(1)}, u32[]{:S(2)}, u32[]{:S(2)}) %all-to-all-start.1) | async-done | bytes 262176 | tf_op jit(solution)/shard_map/all_to_all | solution.py:220
  137.4 0.6 shard_map.131
  138.0 0.0 collective-permute-done.12
  138.0 0.9 multiply_bitcast_fusion
  (23 shorter events, 0.1 us)
Async XLA Ops:
  0.6 16.1 %copy-start = (bf16[1,128,4096]{2,1,0:T(8,128)(2,1)S(1)}, bf16[1,128,4096]{2,1,0:T(8,128)(2,1)}, u32[]{:S(2)}) copy-start(bf16[1,128,4096]{2,1,0:T(8,128)(2,1)} %param.8) | copy-start | bytes 3145732
  2.4 14.4 %copy-start.1 = (bf16[1,128,512]{2,1,0:T(8,128)(2,1)S(1)}, bf16[1,128,512]{2,1,0:T(8,128)(2,1)}, u32[]{:S(2)}) copy-start(bf16[1,128,512]{2,1,0:T(8,128)(2,1)} %param.9) | copy-start | bytes 393220
  2.4 35.6 %all-to-all-start = ((bf16[8,64,256]{2,1,0:T(8,128)(2,1)}), bf16[8,64,256]{2,1,0:T(8,128)(2,1)S(1)}, u32[]{:S(2)}, u32[]{:S(2)}) async-start(bf16[8,64,256]{2,1,0:T(8,128)(2,1)} %bitcast.8), calls=%async_computation | async-start | bytes 524288 | tf_op jit(solution)/shard_map/all_to_all | solution.py:157
  17.7 33.0 %collective-permute-start = (bf16[128,2560]{1,0:T(8,128)(2,1)}, bf16[128,2560]{1,0:T(8,128)(2,1)S(1)}, u32[]{:S(2)}, u32[]{:S(2)}) collective-permute-start(bf16[128,2560]{1,0:T(8,128)(2,1)} %pad_maximum_fusion), channel_id=1, source_target_pairs={{0,32},{32,0},{1,33},{33,1},{2,34},{34,2},{3,35},{35,3},{4,36},{36... | collective-permute-start | bytes 1966088 | tf_op jit(solution)/shard_map/ppermute | solution.py:178
  38.0 15.3 %collective-permute-start.3 = (bf16[512,256]{1,0:T(8,128)(2,1)S(1)}, bf16[512,256]{1,0:T(8,128)(2,1)S(1)}, u32[]{:S(2)}, u32[]{:S(2)}) collective-permute-start(bf16[512,256]{1,0:T(8,128)(2,1)S(1)} %bitcast.42), channel_id=1, source_target_pairs={{0,30},{2,0},{4,2},{6,4},{8,6},{10,8},{12,10},{14,12},{16,14},{18,... | collective-permute-start | bytes 786440 | tf_op jit(solution)/shard_map/ppermute | solution.py:160
  39.9 14.2 %collective-permute-start.4 = (bf16[512,256]{1,0:T(8,128)(2,1)S(1)}, bf16[512,256]{1,0:T(8,128)(2,1)S(1)}, u32[]{:S(2)}, u32[]{:S(2)}) collective-permute-start(bf16[512,256]{1,0:T(8,128)(2,1)S(1)} %bitcast.43), channel_id=1, source_target_pairs={{0,4},{2,6},{4,8},{6,10},{8,12},{10,14},{12,16},{14,18},{16,20},{1... | collective-permute-start | bytes 786440 | tf_op jit(solution)/shard_map/ppermute | solution.py:161
  45.9 12.9 %collective-permute-start.5 = (bf16[512,256]{1,0:T(8,128)(2,1)S(1)}, bf16[512,256]{1,0:T(8,128)(2,1)}, u32[]{:S(2)}, u32[]{:S(2)}) collective-permute-start(bf16[512,256]{1,0:T(8,128)(2,1)S(1)} %bitcast.44), channel_id=1, source_target_pairs={{0,2},{2,4},{4,6},{6,8},{8,10},{10,12},{12,14},{14,16},{16,18},{18... | collective-permute-start | bytes 786440 | tf_op jit(solution)/shard_map/ppermute | solution.py:162
  48.7 13.0 %collective-permute-start.1 = (bf16[128,2304]{1,0:T(8,128)(2,1)}, bf16[128,2304]{1,0:T(8,128)(2,1)S(1)}, u32[]{:S(2)}, u32[]{:S(2)}) collective-permute-start(bf16[128,2304]{1,0:T(8,128)(2,1)} %pad_maximum_fusion.1), channel_id=1, source_target_pairs={{0,1},{1,0},{2,3},{3,2},{4,5},{5,4},{6,7},{7,6},{8,9},{9,8},{10,11... | collective-permute-start | bytes 1769480 | tf_op jit(solution)/shard_map/ppermute | solution.py:180
  50.7 11.1 %copy-start.2 = (f32[1,64,512]{2,1,0:T(8,128)S(1)}, f32[1,64,512]{2,1,0:T(8,128)}, u32[]{:S(2)}) copy-start(f32[1,64,512]{2,1,0:T(8,128)} %param.10) | copy-start | bytes 393220
  50.7 11.1 %copy-start.3 = (f32[64,512]{1,0:T(8,128)S(1)}, f32[64,512]{1,0:T(8,128)}, u32[]{:S(2)}) copy-start(f32[64,512]{1,0:T(8,128)} %refs_6_.1) | copy-start | bytes 393220
  50.7 11.1 %collective-permute-start.2 = (bf16[128,2560]{1,0:T(8,128)(2,1)S(1)}, bf16[128,2560]{1,0:T(8,128)(2,1)S(1)}, u32[]{:S(2)}, u32[]{:S(2)}) collective-permute-start(bf16[128,2560]{1,0:T(8,128)(2,1)S(1)} %collective-permute-done.refs_2_.refs_4_), channel_id=1, source_target_pairs={{0,1},{1,0},{2,3},{3,2},{4,5},{5,4},{6,7},{7,6},{8,9},{9,8},{10,11... | collective-permute-start | bytes 1966088 | tf_op jit(solution)/shard_map/ppermute | solution.py:181
  59.8 42.9 %collective-permute-start.14 = (bf16[4,512,256]{2,1,0:T(8,128)(2,1)S(1)}, bf16[4,512,256]{2,1,0:T(8,128)(2,1)S(1)}, u32[]{:S(2)}, u32[]{:S(2)}) collective-permute-start(bf16[4,512,256]{2,1,0:T(8,128)(2,1)S(1)} %shard_map.127.refs_5_.refs_3_), channel_id=1, source_target_pairs={{0,1},{1,0},{2,3},{3,2},{4,5},{5,4},{6,7},{7,6},{8,9},{9,8},{10,11... | collective-permute-start | bytes 3145736 | tf_op jit(solution)/shard_map/ppermute | solution.py:199
  63.2 17.7 %collective-permute-start.6 = (f32[128,1024]{1,0:T(8,128)S(1)}, f32[128,1024]{1,0:T(8,128)S(1)}, u32[]{:S(2)}, u32[]{:S(2)}) collective-permute-start(f32[128,1024]{1,0:T(8,128)S(1)} %get-tuple-element.18.refs_1_), channel_id=1, source_target_pairs={{0,32},{32,0},{1,33},{33,1},{2,34},{34,2},{3,35},{35,3},{4,36},{36... | collective-permute-start | bytes 1572872 | tf_op jit(solution)/shard_map/ppermute | solution.py:197
  68.3 7.5 %collective-permute-start.7 = (f32[64,512]{1,0:T(8,128)S(1)}, f32[64,512]{1,0:T(8,128)S(1)}, u32[]{:S(2)}, u32[]{:S(2)}) collective-permute-start(f32[64,512]{1,0:T(8,128)S(1)} %get-tuple-element.20), channel_id=1, source_target_pairs={{0,64},{64,0},{128,192},{192,128},{256,320},{320,256},{384,448},{4... | collective-permute-start | bytes 393224 | tf_op jit(solution)/shard_map/ppermute | solution.py:171
  82.3 18.6 %collective-permute-start.8 = (bf16[512,256]{1,0:T(8,128)(2,1)S(1)}, bf16[512,256]{1,0:T(8,128)(2,1)S(1)}, u32[]{:S(2)}, u32[]{:S(2)}) collective-permute-start(bf16[512,256]{1,0:T(8,128)(2,1)S(1)} %get-tuple-element.22), channel_id=1, source_target_pairs={{0,2},{2,4},{4,6},{6,8},{8,10},{10,12},{12,14},{14,16},{16,18},{18... | collective-permute-start | bytes 786440 | tf_op jit(solution)/shard_map/ppermute | solution.py:210
  84.6 16.3 %collective-permute-start.9 = (bf16[512,256]{1,0:T(8,128)(2,1)S(1)}, bf16[512,256]{1,0:T(8,128)(2,1)S(1)}, u32[]{:S(2)}, u32[]{:S(2)}) collective-permute-start(bf16[512,256]{1,0:T(8,128)(2,1)S(1)} %get-tuple-element.23), channel_id=1, source_target_pairs={{0,30},{2,0},{4,2},{6,4},{8,6},{10,8},{12,10},{14,12},{16,14},{18,... | collective-permute-start | bytes 786440 | tf_op jit(solution)/shard_map/ppermute | solution.py:211
  88.1 13.2 %collective-permute-start.10 = (bf16[512,256]{1,0:T(8,128)(2,1)S(1)}, bf16[512,256]{1,0:T(8,128)(2,1)S(1)}, u32[]{:S(2)}, u32[]{:S(2)}) collective-permute-start(bf16[512,256]{1,0:T(8,128)(2,1)S(1)} %get-tuple-element.24), channel_id=1, source_target_pairs={{0,4},{2,6},{4,8},{6,10},{8,12},{10,14},{12,16},{14,18},{16,20},{1... | collective-permute-start | bytes 786440 | tf_op jit(solution)/shard_map/ppermute | solution.py:209
  90.8 8.2 %collective-permute-start.11 = (f32[64,512]{1,0:T(8,128)S(1)}, f32[64,512]{1,0:T(8,128)S(1)}, u32[]{:S(2)}, u32[]{:S(2)}) collective-permute-start(f32[64,512]{1,0:T(8,128)S(1)} %add.42.refs_8_), channel_id=1, source_target_pairs={{0,192},{64,128},{128,64},{192,0},{256,448},{320,384},{384,320},{4... | collective-permute-start | bytes 393224 | tf_op jit(solution)/shard_map/ppermute | solution.py:171
  99.0 3.7 %collective-permute-start.13 = (bf16[256,256]{1,0:T(8,128)(2,1)S(1)}, bf16[256,256]{1,0:T(8,128)(2,1)S(1)}, u32[]{:S(2)}, u32[]{:S(2)}) collective-permute-start(bf16[256,256]{1,0:T(8,128)(2,1)S(1)} %slice.11), channel_id=1, source_target_pairs={{0,1},{1,0},{2,3},{3,2},{4,5},{5,4},{6,7},{7,6},{8,9},{9,8},{10,11... | collective-permute-start | bytes 393224 | tf_op jit(solution)/shard_map/ppermute | solution.py:224
  103.9 18.2 %collective-permute-start.15 = (bf16[128,2048]{1,0:T(8,128)(2,1)S(1)}, bf16[128,2048]{1,0:T(8,128)(2,1)S(1)}, u32[]{:S(2)}, u32[]{:S(2)}) collective-permute-start(bf16[128,2048]{1,0:T(8,128)(2,1)S(1)} %get-tuple-element.29), channel_id=1, source_target_pairs={{0,32},{32,0},{1,33},{33,1},{2,34},{34,2},{3,35},{35,3},{4,36},{36... | collective-permute-start | bytes 1572872 | tf_op jit(solution)/shard_map/ppermute | solution.py:233
  109.8 27.6 %all-to-all-start.1 = ((bf16[8,64,256]{2,1,0:T(8,128)(2,1)}), bf16[8,64,256]{2,1,0:T(8,128)(2,1)S(1)}, u32[]{:S(2)}, u32[]{:S(2)}) async-start(bf16[8,64,256]{2,1,0:T(8,128)(2,1)} %bitcast.12), calls=%async_computation.1 | async-start | bytes 524288 | tf_op jit(solution)/shard_map/all_to_all | solution.py:220
  114.2 23.8 %collective-permute-start.12 = (f32[64,512]{1,0:T(8,128)S(1)}, f32[64,512]{1,0:T(8,128)S(1)}, u32[]{:S(2)}, u32[]{:S(2)}) collective-permute-start(f32[64,512]{1,0:T(8,128)S(1)} %get-tuple-element.25), channel_id=1, source_target_pairs={{0,256},{64,320},{128,384},{192,448},{256,0},{320,64},{384,128},{4... | collective-permute-start | bytes 393224 | tf_op jit(solution)/shard_map/ppermute | solution.py:171
  123.3 14.7 %copy-start.4 = (f32[1,64,512]{2,1,0:T(8,128)S(1)}, f32[1,64,512]{2,1,0:T(8,128)}, u32[]{:S(2)}) copy-start(f32[1,64,512]{2,1,0:T(8,128)} %param.11) | copy-start | bytes 393220
  123.3 14.7 %copy-start.5 = (f32[1,64,512]{2,1,0:T(8,128)S(1)}, f32[1,64,512]{2,1,0:T(8,128)}, u32[]{:S(2)}) copy-start(f32[1,64,512]{2,1,0:T(8,128)} %param.12) | copy-start | bytes 393220
  123.3 14.7 %copy-start.6 = (f32[64,512]{1,0:T(8,128)S(1)}, f32[64,512]{1,0:T(8,128)}, u32[]{:S(2)}) copy-start(f32[64,512]{1,0:T(8,128)} %param.14) | copy-start | bytes 393220

commit v4 on v3

--- a/solution.py
+++ b/solution.py
@@ -54,12 +54,12 @@
     return pl.multiple_of((high * 4 + lax.rem(turn + k, 4)) * 128, 128)
 
 
-def pack_kernel(place, w0, w1, w2, w3, packed):
+def pack_kernel(place, w0, w2, w1, w3, packed):
     for k, weight in enumerate((w0, w1, w2, w3)):
         packed[k] = weight[...]
 
 
-def preact_kernel(place, x, from_y, from_core, from_both, packed, anchor, master, partial, tokens, drift):
+def preact_kernel(place, x, from_y, from_core, from_both, packed, cotangent, anchor, master, partial, tokens, upstream, drift):
     drift[...] = anchor[...] - master[...]
     turn = place[0]
     half = pl.multiple_of(place[1] * 2048, 2048)
@@ -73,27 +73,24 @@
             tokens[k, 256:384, to] = from_core[:, pl.ds(start, 128)]
             tokens[k, 384:512, to] = from_both[:, pl.ds(start, 128)]
         total += jnp.dot(tokens[k], packed[k], preferred_element_type=F32)
+    keys = pl.multiple_of(place[2] * 256, 256)
+    far_keys = pl.multiple_of(2048 + place[2] * 256, 256)
+    upstream[0:128, :] = cotangent[:, pl.ds(keys, 256)]
+    upstream[128:256, :] = from_y[:, pl.ds(far_keys, 256)]
+    upstream[256:384, :] = from_core[:, 2048:2304]
+    upstream[384:512, :] = from_both[:, pl.ds(far_keys, 256)]
     for j in range(4):
         partial[:, j * 256 : j * 256 + 256] = total[j * 128 : j * 128 + 128, :]
 
 
-def delta_kernel(
-    inv_root, place, partial, other, cotangent, from_y, from_core, from_both, tokens, delta, g0, g1, g2, g3
-):
-    keys = pl.multiple_of(place[2] * 256, 256)
-    upstream = (
-        cotangent[:, pl.ds(keys, 256)],
-        from_y[:, pl.ds(pl.multiple_of(2048 + keys, 256), 256)],
-        from_core[:, 2048:2304],
-        from_both[:, pl.ds(pl.multiple_of(2048 + keys, 256), 256)],
-    )
+def delta_kernel(inv_root, place, partial, other, upstream, tokens, delta, g0, g1, g2, g3):
     for j in range(4):
         i = j ^ 1
         preact = partial[:, j * 256 : j * 256 + 256] + other[:, i * 256 : i * 256 + 256]
         preact = preact * inv_root
         gating = jax.nn.sigmoid(preact)
         derivative = gating * (1.0 + preact * (1.0 - gating))
-        rows = upstream[j].astype(F32) * derivative * inv_root
+        rows = upstream[j * 128 : j * 128 + 128, :].astype(F32) * derivative * inv_root
         delta[j * 128 : j * 128 + 128, :] = rows.astype(BF16)
     for k, grad in ((2, g2), (1, g1), (3, g3), (0, g0)):
         full = lax.dot_general(
@@ -117,18 +114,12 @@
             away[:, to] = total[128:256, high * 128 : high * 128 + 128]
 
 
-def join_kernel(place, stay, far, out, sems):
-    copies = []
-    for source, y in ((stay, place[1]), (far, 1 - place[1])):
-        to = out.at[:, pl.ds(pl.multiple_of(y * 2048, 2048), 2048)]
-        copies.append(pltpu.make_async_copy(source, to, sems.at[len(copies)]))
-    for copy in copies:
-        copy.start()
-    for copy in copies:
-        copy.wait()
-
-
-def total_kernel(place, g0, after, before, far, drift, total, kept):
+def join_kernel(place, stay, far, out):
+    out[:, pl.ds(pl.multiple_of(place[1] * 2048, 2048), 2048)] = stay[...]
+    out[:, pl.ds(pl.multiple_of((1 - place[1]) * 2048, 2048), 2048)] = far[...]
+
+
+def total_kernel(place, g0, far, after, before, drift, total, kept):
     kept[...] = drift[...]
     summed = g0[...] + after[...].astype(F32) + before[...].astype(F32) + far[...].astype(F32)
     total[...] = summed.astype(BF16)
@@ -181,18 +172,19 @@
     square = (from_y, from_core, lax.ppermute(from_y, "c", SWAP))
 
     (packed,) = call(
-        pack_kernel, [shape((4, 512, 256), BF16)], BESIDE, 2 << 20, (place, *weight)
-    )
-    partial, tokens, drift = call(
+        pack_kernel, [shape((4, 512, 256), BF16)], 10 * BESIDE, 2 << 20, (place, weight[0], weight[2], weight[1], weight[3])
+    )
+    partial, tokens, both, drift = call(
         preact_kernel,
         [
             shape((rows, 1024), F32),
             shape((4, 512, 512), BF16),
+            shape((512, 256), BF16),
             shape((64, 512), F32),
         ],
         2 * 512 * 2048 * 256,
         6 << 20,
-        (place, tokens_in, *square, packed, anchor, master),
+        (place, tokens_in, *square, packed, cotangent, anchor, master),
     )
     other = lax.ppermute(partial, "y", SWAP)
     drift = fold(drift, 1)
@@ -203,25 +195,26 @@
         + [shape((512, 256), BF16)] * 3,
         2 * 512 * 2048 * 256,
         5 << 20,
-        (place, partial, other, cotangent, *square, tokens),
+        (place, partial, other, both, tokens),
         (drift,),
     )
     far = lax.ppermute(g2, ZC, ring_by_core(2))
     after = lax.ppermute(g1, Z, ring(1))
     before = lax.ppermute(g3, Z, ring(-1))
 
+    near_delta = lax.ppermute(delta[256:], "c", SWAP)
     total, drift = call(
         total_kernel,
         [shape((512, 256), BF16), shape((64, 512), F32)],
         0,
         2 << 20,
-        (place, g0, after, before, far, fold(drift, 3)),
+        (place, g0, far, after, before, fold(drift, 4)),
+        (near_delta,),
     )
     parts = lax.all_to_all(total.reshape(8, 64, 256), ("zh", "c"), split_axis=0, concat_axis=0)
     (weight_grad,) = call(sum_kernel, [shape((64, 512), F32)], BESIDE, 1 << 19, (place, parts))
-    summed = fold(drift, 4)
-
-    near_delta = lax.ppermute(delta[256:], "c", SWAP)
+    summed = fold(drift, 3)
+
     stay, away = call(
         back_kernel,
         [shape((rows, 2048), BF16)] * 2,
@@ -231,8 +224,8 @@
         (total,),
     )
     back_far = lax.ppermute(away, "y", SWAP)
-    input_grad = jnp.concatenate(
-        [jnp.where(mine == 0, stay, back_far), jnp.where(mine == 0, back_far, stay)], axis=1
+    (input_grad,) = call(
+        join_kernel, [shape((rows, features), BF16)], 0, 2 << 20, (place, stay, back_far)
     )
 
     new_first = 0.9 * first_moment[0] + 0.1 * weight_grad

time: 140 us -> 126 us (0.900)
  the two profiles are of different devices: /device:TPU:38 before, /device:TPU:1 now
where the time goes in v4:
time: 126 us; the launch traced here: 125 us
  starting transfers between devices  85.2 us (68%)
  waiting for transfers between devices  25.2 us (20%)
  Pallas kernels  9.08 us (7%)
  other arithmetic  2.91 us (2%)
  between operations  1.71 us (1%)
  local copies, waits for them, and re-layouts  1.32 us (1%)
    all_to_all x1, starting transfers between devices, body(): lax.all_to_all(own, ('zh', 'c'), split_axis=0, concat_axis=0)  16.7 us
    ppermute x3, starting transfers between devices, fold(): return value + lax.ppermute(value, 'replica', pairs)  9.82 us
    all_to_all x1, waiting for transfers between devices, body(): lax.all_to_all(own, ('zh', 'c'), split_axis=0, concat_axis=0)  9.47 us
    pallas_call x7, Pallas kernels, call(): pl.pallas_call(run, out_shape=out_shape, in_specs=[smem] + [vmem] * (used...  9.08 us
    ppermute x1, starting transfers between devices, body(): lax.ppermute(same, ZC, ring_by_core(2))  8.72 us
    ppermute x1, waiting for transfers between devices, body(): back_far = lax.ppermute(away, 'y', SWAP)  7.72 us
    all_to_all x1, starting transfers between devices, body(): lax.all_to_all(total.reshape(8, 64, 256), ('zh', 'c'), split_axis=0, conc...  7.12 us
    ppermute x1, starting transfers between devices, body(): from_core = lax.ppermute(columns(mine, near_keys), 'c', SWAP)  5.48 us
  transfers between devices with their start and end apart: 18, of which 6 were waited for; matrix products, arithmetic and copies ran while one was open for 1% of the time, Pallas kernels for 5%

profile of v4, /device:TPU:1, one launch (start us, length us, event | category | flops | bytes accessed | tf_op | source)
XLA Modules:
  0.0 125.4 jit_solution(8325150000907204440)
XLA Ops:
  0.6 0.0 copy-start
  0.6 1.0 convert_element_type.11
  1.7 0.7 broadcast_in_dim.18
  2.4 16.7 %all-to-all-start = ((bf16[8,64,256]{2,1,0:T(8,128)(2,1)}), bf16[8,64,256]{2,1,0:T(8,128)(2,1)S(1)}, u32[]{:S(2)}, u32[]{:S(2)}) async-start(bf16[8,64,256]{2,1,0:T(8,128)(2,1)} %bitcast.8), calls=%async_computation | async-start | bytes 524288 | tf_op jit(solution)/shard_map/all_to_all | solution.py:148
  19.1 0.1 dynamic-slice_bitcast_fusion
  19.3 4.8 %collective-permute-start = (bf16[128,2560]{1,0:T(8,128)(2,1)S(1)}, bf16[128,2560]{1,0:T(8,128)(2,1)}, u32[]{:S(2)}, u32[]{:S(2)}) collective-permute-start(bf16[128,2560]{1,0:T(8,128)(2,1)S(1)} %pad_maximum_fusion), channel_id=1, source_target_pairs={{0,32},{32,0},{1,33},{33,1},{2,34},{34,2},{3,35},{35,3},{4,36},{36... | collective-permute-start | bytes 1966088 | tf_op jit(solution)/shard_map/ppermute | solution.py:169
  24.2 9.5 %all-to-all-done = bf16[8,64,256]{2,1,0:T(8,128)(2,1)S(1)} async-done(((bf16[8,64,256]{2,1,0:T(8,128)(2,1)}), bf16[8,64,256]{2,1,0:T(8,128)(2,1)S(1)}, u32[]{:S(2)}, u32[]{:S(2)}) %all-to-all-start) | async-done | bytes 262176 | tf_op jit(solution)/shard_map/all_to_all | solution.py:148
  33.6 8.7 %collective-permute-start.3 = (bf16[512,256]{1,0:T(8,128)(2,1)S(1)}, bf16[512,256]{1,0:T(8,128)(2,1)S(1)}, u32[]{:S(2)}, u32[]{:S(2)}) collective-permute-start(bf16[512,256]{1,0:T(8,128)(2,1)S(1)} %bitcast.41), channel_id=1, source_target_pairs={{0,4},{2,6},{4,8},{6,10},{8,12},{10,14},{12,16},{14,18},{16,20},{1... | collective-permute-start | bytes 786440 | tf_op jit(solution)/shard_map/ppermute | solution.py:152
  42.4 1.9 %collective-permute-start.4 = (bf16[512,256]{1,0:T(8,128)(2,1)S(1)}, bf16[512,256]{1,0:T(8,128)(2,1)S(1)}, u32[]{:S(2)}, u32[]{:S(2)}) collective-permute-start(bf16[512,256]{1,0:T(8,128)(2,1)S(1)} %bitcast.42), channel_id=1, source_target_pairs={{0,30},{2,0},{4,2},{6,4},{8,6},{10,8},{12,10},{14,12},{16,14},{18,... | collective-permute-start | bytes 786440 | tf_op jit(solution)/shard_map/ppermute | solution.py:151
  44.3 3.4 %collective-permute-start.5 = (bf16[512,256]{1,0:T(8,128)(2,1)S(1)}, bf16[512,256]{1,0:T(8,128)(2,1)S(1)}, u32[]{:S(2)}, u32[]{:S(2)}) collective-permute-start(bf16[512,256]{1,0:T(8,128)(2,1)S(1)} %bitcast.43), channel_id=1, source_target_pairs={{0,2},{2,4},{4,6},{6,8},{8,10},{10,12},{12,14},{14,16},{16,18},{18... | collective-permute-start | bytes 786440 | tf_op jit(solution)/shard_map/ppermute | solution.py:153
  47.7 0.9 pad_maximum_fusion.1
  48.5 5.5 %collective-permute-start.1 = (bf16[128,2304]{1,0:T(8,128)(2,1)}, bf16[128,2304]{1,0:T(8,128)(2,1)}, u32[]{:S(2)}, u32[]{:S(2)}) collective-permute-start(bf16[128,2304]{1,0:T(8,128)(2,1)} %pad_maximum_fusion.1), channel_id=1, source_target_pairs={{0,1},{1,0},{2,3},{3,2},{4,5},{5,4},{6,7},{7,6},{8,9},{9,8},{10,11... | collective-permute-start | bytes 1769480 | tf_op jit(solution)/shard_map/ppermute | solution.py:171
  54.0 0.1 pad_add_fusion.refs_0_
  54.1 1.9 %collective-permute-start.2 = (bf16[128,2560]{1,0:T(8,128)(2,1)}, bf16[128,2560]{1,0:T(8,128)(2,1)}, u32[]{:S(2)}, u32[]{:S(2)}) collective-permute-start(bf16[128,2560]{1,0:T(8,128)(2,1)} %collective-permute-done.refs_2_), channel_id=1, source_target_pairs={{0,1},{1,0},{2,3},{3,2},{4,5},{5,4},{6,7},{7,6},{8,9},{9,8},{10,11... | collective-permute-start | bytes 1966088 | tf_op jit(solution)/shard_map/ppermute | solution.py:172
  56.0 0.0 collective-permute-done.3.refs_2_
  56.0 0.0 collective-permute-done.4.refs_3_
  56.1 0.0 copy-start.1
  56.1 0.0 copy-start.3
  56.1 0.0 copy-start.4
  56.1 0.6 shard_map.127.refs_5_.refs_3_
  56.7 1.7 %collective-permute-done.2.refs_4_ = bf16[128,2560]{1,0:T(8,128)(2,1)} collective-permute-done((bf16[128,2560]{1,0:T(8,128)(2,1)}, bf16[128,2560]{1,0:T(8,128)(2,1)}, u32[]{:S(2)}, u32[]{:S(2)}) %collective-permute-start.2) | collective-permute-done | bytes 655392 | tf_op jit(solution)/shard_map/ppermute | solution.py:172
  58.4 2.3 %shard_map.128 = (f32[128,1024]{1,0:T(8,128)S(1)}, bf16[4,512,512]{2,1,0:T(8,128)(2,1)S(1)}, bf16[512,256]{1,0:T(8,128)(2,1)S(1)}, f32[64,512]{1,0:T(8,128)S(1)}) custom-call(s32[3]{0:T(128)S(1)} %pad_add_fusion.refs_0_, bf16[128,4096]{1,0:T(8,128)(2,1)S(1)} %bitcast.36, bf16[128,2560]{1,0:T(8,128)(2,1)} %collective-permute-done.refs_2_, ...), custom_call_target="tpu_custom_call" | custom-call | flops 536870912 | bytes 6291456 | tf_op jit(solution)/shard_map/pallas_call | solution.py:39
  60.8 4.8 %collective-permute-start.6 = (f32[128,1024]{1,0:T(8,128)S(1)}, f32[128,1024]{1,0:T(8,128)S(1)}, u32[]{:S(2)}, u32[]{:S(2)}) collective-permute-start(f32[128,1024]{1,0:T(8,128)S(1)} %get-tuple-element.19.refs_1_), channel_id=1, source_target_pairs={{0,32},{32,0},{1,33},{33,1},{2,34},{34,2},{3,35},{35,3},{4,36},{36... | collective-permute-start | bytes 1572872 | tf_op jit(solution)/shard_map/ppermute | solution.py:189
  65.6 2.7 %collective-permute-start.14 = (bf16[4,512,256]{2,1,0:T(8,128)(2,1)S(1)}, bf16[4,512,256]{2,1,0:T(8,128)(2,1)S(1)}, u32[]{:S(2)}, u32[]{:S(2)}) collective-permute-start(bf16[4,512,256]{2,1,0:T(8,128)(2,1)S(1)} %shard_map.127.refs_5_.refs_3_), channel_id=1, source_target_pairs={{0,1},{1,0},{2,3},{3,2},{4,5},{5,4},{6,7},{7,6},{8,9},{9,8},{10,11... | collective-permute-start | bytes 3145736 | tf_op jit(solution)/shard_map/ppermute | solution.py:191
  68.3 3.1 %collective-permute-start.7 = (f32[64,512]{1,0:T(8,128)S(1)}, f32[64,512]{1,0:T(8,128)S(1)}, u32[]{:S(2)}, u32[]{:S(2)}) collective-permute-start(f32[64,512]{1,0:T(8,128)S(1)} %get-tuple-element.22), channel_id=1, source_target_pairs={{0,64},{64,0},{128,192},{192,128},{256,320},{320,256},{384,448},{4... | collective-permute-start | bytes 393224 | tf_op jit(solution)/shard_map/ppermute | solution.py:162
  71.4 3.9 %collective-permute-done.7 = f32[64,512]{1,0:T(8,128)S(1)} collective-permute-done((f32[64,512]{1,0:T(8,128)S(1)}, f32[64,512]{1,0:T(8,128)S(1)}, u32[]{:S(2)}, u32[]{:S(2)}) %collective-permute-start.7) | collective-permute-done | bytes 131104 | tf_op jit(solution)/shard_map/ppermute | solution.py:162
  75.3 2.3 %collective-permute-start.11 = (f32[64,512]{1,0:T(8,128)S(1)}, f32[64,512]{1,0:T(8,128)S(1)}, u32[]{:S(2)}, u32[]{:S(2)}) collective-permute-start(f32[64,512]{1,0:T(8,128)S(1)} %add.42.refs_5_), channel_id=1, source_target_pairs={{0,256},{64,320},{128,384},{192,448},{256,0},{320,64},{384,128},{4... | collective-permute-start | bytes 393224 | tf_op jit(solution)/shard_map/ppermute | solution.py:162
  77.6 1.4 %shard_map.129 = (bf16[512,256]{1,0:T(8,128)(2,1)S(1)}, f32[512,256]{1,0:T(8,128)S(1)}, bf16[512,256]{1,0:T(8,128)(2,1)S(1)}, bf16[512,256]{1,0:T(8,128)(2,1)S(1)}, bf16[512,256]{1,0:T(8,128)(2,1)S(1)}) custom-call(s32[3]{0:T(128)S(1)} %pad_add_fusion.refs_0_, f32[128,1024]{1,0:T(8,128)S(1)} %get-tuple-element.19.refs_1_, ...), custom_call_target="tpu_custom_call" | custom-call | flops 536870912 | bytes 5242880 | tf_op jit(solution)/shard_map/pallas_call | solution.py:39
  79.0 2.9 %collective-permute-start.8 = (bf16[512,256]{1,0:T(8,128)(2,1)S(1)}, bf16[512,256]{1,0:T(8,128)(2,1)S(1)}, u32[]{:S(2)}, u32[]{:S(2)}) collective-permute-start(bf16[512,256]{1,0:T(8,128)(2,1)S(1)} %get-tuple-element.24), channel_id=1, source_target_pairs={{0,4},{2,6},{4,8},{6,10},{8,12},{10,14},{12,16},{14,18},{16,20},{1... | collective-permute-start | bytes 786440 | tf_op jit(solution)/shard_map/ppermute | solution.py:201
  81.9 3.5 %collective-permute-start.9 = (bf16[512,256]{1,0:T(8,128)(2,1)S(1)}, bf16[512,256]{1,0:T(8,128)(2,1)S(1)}, u32[]{:S(2)}, u32[]{:S(2)}) collective-permute-start(bf16[512,256]{1,0:T(8,128)(2,1)S(1)} %get-tuple-element.25), channel_id=1, source_target_pairs={{0,2},{2,4},{4,6},{6,8},{8,10},{10,12},{12,14},{14,16},{16,18},{18... | collective-permute-start | bytes 786440 | tf_op jit(solution)/shard_map/ppermute | solution.py:202
  85.4 3.0 %collective-permute-start.10 = (bf16[512,256]{1,0:T(8,128)(2,1)S(1)}, bf16[512,256]{1,0:T(8,128)(2,1)S(1)}, u32[]{:S(2)}, u32[]{:S(2)}) collective-permute-start(bf16[512,256]{1,0:T(8,128)(2,1)S(1)} %get-tuple-element.26), channel_id=1, source_target_pairs={{0,30},{2,0},{4,2},{6,4},{8,6},{10,8},{12,10},{14,12},{16,14},{18,... | collective-permute-start | bytes 786440 | tf_op jit(solution)/shard_map/ppermute | solution.py:203
  88.4 0.0 collective-permute-done.11
  88.5 4.5 %collective-permute-start.12 = (bf16[256,256]{1,0:T(8,128)(2,1)S(1)}, bf16[256,256]{1,0:T(8,128)(2,1)S(1)}, u32[]{:S(2)}, u32[]{:S(2)}) collective-permute-start(bf16[256,256]{1,0:T(8,128)(2,1)S(1)} %slice.11), channel_id=1, source_target_pairs={{0,1},{1,0},{2,3},{3,2},{4,5},{5,4},{6,7},{7,6},{8,9},{9,8},{10,11... | collective-permute-start | bytes 393224 | tf_op jit(solution)/shard_map/ppermute | solution.py:205
  93.0 0.9 collective-permute-done.12.refs_6_.refs_2_
  93.9 1.4 %collective-permute-done.9.refs_3_ = bf16[512,256]{1,0:T(8,128)(2,1)S(1)} collective-permute-done((bf16[512,256]{1,0:T(8,128)(2,1)S(1)}, bf16[512,256]{1,0:T(8,128)(2,1)S(1)}, u32[]{:S(2)}, u32[]{:S(2)}) %collective-permute-start.9) | collective-permute-done | bytes 262176 | tf_op jit(solution)/shard_map/ppermute | solution.py:202
  95.3 0.0 collective-permute-done.10.refs_4_
  95.3 1.3 %shard_map.130 = (bf16[512,256]{1,0:T(8,128)(2,1)}, f32[64,512]{1,0:T(8,128)S(1)}) custom-call(s32[3]{0:T(128)S(1)} %pad_add_fusion.refs_0_, f32[512,256]{1,0:T(8,128)S(1)} %get-tuple-element.23.refs_1_, bf16[512,256]{1,0:T(8,128)(2,1)S(1)} %collective-permute-done.8.refs_2_, bf16[512,256]{1,0:T(8,128)(2,1)S(1)} %collective-permute-done.9.refs_3_, ...), custom_call_target="tpu_custom_call" | custom-call | bytes 2097152 | tf_op jit(solution)/shard_map/pallas_call | solution.py:39
  96.7 7.1 %all-to-all-start.1 = ((bf16[8,64,256]{2,1,0:T(8,128)(2,1)}), bf16[8,64,256]{2,1,0:T(8,128)(2,1)S(1)}, u32[]{:S(2)}, u32[]{:S(2)}) async-start(bf16[8,64,256]{2,1,0:T(8,128)(2,1)} %bitcast.12), calls=%async_computation.1 | async-start | bytes 524288 | tf_op jit(solution)/shard_map/all_to_all | solution.py:214
  103.8 1.3 %shard_map.132 = (bf16[128,2048]{1,0:T(8,128)(2,1)S(1)}, bf16[128,2048]{1,0:T(8,128)(2,1)S(1)}) custom-call(s32[3]{0:T(128)S(1)} %pad_add_fusion.refs_0_, bf16[512,256]{1,0:T(8,128)(2,1)S(1)} %get-tuple-element.27.refs_1_, bf16[256,256]{1,0:T(8,128)(2,1)S(1)} %collective-permute-done.12.refs_6_.refs_2_, bf16[4,512,256]{2,1,0:T(8,128)(2,1)S(1)} %shard_map.127.refs_5_.refs_3_, ...), custom_call_target="tpu_custom_call" | custom-call | flops 536870912 | bytes 4194304 | tf_op jit(solution)/shard_map/pallas_call | solution.py:39
  105.1 3.9 %collective-permute-start.15 = (bf16[128,2048]{1,0:T(8,128)(2,1)S(1)}, bf16[128,2048]{1,0:T(8,128)(2,1)S(1)}, u32[]{:S(2)}, u32[]{:S(2)}) collective-permute-start(bf16[128,2048]{1,0:T(8,128)(2,1)S(1)} %get-tuple-element.31), channel_id=1, source_target_pairs={{0,32},{32,0},{1,33},{33,1},{2,34},{34,2},{3,35},{35,3},{4,36},{36... | collective-permute-start | bytes 1572872 | tf_op jit(solution)/shard_map/ppermute | solution.py:226
  109.7 4.4 %collective-permute-start.13 = (f32[64,512]{1,0:T(8,128)S(1)}, f32[64,512]{1,0:T(8,128)S(1)}, u32[]{:S(2)}, u32[]{:S(2)}) collective-permute-start(f32[64,512]{1,0:T(8,128)S(1)} %get-tuple-element.28), channel_id=1, source_target_pairs={{0,192},{64,128},{128,64},{192,0},{256,448},{320,384},{384,320},{4... | collective-permute-start | bytes 393224 | tf_op jit(solution)/shard_map/ppermute | solution.py:162
  114.1 7.7 %collective-permute-done.15.refs_2_ = bf16[128,2048]{1,0:T(8,128)(2,1)S(1)} collective-permute-done((bf16[128,2048]{1,0:T(8,128)(2,1)S(1)}, bf16[128,2048]{1,0:T(8,128)(2,1)S(1)}, u32[]{:S(2)}, u32[]{:S(2)}) %collective-permute-start.15) | collective-permute-done | bytes 524320 | tf_op jit(solution)/shard_map/ppermute | solution.py:226
  121.9 1.6 %shard_map.133 = bf16[128,4096]{1,0:T(8,128)(2,1)} custom-call(s32[3]{0:T(128)S(1)} %pad_add_fusion.refs_0_, bf16[128,2048]{1,0:T(8,128)(2,1)S(1)} %get-tuple-element.30.refs_1_, bf16[128,2048]{1,0:T(8,128)(2,1)S(1)} %collective-permute-done.15.refs_2_), custom_call_target="tpu_custom_call" | custom-call | bytes 2097152 | tf_op jit(solution)/shard_map/pallas_call | solution.py:39
  123.4 0.6 shard_map.131
  124.0 0.3 copy-done.5
  124.3 0.1 copy-done.6
  124.4 0.1 copy-done.7
  124.5 0.9 multiply_bitcast_fusion
  (24 shorter events, 0.2 us)
Async XLA Ops:
  0.6 18.5 %copy-start = (bf16[1,128,4096]{2,1,0:T(8,128)(2,1)S(1)}, bf16[1,128,4096]{2,1,0:T(8,128)(2,1)}, u32[]{:S(2)}) copy-start(bf16[1,128,4096]{2,1,0:T(8,128)(2,1)} %param.8) | copy-start | bytes 3145732
  2.4 16.8 %copy-start.2 = (bf16[1,128,512]{2,1,0:T(8,128)(2,1)S(1)}, bf16[1,128,512]{2,1,0:T(8,128)(2,1)}, u32[]{:S(2)}) copy-start(bf16[1,128,512]{2,1,0:T(8,128)(2,1)} %param.9) | copy-start | bytes 393220
  2.4 31.2 %all-to-all-start = ((bf16[8,64,256]{2,1,0:T(8,128)(2,1)}), bf16[8,64,256]{2,1,0:T(8,128)(2,1)S(1)}, u32[]{:S(2)}, u32[]{:S(2)}) async-start(bf16[8,64,256]{2,1,0:T(8,128)(2,1)} %bitcast.8), calls=%async_computation | async-start | bytes 524288 | tf_op jit(solution)/shard_map/all_to_all | solution.py:148
  19.3 34.8 %collective-permute-start = (bf16[128,2560]{1,0:T(8,128)(2,1)S(1)}, bf16[128,2560]{1,0:T(8,128)(2,1)}, u32[]{:S(2)}, u32[]{:S(2)}) collective-permute-start(bf16[128,2560]{1,0:T(8,128)(2,1)S(1)} %pad_maximum_fusion), channel_id=1, source_target_pairs={{0,32},{32,0},{1,33},{33,1},{2,34},{34,2},{3,35},{35,3},{4,36},{36... | collective-permute-start | bytes 1966088 | tf_op jit(solution)/shard_map/ppermute | solution.py:169
  33.6 22.4 %collective-permute-start.3 = (bf16[512,256]{1,0:T(8,128)(2,1)S(1)}, bf16[512,256]{1,0:T(8,128)(2,1)S(1)}, u32[]{:S(2)}, u32[]{:S(2)}) collective-permute-start(bf16[512,256]{1,0:T(8,128)(2,1)S(1)} %bitcast.41), channel_id=1, source_target_pairs={{0,4},{2,6},{4,8},{6,10},{8,12},{10,14},{12,16},{14,18},{16,20},{1... | collective-permute-start | bytes 786440 | tf_op jit(solution)/shard_map/ppermute | solution.py:152
  42.4 13.7 %collective-permute-start.4 = (bf16[512,256]{1,0:T(8,128)(2,1)S(1)}, bf16[512,256]{1,0:T(8,128)(2,1)S(1)}, u32[]{:S(2)}, u32[]{:S(2)}) collective-permute-start(bf16[512,256]{1,0:T(8,128)(2,1)S(1)} %bitcast.42), channel_id=1, source_target_pairs={{0,30},{2,0},{4,2},{6,4},{8,6},{10,8},{12,10},{14,12},{16,14},{18,... | collective-permute-start | bytes 786440 | tf_op jit(solution)/shard_map/ppermute | solution.py:151
  44.3 11.7 %collective-permute-start.5 = (bf16[512,256]{1,0:T(8,128)(2,1)S(1)}, bf16[512,256]{1,0:T(8,128)(2,1)S(1)}, u32[]{:S(2)}, u32[]{:S(2)}) collective-permute-start(bf16[512,256]{1,0:T(8,128)(2,1)S(1)} %bitcast.43), channel_id=1, source_target_pairs={{0,2},{2,4},{4,6},{6,8},{8,10},{10,12},{12,14},{14,16},{16,18},{18... | collective-permute-start | bytes 786440 | tf_op jit(solution)/shard_map/ppermute | solution.py:153
  48.5 8.2 %collective-permute-start.1 = (bf16[128,2304]{1,0:T(8,128)(2,1)}, bf16[128,2304]{1,0:T(8,128)(2,1)}, u32[]{:S(2)}, u32[]{:S(2)}) collective-permute-start(bf16[128,2304]{1,0:T(8,128)(2,1)} %pad_maximum_fusion.1), channel_id=1, source_target_pairs={{0,1},{1,0},{2,3},{3,2},{4,5},{5,4},{6,7},{7,6},{8,9},{9,8},{10,11... | collective-permute-start | bytes 1769480 | tf_op jit(solution)/shard_map/ppermute | solution.py:171
  54.1 4.3 %collective-permute-start.2 = (bf16[128,2560]{1,0:T(8,128)(2,1)}, bf16[128,2560]{1,0:T(8,128)(2,1)}, u32[]{:S(2)}, u32[]{:S(2)}) collective-permute-start(bf16[128,2560]{1,0:T(8,128)(2,1)} %collective-permute-done.refs_2_), channel_id=1, source_target_pairs={{0,1},{1,0},{2,3},{3,2},{4,5},{5,4},{6,7},{7,6},{8,9},{9,8},{10,11... | collective-permute-start | bytes 1966088 | tf_op jit(solution)/shard_map/ppermute | solution.py:172
  56.1 2.4 %copy-start.1 = (bf16[1,128,4096]{2,1,0:T(8,128)(2,1)S(1)}, bf16[1,128,4096]{2,1,0:T(8,128)(2,1)}, u32[]{:S(2)}) copy-start(bf16[1,128,4096]{2,1,0:T(8,128)(2,1)} %param.8) | copy-start | bytes 3145732
  56.1 2.4 %copy-start.3 = (f32[1,64,512]{2,1,0:T(8,128)S(1)}, f32[1,64,512]{2,1,0:T(8,128)}, u32[]{:S(2)}) copy-start(f32[1,64,512]{2,1,0:T(8,128)} %param.10) | copy-start | bytes 393220
  56.1 2.4 %copy-start.4 = (f32[64,512]{1,0:T(8,128)S(1)}, f32[64,512]{1,0:T(8,128)}, u32[]{:S(2)}) copy-start(f32[64,512]{1,0:T(8,128)} %refs_7_.1) | copy-start | bytes 393220
  60.8 16.9 %collective-permute-start.6 = (f32[128,1024]{1,0:T(8,128)S(1)}, f32[128,1024]{1,0:T(8,128)S(1)}, u32[]{:S(2)}, u32[]{:S(2)}) collective-permute-start(f32[128,1024]{1,0:T(8,128)S(1)} %get-tuple-element.19.refs_1_), channel_id=1, source_target_pairs={{0,32},{32,0},{1,33},{33,1},{2,34},{34,2},{3,35},{35,3},{4,36},{36... | collective-permute-start | bytes 1572872 | tf_op jit(solution)/shard_map/ppermute | solution.py:189
  65.6 38.2 %collective-permute-start.14 = (bf16[4,512,256]{2,1,0:T(8,128)(2,1)S(1)}, bf16[4,512,256]{2,1,0:T(8,128)(2,1)S(1)}, u32[]{:S(2)}, u32[]{:S(2)}) collective-permute-start(bf16[4,512,256]{2,1,0:T(8,128)(2,1)S(1)} %shard_map.127.refs_5_.refs_3_), channel_id=1, source_target_pairs={{0,1},{1,0},{2,3},{3,2},{4,5},{5,4},{6,7},{7,6},{8,9},{9,8},{10,11... | collective-permute-start | bytes 3145736 | tf_op jit(solution)/shard_map/ppermute | solution.py:191
  68.3 7.0 %collective-permute-start.7 = (f32[64,512]{1,0:T(8,128)S(1)}, f32[64,512]{1,0:T(8,128)S(1)}, u32[]{:S(2)}, u32[]{:S(2)}) collective-permute-start(f32[64,512]{1,0:T(8,128)S(1)} %get-tuple-element.22), channel_id=1, source_target_pairs={{0,64},{64,0},{128,192},{192,128},{256,320},{320,256},{384,448},{4... | collective-permute-start | bytes 393224 | tf_op jit(solution)/shard_map/ppermute | solution.py:162
  75.3 13.1 %collective-permute-start.11 = (f32[64,512]{1,0:T(8,128)S(1)}, f32[64,512]{1,0:T(8,128)S(1)}, u32[]{:S(2)}, u32[]{:S(2)}) collective-permute-start(f32[64,512]{1,0:T(8,128)S(1)} %add.42.refs_5_), channel_id=1, source_target_pairs={{0,256},{64,320},{128,384},{192,448},{256,0},{320,64},{384,128},{4... | collective-permute-start | bytes 393224 | tf_op jit(solution)/shard_map/ppermute | solution.py:162
  79.0 14.9 %collective-permute-start.8 = (bf16[512,256]{1,0:T(8,128)(2,1)S(1)}, bf16[512,256]{1,0:T(8,128)(2,1)S(1)}, u32[]{:S(2)}, u32[]{:S(2)}) collective-permute-start(bf16[512,256]{1,0:T(8,128)(2,1)S(1)} %get-tuple-element.24), channel_id=1, source_target_pairs={{0,4},{2,6},{4,8},{6,10},{8,12},{10,14},{12,16},{14,18},{16,20},{1... | collective-permute-start | bytes 786440 | tf_op jit(solution)/shard_map/ppermute | solution.py:201
  81.9 13.4 %collective-permute-start.9 = (bf16[512,256]{1,0:T(8,128)(2,1)S(1)}, bf16[512,256]{1,0:T(8,128)(2,1)S(1)}, u32[]{:S(2)}, u32[]{:S(2)}) collective-permute-start(bf16[512,256]{1,0:T(8,128)(2,1)S(1)} %get-tuple-element.25), channel_id=1, source_target_pairs={{0,2},{2,4},{4,6},{6,8},{8,10},{10,12},{12,14},{14,16},{16,18},{18... | collective-permute-start | bytes 786440 | tf_op jit(solution)/shard_map/ppermute | solution.py:202
  85.4 9.9 %collective-permute-start.10 = (bf16[512,256]{1,0:T(8,128)(2,1)S(1)}, bf16[512,256]{1,0:T(8,128)(2,1)S(1)}, u32[]{:S(2)}, u32[]{:S(2)}) collective-permute-start(bf16[512,256]{1,0:T(8,128)(2,1)S(1)} %get-tuple-element.26), channel_id=1, source_target_pairs={{0,30},{2,0},{4,2},{6,4},{8,6},{10,8},{12,10},{14,12},{16,14},{18,... | collective-permute-start | bytes 786440 | tf_op jit(solution)/shard_map/ppermute | solution.py:203
  88.5 5.5 %collective-permute-start.12 = (bf16[256,256]{1,0:T(8,128)(2,1)S(1)}, bf16[256,256]{1,0:T(8,128)(2,1)S(1)}, u32[]{:S(2)}, u32[]{:S(2)}) collective-permute-start(bf16[256,256]{1,0:T(8,128)(2,1)S(1)} %slice.11), channel_id=1, source_target_pairs={{0,1},{1,0},{2,3},{3,2},{4,5},{5,4},{6,7},{7,6},{8,9},{9,8},{10,11... | collective-permute-start | bytes 393224 | tf_op jit(solution)/shard_map/ppermute | solution.py:205
  96.7 26.8 %all-to-all-start.1 = ((bf16[8,64,256]{2,1,0:T(8,128)(2,1)}), bf16[8,64,256]{2,1,0:T(8,128)(2,1)S(1)}, u32[]{:S(2)}, u32[]{:S(2)}) async-start(bf16[8,64,256]{2,1,0:T(8,128)(2,1)} %bitcast.12), calls=%async_computation.1 | async-start | bytes 524288 | tf_op jit(solution)/shard_map/all_to_all | solution.py:214
  105.1 16.8 %collective-permute-start.15 = (bf16[128,2048]{1,0:T(8,128)(2,1)S(1)}, bf16[128,2048]{1,0:T(8,128)(2,1)S(1)}, u32[]{:S(2)}, u32[]{:S(2)}) collective-permute-start(bf16[128,2048]{1,0:T(8,128)(2,1)S(1)} %get-tuple-element.31), channel_id=1, source_target_pairs={{0,32},{32,0},{1,33},{33,1},{2,34},{34,2},{3,35},{35,3},{4,36},{36... | collective-permute-start | bytes 1572872 | tf_op jit(solution)/shard_map/ppermute | solution.py:226
  109.7 14.3 %collective-permute-start.13 = (f32[64,512]{1,0:T(8,128)S(1)}, f32[64,512]{1,0:T(8,128)S(1)}, u32[]{:S(2)}, u32[]{:S(2)}) collective-permute-start(f32[64,512]{1,0:T(8,128)S(1)} %get-tuple-element.28), channel_id=1, source_target_pairs={{0,192},{64,128},{128,64},{192,0},{256,448},{320,384},{384,320},{4... | collective-permute-start | bytes 393224 | tf_op jit(solution)/shard_map/ppermute | solution.py:162
  123.4 0.9 copy-start.5
  123.4 1.0 copy-start.6
  123.4 1.0 copy-start.7

commit v5 on v4

--- a/solution.py
+++ b/solution.py
@@ -54,7 +54,7 @@
     return pl.multiple_of((high * 4 + lax.rem(turn + k, 4)) * 128, 128)
 
 
-def pack_kernel(place, w0, w2, w1, w3, packed):
+def pack_kernel(place, w0, w2, w3, w1, packed):
     for k, weight in enumerate((w0, w1, w2, w3)):
         packed[k] = weight[...]
 
@@ -119,7 +119,7 @@
     out[:, pl.ds(pl.multiple_of((1 - place[1]) * 2048, 2048), 2048)] = far[...]
 
 
-def total_kernel(place, g0, far, after, before, drift, total, kept):
+def total_kernel(place, g0, far, before, after, drift, total, kept):
     kept[...] = drift[...]
     summed = g0[...] + after[...].astype(F32) + before[...].astype(F32) + far[...].astype(F32)
     total[...] = summed.astype(BF16)
@@ -172,7 +172,7 @@
     square = (from_y, from_core, lax.ppermute(from_y, "c", SWAP))
 
     (packed,) = call(
-        pack_kernel, [shape((4, 512, 256), BF16)], 10 * BESIDE, 2 << 20, (place, weight[0], weight[2], weight[1], weight[3])
+        pack_kernel, [shape((4, 512, 256), BF16)], 10 * BESIDE, 2 << 20, (place, weight[0], weight[2], weight[3], weight[1])
     )
     partial, tokens, both, drift = call(
         preact_kernel,
@@ -208,7 +208,7 @@
         [shape((512, 256), BF16), shape((64, 512), F32)],
         0,
         2 << 20,
-        (place, g0, far, after, before, fold(drift, 4)),
+        (place, g0, far, before, after, fold(drift, 4)),
         (near_delta,),
     )
     parts = lax.all_to_all(total.reshape(8, 64, 256), ("zh", "c"), split_axis=0, concat_axis=0)

time: 126 us -> 126 us (level)
  starting transfers between devices: 85.2 us -> 82.9 us
  waiting for transfers between devices: 25.2 us -> 27.1 us
    ppermute x1, waiting for transfers between devices: 0.01 us -> 3.99 us  [body(): before = lax.ppermute(g3, Z, ring(-1))]
    ppermute x1, starting transfers between devices: 1.92 us -> 4.57 us  [body(): lax.ppermute(same, Z, ring(-1))]
    all_to_all x1, starting transfers between devices: 7.12 us -> 5.46 us  [body(): lax.all_to_all(total.reshape(8, 64, 256), ('zh', 'c'), split_axis=0, conc...]
    ppermute x1, starting transfers between devices: 3.36 us -> 1.92 us  [body(): lax.ppermute(same, Z, ring(1))]
    ppermute x1, waiting for transfers between devices: 1.4 us -> 0.01 us  [body(): after = lax.ppermute(g1, Z, ring(1))]
  transfers between devices with their start and end apart: 18 -> 18, of which waited for: 6 -> 7; matrix products, arithmetic and copies ran while one was open for 1% -> 1% of each run, Pallas kernels for 5% -> 5%
where the time goes in v5:
time: 126 us; the launch traced here: 125 us
  starting transfers between devices  82.9 us (66%)
  waiting for transfers between devices  27.1 us (22%)
  Pallas kernels  9.07 us (7%)
  other arithmetic  2.91 us (2%)
  between operations  1.7 us (1%)
  local copies, waits for them, and re-layouts  1.32 us (1%)
    all_to_all x1, starting transfers between devices, body(): lax.all_to_all(own, ('zh', 'c'), split_axis=0, concat_axis=0)  16.7 us
    ppermute x3, starting transfers between devices, fold(): return value + lax.ppermute(value, 'replica', pairs)  9.83 us
    all_to_all x1, waiting for transfers between devices, body(): lax.all_to_all(own, ('zh', 'c'), split_axis=0, concat_axis=0)  9.47 us
    pallas_call x7, Pallas kernels, call(): pl.pallas_call(run, out_shape=out_shape, in_specs=[smem] + [vmem] * (used...  9.07 us
    ppermute x1, starting transfers between devices, body(): lax.ppermute(same, ZC, ring_by_core(2))  8.72 us
    ppermute x1, waiting for transfers between devices, body(): back_far = lax.ppermute(away, 'y', SWAP)  6.8 us
    ppermute x1, starting transfers between devices, body(): from_core = lax.ppermute(columns(mine, near_keys), 'c', SWAP)  5.48 us
    all_to_all x1, starting transfers between devices, body(): lax.all_to_all(total.reshape(8, 64, 256), ('zh', 'c'), split_axis=0, conc...  5.46 us
  transfers between devices with their start and end apart: 18, of which 7 were waited for; matrix products, arithmetic and copies ran while one was open for 1% of the time, Pallas kernels for 5%

profile of v5, /device:TPU:1, one launch (start us, length us, event | category | flops | bytes accessed | tf_op | source)
XLA Modules:
  0.0 125.0 jit_solution(2519810873001124909)
XLA Ops:
  0.6 0.0 copy-start
  0.6 1.0 convert_element_type.11
  1.7 0.7 broadcast_in_dim.18
  2.4 16.7 %all-to-all-start = ((bf16[8,64,256]{2,1,0:T(8,128)(2,1)}), bf16[8,64,256]{2,1,0:T(8,128)(2,1)S(1)}, u32[]{:S(2)}, u32[]{:S(2)}) async-start(bf16[8,64,256]{2,1,0:T(8,128)(2,1)} %bitcast.8), calls=%async_computation | async-start | bytes 524288 | tf_op jit(solution)/shard_map/all_to_all | solution.py:148
  19.1 0.1 dynamic-slice_bitcast_fusion
  19.3 4.8 %collective-permute-start = (bf16[128,2560]{1,0:T(8,128)(2,1)S(1)}, bf16[128,2560]{1,0:T(8,128)(2,1)}, u32[]{:S(2)}, u32[]{:S(2)}) collective-permute-start(bf16[128,2560]{1,0:T(8,128)(2,1)S(1)} %pad_maximum_fusion), channel_id=1, source_target_pairs={{0,32},{32,0},{1,33},{33,1},{2,34},{34,2},{3,35},{35,3},{4,36},{36... | collective-permute-start | bytes 1966088 | tf_op jit(solution)/shard_map/ppermute | solution.py:169
  24.2 9.5 %all-to-all-done = bf16[8,64,256]{2,1,0:T(8,128)(2,1)S(1)} async-done(((bf16[8,64,256]{2,1,0:T(8,128)(2,1)}), bf16[8,64,256]{2,1,0:T(8,128)(2,1)S(1)}, u32[]{:S(2)}, u32[]{:S(2)}) %all-to-all-start) | async-done | bytes 262176 | tf_op jit(solution)/shard_map/all_to_all | solution.py:148
  33.6 8.7 %collective-permute-start.3 = (bf16[512,256]{1,0:T(8,128)(2,1)S(1)}, bf16[512,256]{1,0:T(8,128)(2,1)S(1)}, u32[]{:S(2)}, u32[]{:S(2)}) collective-permute-start(bf16[512,256]{1,0:T(8,128)(2,1)S(1)} %bitcast.41), channel_id=1, source_target_pairs={{0,4},{2,6},{4,8},{6,10},{8,12},{10,14},{12,16},{14,18},{16,20},{1... | collective-permute-start | bytes 786440 | tf_op jit(solution)/shard_map/ppermute | solution.py:152
  42.4 1.9 %collective-permute-start.4 = (bf16[512,256]{1,0:T(8,128)(2,1)S(1)}, bf16[512,256]{1,0:T(8,128)(2,1)S(1)}, u32[]{:S(2)}, u32[]{:S(2)}) collective-permute-start(bf16[512,256]{1,0:T(8,128)(2,1)S(1)} %bitcast.42), channel_id=1, source_target_pairs={{0,2},{2,4},{4,6},{6,8},{8,10},{10,12},{12,14},{14,16},{16,18},{18... | collective-permute-start | bytes 786440 | tf_op jit(solution)/shard_map/ppermute | solution.py:153
  44.3 4.6 %collective-permute-start.5 = (bf16[512,256]{1,0:T(8,128)(2,1)S(1)}, bf16[512,256]{1,0:T(8,128)(2,1)S(1)}, u32[]{:S(2)}, u32[]{:S(2)}) collective-permute-start(bf16[512,256]{1,0:T(8,128)(2,1)S(1)} %bitcast.43), channel_id=1, source_target_pairs={{0,30},{2,0},{4,2},{6,4},{8,6},{10,8},{12,10},{14,12},{16,14},{18,... | collective-permute-start | bytes 786440 | tf_op jit(solution)/shard_map/ppermute | solution.py:151
  48.9 0.9 pad_maximum_fusion.1
  49.7 5.5 %collective-permute-start.1 = (bf16[128,2304]{1,0:T(8,128)(2,1)}, bf16[128,2304]{1,0:T(8,128)(2,1)}, u32[]{:S(2)}, u32[]{:S(2)}) collective-permute-start(bf16[128,2304]{1,0:T(8,128)(2,1)} %pad_maximum_fusion.1), channel_id=1, source_target_pairs={{0,1},{1,0},{2,3},{3,2},{4,5},{5,4},{6,7},{7,6},{8,9},{9,8},{10,11... | collective-permute-start | bytes 1769480 | tf_op jit(solution)/shard_map/ppermute | solution.py:171
  55.2 0.1 pad_add_fusion.refs_0_
  55.3 1.9 %collective-permute-start.2 = (bf16[128,2560]{1,0:T(8,128)(2,1)}, bf16[128,2560]{1,0:T(8,128)(2,1)}, u32[]{:S(2)}, u32[]{:S(2)}) collective-permute-start(bf16[128,2560]{1,0:T(8,128)(2,1)} %collective-permute-done.refs_2_), channel_id=1, source_target_pairs={{0,1},{1,0},{2,3},{3,2},{4,5},{5,4},{6,7},{7,6},{8,9},{9,8},{10,11... | collective-permute-start | bytes 1966088 | tf_op jit(solution)/shard_map/ppermute | solution.py:172
  57.2 0.0 collective-permute-done.3.refs_2_
  57.2 0.0 collective-permute-done.4.refs_3_
  57.3 0.0 copy-start.1
  57.3 0.0 copy-start.3
  57.3 0.0 copy-start.4
  57.3 0.6 shard_map.127.refs_5_.refs_3_
  57.9 0.0 collective-permute-done.1.refs_3_
  57.9 1.7 %collective-permute-done.2.refs_4_ = bf16[128,2560]{1,0:T(8,128)(2,1)} collective-permute-done((bf16[128,2560]{1,0:T(8,128)(2,1)}, bf16[128,2560]{1,0:T(8,128)(2,1)}, u32[]{:S(2)}, u32[]{:S(2)}) %collective-permute-start.2) | collective-permute-done | bytes 655392 | tf_op jit(solution)/shard_map/ppermute | solution.py:172
  59.6 2.3 %shard_map.128 = (f32[128,1024]{1,0:T(8,128)S(1)}, bf16[4,512,512]{2,1,0:T(8,128)(2,1)S(1)}, bf16[512,256]{1,0:T(8,128)(2,1)S(1)}, f32[64,512]{1,0:T(8,128)S(1)}) custom-call(s32[3]{0:T(128)S(1)} %pad_add_fusion.refs_0_, bf16[128,4096]{1,0:T(8,128)(2,1)S(1)} %bitcast.36, bf16[128,2560]{1,0:T(8,128)(2,1)} %collective-permute-done.refs_2_, ...), custom_call_target="tpu_custom_call" | custom-call | flops 536870912 | bytes 6291456 | tf_op jit(solution)/shard_map/pallas_call | solution.py:39
  62.0 4.8 %collective-permute-start.6 = (f32[128,1024]{1,0:T(8,128)S(1)}, f32[128,1024]{1,0:T(8,128)S(1)}, u32[]{:S(2)}, u32[]{:S(2)}) collective-permute-start(f32[128,1024]{1,0:T(8,128)S(1)} %get-tuple-element.19.refs_1_), channel_id=1, source_target_pairs={{0,32},{32,0},{1,33},{33,1},{2,34},{34,2},{3,35},{35,3},{4,36},{36... | collective-permute-start | bytes 1572872 | tf_op jit(solution)/shard_map/ppermute | solution.py:189
  66.8 2.3 %collective-permute-start.14 = (bf16[4,512,256]{2,1,0:T(8,128)(2,1)S(1)}, bf16[4,512,256]{2,1,0:T(8,128)(2,1)S(1)}, u32[]{:S(2)}, u32[]{:S(2)}) collective-permute-start(bf16[4,512,256]{2,1,0:T(8,128)(2,1)S(1)} %shard_map.127.refs_5_.refs_3_), channel_id=1, source_target_pairs={{0,1},{1,0},{2,3},{3,2},{4,5},{5,4},{6,7},{7,6},{8,9},{9,8},{10,11... | collective-permute-start | bytes 3145736 | tf_op jit(solution)/shard_map/ppermute | solution.py:191
  69.1 3.1 %collective-permute-start.7 = (f32[64,512]{1,0:T(8,128)S(1)}, f32[64,512]{1,0:T(8,128)S(1)}, u32[]{:S(2)}, u32[]{:S(2)}) collective-permute-start(f32[64,512]{1,0:T(8,128)S(1)} %get-tuple-element.22), channel_id=1, source_target_pairs={{0,64},{64,0},{128,192},{192,128},{256,320},{320,256},{384,448},{4... | collective-permute-start | bytes 393224 | tf_op jit(solution)/shard_map/ppermute | solution.py:162
  72.3 3.8 %collective-permute-done.7 = f32[64,512]{1,0:T(8,128)S(1)} collective-permute-done((f32[64,512]{1,0:T(8,128)S(1)}, f32[64,512]{1,0:T(8,128)S(1)}, u32[]{:S(2)}, u32[]{:S(2)}) %collective-permute-start.7) | collective-permute-done | bytes 131104 | tf_op jit(solution)/shard_map/ppermute | solution.py:162
  76.1 2.3 %collective-permute-start.11 = (f32[64,512]{1,0:T(8,128)S(1)}, f32[64,512]{1,0:T(8,128)S(1)}, u32[]{:S(2)}, u32[]{:S(2)}) collective-permute-start(f32[64,512]{1,0:T(8,128)S(1)} %add.42.refs_5_), channel_id=1, source_target_pairs={{0,256},{64,320},{128,384},{192,448},{256,0},{320,64},{384,128},{4... | collective-permute-start | bytes 393224 | tf_op jit(solution)/shard_map/ppermute | solution.py:162
  78.4 0.3 collective-permute-done.6.refs_2_
  78.8 1.4 %shard_map.129 = (bf16[512,256]{1,0:T(8,128)(2,1)S(1)}, f32[512,256]{1,0:T(8,128)S(1)}, bf16[512,256]{1,0:T(8,128)(2,1)S(1)}, bf16[512,256]{1,0:T(8,128)(2,1)S(1)}, bf16[512,256]{1,0:T(8,128)(2,1)S(1)}) custom-call(s32[3]{0:T(128)S(1)} %pad_add_fusion.refs_0_, f32[128,1024]{1,0:T(8,128)S(1)} %get-tuple-element.19.refs_1_, ...), custom_call_target="tpu_custom_call" | custom-call | flops 536870912 | bytes 5242880 | tf_op jit(solution)/shard_map/pallas_call | solution.py:39
  80.1 1.9 %collective-permute-start.8 = (bf16[512,256]{1,0:T(8,128)(2,1)S(1)}, bf16[512,256]{1,0:T(8,128)(2,1)S(1)}, u32[]{:S(2)}, u32[]{:S(2)}) collective-permute-start(bf16[512,256]{1,0:T(8,128)(2,1)S(1)} %get-tuple-element.24), channel_id=1, source_target_pairs={{0,4},{2,6},{4,8},{6,10},{8,12},{10,14},{12,16},{14,18},{16,20},{1... | collective-permute-start | bytes 786440 | tf_op jit(solution)/shard_map/ppermute | solution.py:201
  82.1 2.8 %collective-permute-start.9 = (bf16[512,256]{1,0:T(8,128)(2,1)S(1)}, bf16[512,256]{1,0:T(8,128)(2,1)S(1)}, u32[]{:S(2)}, u32[]{:S(2)}) collective-permute-start(bf16[512,256]{1,0:T(8,128)(2,1)S(1)} %get-tuple-element.25), channel_id=1, source_target_pairs={{0,30},{2,0},{4,2},{6,4},{8,6},{10,8},{12,10},{14,12},{16,14},{18,... | collective-permute-start | bytes 786440 | tf_op jit(solution)/shard_map/ppermute | solution.py:203
  84.9 3.1 %collective-permute-start.10 = (bf16[512,256]{1,0:T(8,128)(2,1)S(1)}, bf16[512,256]{1,0:T(8,128)(2,1)S(1)}, u32[]{:S(2)}, u32[]{:S(2)}) collective-permute-start(bf16[512,256]{1,0:T(8,128)(2,1)S(1)} %get-tuple-element.26), channel_id=1, source_target_pairs={{0,2},{2,4},{4,6},{6,8},{8,10},{10,12},{12,14},{14,16},{16,18},{18... | collective-permute-start | bytes 786440 | tf_op jit(solution)/shard_map/ppermute | solution.py:202
  88.0 3.6 %collective-permute-start.12 = (bf16[256,256]{1,0:T(8,128)(2,1)S(1)}, bf16[256,256]{1,0:T(8,128)(2,1)S(1)}, u32[]{:S(2)}, u32[]{:S(2)}) collective-permute-start(bf16[256,256]{1,0:T(8,128)(2,1)S(1)} %slice.11), channel_id=1, source_target_pairs={{0,1},{1,0},{2,3},{3,2},{4,5},{5,4},{6,7},{7,6},{8,9},{9,8},{10,11... | collective-permute-start | bytes 393224 | tf_op jit(solution)/shard_map/ppermute | solution.py:205
  91.7 0.9 collective-permute-done.12.refs_6_.refs_2_
  92.6 4.0 %collective-permute-done.9.refs_3_ = bf16[512,256]{1,0:T(8,128)(2,1)S(1)} collective-permute-done((bf16[512,256]{1,0:T(8,128)(2,1)S(1)}, bf16[512,256]{1,0:T(8,128)(2,1)S(1)}, u32[]{:S(2)}, u32[]{:S(2)}) %collective-permute-start.9) | collective-permute-done | bytes 262176 | tf_op jit(solution)/shard_map/ppermute | solution.py:203
  96.6 1.3 %shard_map.130 = (bf16[512,256]{1,0:T(8,128)(2,1)}, f32[64,512]{1,0:T(8,128)S(1)}) custom-call(s32[3]{0:T(128)S(1)} %pad_add_fusion.refs_0_, f32[512,256]{1,0:T(8,128)S(1)} %get-tuple-element.23.refs_1_, bf16[512,256]{1,0:T(8,128)(2,1)S(1)} %collective-permute-done.8.refs_2_, bf16[512,256]{1,0:T(8,128)(2,1)S(1)} %collective-permute-done.9.refs_3_, ...), custom_call_target="tpu_custom_call" | custom-call | bytes 2097152 | tf_op jit(solution)/shard_map/pallas_call | solution.py:39
  98.0 5.5 %all-to-all-start.1 = ((bf16[8,64,256]{2,1,0:T(8,128)(2,1)}), bf16[8,64,256]{2,1,0:T(8,128)(2,1)S(1)}, u32[]{:S(2)}, u32[]{:S(2)}) async-start(bf16[8,64,256]{2,1,0:T(8,128)(2,1)} %bitcast.12), calls=%async_computation.1 | async-start | bytes 524288 | tf_op jit(solution)/shard_map/all_to_all | solution.py:214
  103.4 1.3 %shard_map.132 = (bf16[128,2048]{1,0:T(8,128)(2,1)S(1)}, bf16[128,2048]{1,0:T(8,128)(2,1)S(1)}) custom-call(s32[3]{0:T(128)S(1)} %pad_add_fusion.refs_0_, bf16[512,256]{1,0:T(8,128)(2,1)S(1)} %get-tuple-element.27.refs_1_, bf16[256,256]{1,0:T(8,128)(2,1)S(1)} %collective-permute-done.12.refs_6_.refs_2_, bf16[4,512,256]{2,1,0:T(8,128)(2,1)S(1)} %shard_map.127.refs_5_.refs_3_, ...), custom_call_target="tpu_custom_call" | custom-call | flops 536870912 | bytes 4194304 | tf_op jit(solution)/shard_map/pallas_call | solution.py:39
  104.7 4.9 %collective-permute-start.15 = (bf16[128,2048]{1,0:T(8,128)(2,1)S(1)}, bf16[128,2048]{1,0:T(8,128)(2,1)S(1)}, u32[]{:S(2)}, u32[]{:S(2)}) collective-permute-start(bf16[128,2048]{1,0:T(8,128)(2,1)S(1)} %get-tuple-element.31), channel_id=1, source_target_pairs={{0,32},{32,0},{1,33},{33,1},{2,34},{34,2},{3,35},{35,3},{4,36},{36... | collective-permute-start | bytes 1572872 | tf_op jit(solution)/shard_map/ppermute | solution.py:226
  110.3 4.4 %collective-permute-start.13 = (f32[64,512]{1,0:T(8,128)S(1)}, f32[64,512]{1,0:T(8,128)S(1)}, u32[]{:S(2)}, u32[]{:S(2)}) collective-permute-start(f32[64,512]{1,0:T(8,128)S(1)} %get-tuple-element.28), channel_id=1, source_target_pairs={{0,192},{64,128},{128,64},{192,0},{256,448},{320,384},{384,320},{4... | collective-permute-start | bytes 393224 | tf_op jit(solution)/shard_map/ppermute | solution.py:162
  114.7 6.8 %collective-permute-done.15.refs_2_ = bf16[128,2048]{1,0:T(8,128)(2,1)S(1)} collective-permute-done((bf16[128,2048]{1,0:T(8,128)(2,1)S(1)}, bf16[128,2048]{1,0:T(8,128)(2,1)S(1)}, u32[]{:S(2)}, u32[]{:S(2)}) %collective-permute-start.15) | collective-permute-done | bytes 524320 | tf_op jit(solution)/shard_map/ppermute | solution.py:226
  121.5 1.6 %shard_map.133 = bf16[128,4096]{1,0:T(8,128)(2,1)} custom-call(s32[3]{0:T(128)S(1)} %pad_add_fusion.refs_0_, bf16[128,2048]{1,0:T(8,128)(2,1)S(1)} %get-tuple-element.30.refs_1_, bf16[128,2048]{1,0:T(8,128)(2,1)S(1)} %collective-permute-done.15.refs_2_), custom_call_target="tpu_custom_call" | custom-call | bytes 2097152 | tf_op jit(solution)/shard_map/pallas_call | solution.py:39
  123.1 0.6 shard_map.131
  123.7 0.3 copy-done.5
  124.0 0.1 copy-done.6
  124.1 0.1 copy-done.7
  124.1 0.9 multiply_bitcast_fusion
  (24 shorter events, 0.2 us)
Async XLA Ops:
  0.6 18.5 %copy-start = (bf16[1,128,4096]{2,1,0:T(8,128)(2,1)S(1)}, bf16[1,128,4096]{2,1,0:T(8,128)(2,1)}, u32[]{:S(2)}) copy-start(bf16[1,128,4096]{2,1,0:T(8,128)(2,1)} %param.8) | copy-start | bytes 3145732
  2.4 16.8 %copy-start.2 = (bf16[1,128,512]{2,1,0:T(8,128)(2,1)S(1)}, bf16[1,128,512]{2,1,0:T(8,128)(2,1)}, u32[]{:S(2)}) copy-start(bf16[1,128,512]{2,1,0:T(8,128)(2,1)} %param.9) | copy-start | bytes 393220
  2.4 31.2 %all-to-all-start = ((bf16[8,64,256]{2,1,0:T(8,128)(2,1)}), bf16[8,64,256]{2,1,0:T(8,128)(2,1)S(1)}, u32[]{:S(2)}, u32[]{:S(2)}) async-start(bf16[8,64,256]{2,1,0:T(8,128)(2,1)} %bitcast.8), calls=%async_computation | async-start | bytes 524288 | tf_op jit(solution)/shard_map/all_to_all | solution.py:148
  19.3 36.0 %collective-permute-start = (bf16[128,2560]{1,0:T(8,128)(2,1)S(1)}, bf16[128,2560]{1,0:T(8,128)(2,1)}, u32[]{:S(2)}, u32[]{:S(2)}) collective-permute-start(bf16[128,2560]{1,0:T(8,128)(2,1)S(1)} %pad_maximum_fusion), channel_id=1, source_target_pairs={{0,32},{32,0},{1,33},{33,1},{2,34},{34,2},{3,35},{35,3},{4,36},{36... | collective-permute-start | bytes 1966088 | tf_op jit(solution)/shard_map/ppermute | solution.py:169
  33.6 23.6 %collective-permute-start.3 = (bf16[512,256]{1,0:T(8,128)(2,1)S(1)}, bf16[512,256]{1,0:T(8,128)(2,1)S(1)}, u32[]{:S(2)}, u32[]{:S(2)}) collective-permute-start(bf16[512,256]{1,0:T(8,128)(2,1)S(1)} %bitcast.41), channel_id=1, source_target_pairs={{0,4},{2,6},{4,8},{6,10},{8,12},{10,14},{12,16},{14,18},{16,20},{1... | collective-permute-start | bytes 786440 | tf_op jit(solution)/shard_map/ppermute | solution.py:152
  42.4 14.9 %collective-permute-start.4 = (bf16[512,256]{1,0:T(8,128)(2,1)S(1)}, bf16[512,256]{1,0:T(8,128)(2,1)S(1)}, u32[]{:S(2)}, u32[]{:S(2)}) collective-permute-start(bf16[512,256]{1,0:T(8,128)(2,1)S(1)} %bitcast.42), channel_id=1, source_target_pairs={{0,2},{2,4},{4,6},{6,8},{8,10},{10,12},{12,14},{14,16},{16,18},{18... | collective-permute-start | bytes 786440 | tf_op jit(solution)/shard_map/ppermute | solution.py:153
  44.3 13.0 %collective-permute-start.5 = (bf16[512,256]{1,0:T(8,128)(2,1)S(1)}, bf16[512,256]{1,0:T(8,128)(2,1)S(1)}, u32[]{:S(2)}, u32[]{:S(2)}) collective-permute-start(bf16[512,256]{1,0:T(8,128)(2,1)S(1)} %bitcast.43), channel_id=1, source_target_pairs={{0,30},{2,0},{4,2},{6,4},{8,6},{10,8},{12,10},{14,12},{16,14},{18,... | collective-permute-start | bytes 786440 | tf_op jit(solution)/shard_map/ppermute | solution.py:151
  49.7 8.2 %collective-permute-start.1 = (bf16[128,2304]{1,0:T(8,128)(2,1)}, bf16[128,2304]{1,0:T(8,128)(2,1)}, u32[]{:S(2)}, u32[]{:S(2)}) collective-permute-start(bf16[128,2304]{1,0:T(8,128)(2,1)} %pad_maximum_fusion.1), channel_id=1, source_target_pairs={{0,1},{1,0},{2,3},{3,2},{4,5},{5,4},{6,7},{7,6},{8,9},{9,8},{10,11... | collective-permute-start | bytes 1769480 | tf_op jit(solution)/shard_map/ppermute | solution.py:171
  55.3 4.3 %collective-permute-start.2 = (bf16[128,2560]{1,0:T(8,128)(2,1)}, bf16[128,2560]{1,0:T(8,128)(2,1)}, u32[]{:S(2)}, u32[]{:S(2)}) collective-permute-start(bf16[128,2560]{1,0:T(8,128)(2,1)} %collective-permute-done.refs_2_), channel_id=1, source_target_pairs={{0,1},{1,0},{2,3},{3,2},{4,5},{5,4},{6,7},{7,6},{8,9},{9,8},{10,11... | collective-permute-start | bytes 1966088 | tf_op jit(solution)/shard_map/ppermute | solution.py:172
  57.3 2.4 %copy-start.1 = (bf16[1,128,4096]{2,1,0:T(8,128)(2,1)S(1)}, bf16[1,128,4096]{2,1,0:T(8,128)(2,1)}, u32[]{:S(2)}) copy-start(bf16[1,128,4096]{2,1,0:T(8,128)(2,1)} %param.8) | copy-start | bytes 3145732
  57.3 2.4 %copy-start.3 = (f32[1,64,512]{2,1,0:T(8,128)S(1)}, f32[1,64,512]{2,1,0:T(8,128)}, u32[]{:S(2)}) copy-start(f32[1,64,512]{2,1,0:T(8,128)} %param.10) | copy-start | bytes 393220
  57.3 2.4 %copy-start.4 = (f32[64,512]{1,0:T(8,128)S(1)}, f32[64,512]{1,0:T(8,128)}, u32[]{:S(2)}) copy-start(f32[64,512]{1,0:T(8,128)} %refs_7_.1) | copy-start | bytes 393220
  62.0 16.8 %collective-permute-start.6 = (f32[128,1024]{1,0:T(8,128)S(1)}, f32[128,1024]{1,0:T(8,128)S(1)}, u32[]{:S(2)}, u32[]{:S(2)}) collective-permute-start(f32[128,1024]{1,0:T(8,128)S(1)} %get-tuple-element.19.refs_1_), channel_id=1, source_target_pairs={{0,32},{32,0},{1,33},{33,1},{2,34},{34,2},{3,35},{35,3},{4,36},{36... | collective-permute-start | bytes 1572872 | tf_op jit(solution)/shard_map/ppermute | solution.py:189
  66.8 36.6 %collective-permute-start.14 = (bf16[4,512,256]{2,1,0:T(8,128)(2,1)S(1)}, bf16[4,512,256]{2,1,0:T(8,128)(2,1)S(1)}, u32[]{:S(2)}, u32[]{:S(2)}) collective-permute-start(bf16[4,512,256]{2,1,0:T(8,128)(2,1)S(1)} %shard_map.127.refs_5_.refs_3_), channel_id=1, source_target_pairs={{0,1},{1,0},{2,3},{3,2},{4,5},{5,4},{6,7},{7,6},{8,9},{9,8},{10,11... | collective-permute-start | bytes 3145736 | tf_op jit(solution)/shard_map/ppermute | solution.py:191
  69.1 7.0 %collective-permute-start.7 = (f32[64,512]{1,0:T(8,128)S(1)}, f32[64,512]{1,0:T(8,128)S(1)}, u32[]{:S(2)}, u32[]{:S(2)}) collective-permute-start(f32[64,512]{1,0:T(8,128)S(1)} %get-tuple-element.22), channel_id=1, source_target_pairs={{0,64},{64,0},{128,192},{192,128},{256,320},{320,256},{384,448},{4... | collective-permute-start | bytes 393224 | tf_op jit(solution)/shard_map/ppermute | solution.py:162
  76.1 11.9 %collective-permute-start.11 = (f32[64,512]{1,0:T(8,128)S(1)}, f32[64,512]{1,0:T(8,128)S(1)}, u32[]{:S(2)}, u32[]{:S(2)}) collective-permute-start(f32[64,512]{1,0:T(8,128)S(1)} %add.42.refs_5_), channel_id=1, source_target_pairs={{0,256},{64,320},{128,384},{192,448},{256,0},{320,64},{384,128},{4... | collective-permute-start | bytes 393224 | tf_op jit(solution)/shard_map/ppermute | solution.py:162
  80.1 12.5 %collective-permute-start.8 = (bf16[512,256]{1,0:T(8,128)(2,1)S(1)}, bf16[512,256]{1,0:T(8,128)(2,1)S(1)}, u32[]{:S(2)}, u32[]{:S(2)}) collective-permute-start(bf16[512,256]{1,0:T(8,128)(2,1)S(1)} %get-tuple-element.24), channel_id=1, source_target_pairs={{0,4},{2,6},{4,8},{6,10},{8,12},{10,14},{12,16},{14,18},{16,20},{1... | collective-permute-start | bytes 786440 | tf_op jit(solution)/shard_map/ppermute | solution.py:201
  82.1 14.6 %collective-permute-start.9 = (bf16[512,256]{1,0:T(8,128)(2,1)S(1)}, bf16[512,256]{1,0:T(8,128)(2,1)S(1)}, u32[]{:S(2)}, u32[]{:S(2)}) collective-permute-start(bf16[512,256]{1,0:T(8,128)(2,1)S(1)} %get-tuple-element.25), channel_id=1, source_target_pairs={{0,30},{2,0},{4,2},{6,4},{8,6},{10,8},{12,10},{14,12},{16,14},{18,... | collective-permute-start | bytes 786440 | tf_op jit(solution)/shard_map/ppermute | solution.py:203
  84.9 11.7 %collective-permute-start.10 = (bf16[512,256]{1,0:T(8,128)(2,1)S(1)}, bf16[512,256]{1,0:T(8,128)(2,1)S(1)}, u32[]{:S(2)}, u32[]{:S(2)}) collective-permute-start(bf16[512,256]{1,0:T(8,128)(2,1)S(1)} %get-tuple-element.26), channel_id=1, source_target_pairs={{0,2},{2,4},{4,6},{6,8},{8,10},{10,12},{12,14},{14,16},{16,18},{18... | collective-permute-start | bytes 786440 | tf_op jit(solution)/shard_map/ppermute | solution.py:202
  88.0 4.6 %collective-permute-start.12 = (bf16[256,256]{1,0:T(8,128)(2,1)S(1)}, bf16[256,256]{1,0:T(8,128)(2,1)S(1)}, u32[]{:S(2)}, u32[]{:S(2)}) collective-permute-start(bf16[256,256]{1,0:T(8,128)(2,1)S(1)} %slice.11), channel_id=1, source_target_pairs={{0,1},{1,0},{2,3},{3,2},{4,5},{5,4},{6,7},{7,6},{8,9},{9,8},{10,11... | collective-permute-start | bytes 393224 | tf_op jit(solution)/shard_map/ppermute | solution.py:205
  98.0 25.1 %all-to-all-start.1 = ((bf16[8,64,256]{2,1,0:T(8,128)(2,1)}), bf16[8,64,256]{2,1,0:T(8,128)(2,1)S(1)}, u32[]{:S(2)}, u32[]{:S(2)}) async-start(bf16[8,64,256]{2,1,0:T(8,128)(2,1)} %bitcast.12), calls=%async_computation.1 | async-start | bytes 524288 | tf_op jit(solution)/shard_map/all_to_all | solution.py:214
  104.7 16.8 %collective-permute-start.15 = (bf16[128,2048]{1,0:T(8,128)(2,1)S(1)}, bf16[128,2048]{1,0:T(8,128)(2,1)S(1)}, u32[]{:S(2)}, u32[]{:S(2)}) collective-permute-start(bf16[128,2048]{1,0:T(8,128)(2,1)S(1)} %get-tuple-element.31), channel_id=1, source_target_pairs={{0,32},{32,0},{1,33},{33,1},{2,34},{34,2},{3,35},{35,3},{4,36},{36... | collective-permute-start | bytes 1572872 | tf_op jit(solution)/shard_map/ppermute | solution.py:226
  110.3 13.4 %collective-permute-start.13 = (f32[64,512]{1,0:T(8,128)S(1)}, f32[64,512]{1,0:T(8,128)S(1)}, u32[]{:S(2)}, u32[]{:S(2)}) collective-permute-start(f32[64,512]{1,0:T(8,128)S(1)} %get-tuple-element.28), channel_id=1, source_target_pairs={{0,192},{64,128},{128,64},{192,0},{256,448},{320,384},{384,320},{4... | collective-permute-start | bytes 393224 | tf_op jit(solution)/shard_map/ppermute | solution.py:162
  123.1 0.9 copy-start.5
  123.1 1.0 copy-start.6
  123.1 1.0 copy-start.7
